TPU v7x, 256 devices: a whole 4x4x8 slice. The times are simulated.
256 devices in a mesh: view: 8 (over x, y_hi), blk: 32 (over z, y_lo, core).
Axes of the slice: x: 4, y: 4 (y_hi: 2, y_lo: 2; y = y_hi * 2 + y_lo), z: 8, core: 2. Of those that a mesh axis runs over, the one named last changes fastest.
Arguments:
- estimate: float32 [32, 32, 64, 128], P('blk'), may hold values from 0.25 to 32, as said below
- observed: float32 [8, 32, 32, 64, 128], P('view', 'blk'), may hold values from 0.15 to 40, as said below
- kernels: float32 [8, 3, 63], P('view'), may hold values from 0.005 to 2, as said below
- offsets: int32 [8, 3], P('view'), may hold values from -16 to 16, as said below
Outputs:
- restored: float32 [32, 32, 64, 128], P('blk')
Inputs may be any that keep to these rules, and one draw needn't show every extreme that they name: `offsets`: shifts of every view along every dimension; some entry equals 16 and some equals -16. `estimate`: positive voxel values. `observed`: positive voxel values. `kernels`: positive taps.
All inputs are finite; a program needn't handle non-finite values.
Results may differ from a plain program's by a relative error of at most 0.00016.
Values sent between devices are 32-bit elements; how exact they have to be, the bound alone decides.
No kernel may reach another device: no remote copies, remote signals or barrier semaphores. Data moves between devices by JAX's collectives and lax.ppermute only.
A program may use at most 64 MiB of HBM per device.

v0:
```python
import jax
import jax.numpy as jnp
from jax import lax
from jax.sharding import PartitionSpec as P

TAPS = 63
OFF = 16
ITERS = 2
BLOCKS_Y = 4
HALF = 31


def passed_along(x, axis, by):
    devices = lax.axis_size(axis)
    pairs = [(i, i + by) for i in range(devices) if 0 <= i + by < devices]
    return lax.ppermute(x, axis, pairs)


def band_matrix(taps, shift, rows, cols, margin):
    out_pos = lax.broadcasted_iota(jnp.int32, (rows, cols), 0)
    in_pos = lax.broadcasted_iota(jnp.int32, (rows, cols), 1)
    tap_index = out_pos - in_pos + HALF - shift + margin
    picks = lax.broadcasted_iota(jnp.int32, (rows, cols, TAPS), 2)
    chosen = jnp.where(tap_index[:, :, None] == picks, taps[None, None, :], 0.0)
    return jnp.sum(chosen, axis=2)


def rows_rims(field):
    margin = HALF + OFF
    depth_rows = field.shape[1]
    below = passed_along(field[:, depth_rows - margin :, :], "blk", BLOCKS_Y)
    above = passed_along(field[:, :margin, :], "blk", -BLOCKS_Y)
    return jnp.concatenate([below, field, above], axis=1)


def full_rims(field, column):
    margin = HALF + OFF
    width = field.shape[2]
    left = passed_along(field[:, :, width - margin :], "blk", 1)
    right = passed_along(field[:, :, :margin], "blk", -1)
    left = left * (column > 0).astype(jnp.float32)
    right = right * (column < BLOCKS_Y - 1).astype(jnp.float32)
    return jnp.concatenate([left, field, right], axis=2)


def operator(field, taps, shifts, column):
    margin = HALF + OFF
    depth, rows, cols = field.shape
    highest = lax.Precision.HIGHEST
    matrix_x = band_matrix(taps[0], shifts[0], rows, rows + 2 * margin, margin)
    matrix_y = band_matrix(taps[1], shifts[1], cols, cols + 2 * margin, margin)
    matrix_z = band_matrix(taps[2], shifts[2], depth, depth, 0)
    wide_rows = rows_rims(field)
    wide = full_rims(wide_rows, column)
    along_x = jnp.einsum("xu,zuy->zxy", matrix_x, wide, precision=highest)
    along_y = jnp.einsum("zxu,yu->zxy", along_x, matrix_y, precision=highest)
    return jnp.einsum("zc,cxy->zxy", matrix_z, along_y, precision=highest)


def profile(taps, shift, start, count, length):
    position = start + lax.broadcasted_iota(jnp.int32, (count, TAPS), 0)
    source = position + lax.broadcasted_iota(jnp.int32, (count, TAPS), 1) - HALF + shift
    inside = (source >= 0) & (source < length)
    return jnp.sum(jnp.where(inside, taps[None, :], 0.0), axis=1)


def local(estimate, observed, kernels, offsets):
    field = estimate[0]
    seen = observed[0, 0]
    taps = kernels[0]
    shifts = offsets[0]
    depth, rows, cols = field.shape
    block = lax.axis_index("blk")
    column = block % BLOCKS_Y
    row_block = block // BLOCKS_Y
    total_rows = rows * (lax.axis_size("blk") // BLOCKS_Y)
    total_cols = cols * BLOCKS_Y
    prof_x = profile(taps[0], shifts[0], row_block * rows, rows, total_rows)
    prof_y = profile(taps[1], shifts[1], column * cols, cols, total_cols)
    prof_z = profile(taps[2], shifts[2], 0, depth, depth)
    every_x, every_y, every_z = (
        lax.all_gather(prof_x[None], "view", axis=0, tiled=True),
        lax.all_gather(prof_y[None], "view", axis=0, tiled=True),
        lax.all_gather(prof_z[None], "view", axis=0, tiled=True),
    )
    weight = jnp.einsum("vz,vx,vy->zxy", every_z, every_x, every_y, precision=lax.Precision.HIGHEST)
    flipped = taps[:, ::-1]
    negated = -shifts
    for step in range(ITERS):
        blurred = operator(field, taps, shifts, column)
        back = operator(seen / blurred, flipped, negated, column)
        total = lax.psum(back, "view")
        field = field * total / weight
    return field[None]


def solution(mesh):
    in_specs = (
        P("blk", None, None, None),
        P("view", "blk", None, None, None),
        P("view", None, None),
        P("view", None),
    )
    out_specs = P("blk", None, None, None)
    return jax.shard_map(local, mesh=mesh, in_specs=in_specs, out_specs=out_specs, check_vma=False)
```

profile of v0, /device:TPU:32, one launch (start us, length us, event | category | flops | bytes accessed | tf_op | source)
XLA Modules:
  0.0 580.0 jit_solution(14534726744110179264)
XLA Ops:
  8.3 3.9 collective-permute-start.1
  17.3 12.2 %collective-permute-done.1 = f32[32,47,128]{2,0,1:T(8,128)S(1)} collective-permute-done((f32[32,47,128]{2,0,1:T(8,128)S(1)}, f32[32,47,128]{2,0,1:T(8,128)S(1)}, u32[]{:S(2)}, u32[]{:S(2)}) %collective-permute-start.1) | collective-permute-done | bytes 770080 | tf_op jit(solution)/shard_map/ppermute | solution.py:16
  52.3 6.7 %collective-permute-done.3 = f32[32,158,47]{1,0,2:T(8,128)} collective-permute-done((f32[32,158,47]{1,0,2:T(8,128)S(1)}, f32[32,158,47]{1,0,2:T(8,128)}, u32[]{:S(2)}, u32[]{:S(2)}) %collective-permute-start.3) | collective-permute-done | bytes 950560 | tf_op jit(solution)/shard_map/ppermute | solution.py:16
  62.7 5.7 collective-permute-done.2
  72.1 7.5 %fusion.41 = f32[32,64,222]{2,1,0:T(8,128)S(1)} fusion(f32[32,158,47]{2,1,0:T(8,128)} %copy.131, f32[32,47,128]{2,1,0:T(8,128)S(1)} %copy.127, f32[32,64,128]{2,1,0:T(8,128)S(1)} %bitcast.81, f32[32,47,128]{2,1,0:T(8,128)} %copy-done.1, f32[32,158,47]{2,1,0:T(8,128)} %copy.130, f32[64,158]{1,0:T(8,128)S(1)} %select_reduce_fusion.3), kind=kOutput, calls=%fused_computation.49 | convolution fusion | flops 866517504 | bytes 6348800 | tf_op jit(solution)/shard_map/xu,zuy->zxy/dot_general | solution.py:55
  84.3 3.8 collective-permute-start.4
  91.1 6.9 %collective-permute-done.4 = f32[32,47,128]{2,0,1:T(8,128)S(1)} collective-permute-done((f32[32,47,128]{2,0,1:T(8,128)S(1)}, f32[32,47,128]{2,0,1:T(8,128)S(1)}, u32[]{:S(2)}, u32[]{:S(2)}) %collective-permute-start.4) | collective-permute-done | bytes 770080 | tf_op jit(solution)/shard_map/ppermute | solution.py:16
  98.0 4.4 collective-permute-done.5
  106.7 4.1 copy.134
  114.1 4.1 copy.133
  118.2 13.4 %collective-permute-start.6 = (f32[32,158,47]{1,0,2:T(8,128)}, f32[32,158,47]{1,0,2:T(8,128)}, u32[]{:S(2)}, u32[]{:S(2)}) collective-permute-start(f32[32,158,47]{1,0,2:T(8,128)} %copy.133), channel_id=1, source_target_pairs={{0,1},{1,2},{2,3},{3,4},{4,5},{5,6},{6,7},{7,8},{8,9},{9,10},{10,1... | collective-permute-start | bytes 2851592 | tf_op jit(solution)/shard_map/ppermute | solution.py:16
  137.0 4.2 copy.136
  141.2 8.5 %collective-permute-done.6 = f32[32,158,47]{1,0,2:T(8,128)} collective-permute-done((f32[32,158,47]{1,0,2:T(8,128)}, f32[32,158,47]{1,0,2:T(8,128)}, u32[]{:S(2)}, u32[]{:S(2)}) %collective-permute-start.6) | collective-permute-done | bytes 950560 | tf_op jit(solution)/shard_map/ppermute | solution.py:16
  152.4 4.2 copy.135
  156.6 5.5 pad_maximum_fusion
  162.1 6.8 %fusion.32 = f32[32,64,222]{2,1,0:T(8,128)S(1)} fusion(f32[32,158,222]{2,0,1:T(8,128)S(1)} %pad_maximum_fusion, f32[64,158]{1,0:T(8,128)S(1)} %select_reduce_fusion.2), kind=kOutput, calls=%fused_computation.46 | convolution fusion | flops 862027776 | bytes 6348800 | tf_op jit(solution)/shard_map/xu,zuy->zxy/dot_general | solution.py:55
  178.7 24.0 %all-reduce.2 = (f32[256]{0:T(256)S(1)}, f32[512]{0:T(512)S(1)}) all-reduce(f32[256]{0:T(256)S(1)} %dynamic-update-slice.1, f32[512]{0:T(512)S(1)} %dynamic-update-slice), channel_id=3, replica_groups=mesh['view'=8,'blk'=32] {'view'}, use_global_device_ids=true, to_apply=%add.1 | all-reduce | flops 768 | bytes 6144
  204.7 18.4 %all-gather.3 = f32[8,1,128]{2,1,0:T(1,128)S(1)} all-gather(f32[1,1,128]{2,1,0:T(1,128)S(1)} %bitcast.83), channel_id=4, replica_groups=mesh['view'=8,'blk'=32] {'view'}, dimensions={0}, use_global_device_ids=true | all-gather | bytes 4608 | tf_op jit(solution)/shard_map/all_gather | solution.py:83
  223.0 65.4 %all-reduce.6.cloned.1.call-done = f32[32,64,128]{2,1,0:T(8,128)} async-done(((f32[32,64,128]{2,1,0:T(8,128)}), f32[32,64,128]{2,1,0:T(8,128)}) %all-reduce.6.cloned.1.call-update) | async-done | bytes 1048592 | tf_op jit(solution)/shard_map/psum | solution.py:92
  298.1 9.8 %collective-permute-done.9 = f32[32,47,128]{2,0,1:T(8,128)S(1)} collective-permute-done((f32[32,47,128]{2,0,1:T(8,128)S(1)}, f32[32,47,128]{2,0,1:T(8,128)S(1)}, u32[]{:S(2)}, u32[]{:S(2)}) %collective-permute-start.9) | collective-permute-done | bytes 770080 | tf_op jit(solution)/shard_map/ppermute | solution.py:16
  327.1 11.8 %collective-permute-done.11 = f32[32,158,47]{1,0,2:T(8,128)} collective-permute-done((f32[32,158,47]{1,0,2:T(8,128)}, f32[32,158,47]{1,0,2:T(8,128)}, u32[]{:S(2)}, u32[]{:S(2)}) %collective-permute-start.11) | collective-permute-done | bytes 950560 | tf_op jit(solution)/shard_map/ppermute | solution.py:16
  353.3 7.5 %fusion.38 = f32[32,64,222]{2,1,0:T(8,128)S(1)} fusion(f32[32,158,47]{2,1,0:T(8,128)} %copy.149, f32[32,47,128]{2,1,0:T(8,128)S(1)} %copy.145, f32[32,64,128]{2,1,0:T(8,128)S(1)} %get-tuple-element.35, f32[32,47,128]{2,1,0:T(8,128)} %copy-done.2, f32[32,158,47]{2,1,0:T(8,128)} %copy.148, f32[64,158]{1,0:T(8,128)S(1)} %select_reduce_fusion.3), kind=kOutput, calls=%fused_computation.48 | convolution fusion | flops 866517504 | bytes 6348800 | tf_op jit(solution)/shard_map/xu,zuy->zxy/dot_general | solution.py:55
  371.4 7.8 %collective-permute-done.12 = f32[32,47,128]{2,0,1:T(8,128)S(1)} collective-permute-done((f32[32,47,128]{2,0,1:T(8,128)S(1)}, f32[32,47,128]{2,0,1:T(8,128)S(1)}, u32[]{:S(2)}, u32[]{:S(2)}) %collective-permute-start.12) | collective-permute-done | bytes 770080 | tf_op jit(solution)/shard_map/ppermute | solution.py:16
  387.0 4.1 copy.152
  393.0 4.1 copy.151
  397.1 15.5 %collective-permute-start.14 = (f32[32,158,47]{1,0,2:T(8,128)}, f32[32,158,47]{1,0,2:T(8,128)}, u32[]{:S(2)}, u32[]{:S(2)}) collective-permute-start(f32[32,158,47]{1,0,2:T(8,128)} %copy.151), channel_id=1, source_target_pairs={{0,1},{1,2},{2,3},{3,4},{4,5},{5,6},{6,7},{7,8},{8,9},{9,10},{10,1... | collective-permute-start | bytes 2851592 | tf_op jit(solution)/shard_map/ppermute | solution.py:16
  415.3 4.2 copy.154
  419.5 12.2 %collective-permute-done.14 = f32[32,158,47]{1,0,2:T(8,128)} collective-permute-done((f32[32,158,47]{1,0,2:T(8,128)}, f32[32,158,47]{1,0,2:T(8,128)}, u32[]{:S(2)}, u32[]{:S(2)}) %collective-permute-start.14) | collective-permute-done | bytes 950560 | tf_op jit(solution)/shard_map/ppermute | solution.py:16
  434.5 4.2 copy.153
  438.6 5.1 pad_maximum_fusion.1
  443.7 6.8 %fusion.35 = f32[32,64,222]{2,1,0:T(8,128)S(1)} fusion(f32[32,158,222]{2,0,1:T(8,128)S(1)} %pad_maximum_fusion.1, f32[64,158]{1,0:T(8,128)S(1)} %select_reduce_fusion.2), kind=kOutput, calls=%fused_computation.47 | convolution fusion | flops 862027776 | bytes 6348800 | tf_op jit(solution)/shard_map/xu,zuy->zxy/dot_general | solution.py:55
  456.0 114.3 %all-reduce.8.cloned.1.call-done = f32[32,64,128]{2,1,0:T(8,128)} async-done(((f32[32,64,128]{2,1,0:T(8,128)}), f32[32,64,128]{2,1,0:T(8,128)}) %all-reduce.8.cloned.1.call-update) | async-done | bytes 1048592 | tf_op jit(solution)/shard_map/psum | solution.py:92
  (148 shorter events, 147.1 us)
Async XLA Ops:
  6.5 281.9 %all-reduce.6.cloned.1.call-start = ((), (), s32[]{:S(2)}) async-start(), calls=%async_computation | async-start | bytes 2097152 | tf_op jit(solution)/shard_map/psum | solution.py:92
  6.5 8.0 %copy-start.11 = (s32[1,3]{1,0:T(1,128)S(1)}, s32[1,3]{1,0:T(1,128)}, u32[]{:S(2)}) copy-start(s32[1,3]{1,0:T(1,128)} %param.7) | copy-start | bytes 40
  8.3 24.5 %copy-start = (f32[1,32,64,128]{3,2,1,0:T(8,128)S(1)}, f32[1,32,64,128]{3,2,1,0:T(8,128)}, u32[]{:S(2)}) copy-start(f32[1,32,64,128]{3,2,1,0:T(8,128)} %param.4) | copy-start | bytes 3145732
  8.3 21.1 %collective-permute-start.1 = (f32[32,47,128]{2,0,1:T(8,128)S(1)}, f32[32,47,128]{2,0,1:T(8,128)S(1)}, u32[]{:S(2)}, u32[]{:S(2)}) collective-permute-start(f32[32,47,128]{2,0,1:T(8,128)S(1)} %copy.125), channel_id=1, source_target_pairs={{4,0},{5,1},{6,2},{7,3},{8,4},{9,5},{10,6},{11,7},{12,8},{13,9},{1... | collective-permute-start | bytes 2310152 | tf_op jit(solution)/shard_map/ppermute | solution.py:16
  12.5 19.0 %collective-permute-start = (f32[32,47,128]{2,0,1:T(8,128)S(1)}, f32[32,47,128]{2,0,1:T(8,128)S(1)}, u32[]{:S(2)}, u32[]{:S(2)}) collective-permute-start(f32[32,47,128]{2,0,1:T(8,128)S(1)} %copy.124), channel_id=1, source_target_pairs={{0,4},{1,5},{2,6},{3,7},{4,8},{5,9},{6,10},{7,11},{8,12},{9,13},{1... | collective-permute-start | bytes 2310152 | tf_op jit(solution)/shard_map/ppermute | solution.py:16
  36.4 4.9 copy-start.15
  39.4 19.5 %collective-permute-start.3 = (f32[32,158,47]{1,0,2:T(8,128)S(1)}, f32[32,158,47]{1,0,2:T(8,128)}, u32[]{:S(2)}, u32[]{:S(2)}) collective-permute-start(f32[32,158,47]{1,0,2:T(8,128)S(1)} %copy.129), channel_id=1, source_target_pairs={{1,0},{2,1},{3,2},{4,3},{5,4},{6,5},{7,6},{8,7},{9,8},{10,9},{11,1... | collective-permute-start | bytes 2851592 | tf_op jit(solution)/shard_map/ppermute | solution.py:16
  41.9 8.6 %copy-start.9 = (f32[63]{0:T(128)}, f32[63]{0:T(128)S(1)}, u32[]{:S(2)}) copy-start(f32[63]{0:T(128)S(1)} %get-tuple-element.28) | copy-start | bytes 760
  41.9 8.6 %copy-start.13 = (f32[63]{0:T(128)}, f32[63]{0:T(128)S(1)}, u32[]{:S(2)}) copy-start(f32[63]{0:T(128)S(1)} %get-tuple-element.24) | copy-start | bytes 760
  45.7 22.7 %collective-permute-start.2 = (f32[32,158,47]{1,0,2:T(8,128)}, f32[32,158,47]{1,0,2:T(8,128)}, u32[]{:S(2)}, u32[]{:S(2)}) collective-permute-start(f32[32,158,47]{1,0,2:T(8,128)} %copy.128), channel_id=1, source_target_pairs={{0,1},{1,2},{2,3},{3,4},{4,5},{5,6},{6,7},{7,8},{8,9},{9,10},{10,1... | collective-permute-start | bytes 2851592 | tf_op jit(solution)/shard_map/ppermute | solution.py:16
  79.7 2.9 copy-start.6
  82.6 7.9 %copy-start.12 = (s32[1,3]{1,0:T(1,128)S(1)}, s32[1,3]{1,0:T(1,128)}, u32[]{:S(2)}) copy-start(s32[1,3]{1,0:T(1,128)} %param.7) | copy-start | bytes 40
  84.3 13.7 %collective-permute-start.4 = (f32[32,47,128]{2,0,1:T(8,128)S(1)}, f32[32,47,128]{2,0,1:T(8,128)S(1)}, u32[]{:S(2)}, u32[]{:S(2)}) collective-permute-start(f32[32,47,128]{2,0,1:T(8,128)S(1)} %get-tuple-element.19), channel_id=1, source_target_pairs={{0,4},{1,5},{2,6},{3,7},{4,8},{5,9},{6,10},{7,11},{8,12},{9,13},{1... | collective-permute-start | bytes 2310152 | tf_op jit(solution)/shard_map/ppermute | solution.py:16
  88.1 14.3 %collective-permute-start.5 = (f32[32,47,128]{2,0,1:T(8,128)S(1)}, f32[32,47,128]{2,0,1:T(8,128)S(1)}, u32[]{:S(2)}, u32[]{:S(2)}) collective-permute-start(f32[32,47,128]{2,0,1:T(8,128)S(1)} %get-tuple-element.20), channel_id=1, source_target_pairs={{4,0},{5,1},{6,2},{7,3},{8,4},{9,5},{10,6},{11,7},{12,8},{13,9},{1... | collective-permute-start | bytes 2310152 | tf_op jit(solution)/shard_map/ppermute | solution.py:16
  110.8 21.3 %copy-start.18 = (f32[1,63]{1,0:T(1,128)S(1)}, f32[1,63]{1,0:T(1,128)}, u32[]{:S(2)}) copy-start(f32[1,63]{1,0:T(1,128)} %get-tuple-element.23) | copy-start | bytes 760
  110.8 21.4 %copy-start.17 = (f32[1,63]{1,0:T(1,128)S(1)}, f32[1,63]{1,0:T(1,128)}, u32[]{:S(2)}) copy-start(f32[1,63]{1,0:T(1,128)} %get-tuple-element.25) | copy-start | bytes 760
  110.8 21.5 %copy-start.16 = (f32[1,63]{1,0:T(1,128)S(1)}, f32[1,63]{1,0:T(1,128)}, u32[]{:S(2)}) copy-start(f32[1,63]{1,0:T(1,128)} %get-tuple-element.26) | copy-start | bytes 760
  110.8 23.4 %collective-permute-start.7 = (f32[32,158,47]{1,0,2:T(8,128)}, f32[32,158,47]{1,0,2:T(8,128)}, u32[]{:S(2)}, u32[]{:S(2)}) collective-permute-start(f32[32,158,47]{1,0,2:T(8,128)} %copy.134), channel_id=1, source_target_pairs={{1,0},{2,1},{3,2},{4,3},{5,4},{6,5},{7,6},{8,7},{9,8},{10,9},{11,1... | collective-permute-start | bytes 2851592 | tf_op jit(solution)/shard_map/ppermute | solution.py:16
  118.2 31.5 %collective-permute-start.6 = (f32[32,158,47]{1,0,2:T(8,128)}, f32[32,158,47]{1,0,2:T(8,128)}, u32[]{:S(2)}, u32[]{:S(2)}) collective-permute-start(f32[32,158,47]{1,0,2:T(8,128)} %copy.133), channel_id=1, source_target_pairs={{0,1},{1,2},{2,3},{3,4},{4,5},{5,6},{6,7},{7,8},{8,9},{9,10},{10,1... | collective-permute-start | bytes 2851592 | tf_op jit(solution)/shard_map/ppermute | solution.py:16
  171.8 4.7 copy-start.10
  171.8 5.9 %copy-start.14 = (f32[63]{0:T(128)S(1)}, f32[63]{0:T(128)}, u32[]{:S(2)}) copy-start(f32[63]{0:T(128)} %copy-done.13) | copy-start | bytes 760
  171.8 32.1 %copy-start.8 = (f32[63]{0:T(128)S(1)}, f32[63]{0:T(128)}, u32[]{:S(2)}) copy-start(f32[63]{0:T(128)} %get-tuple-element.27) | copy-start | bytes 760
  174.5 395.9 %all-reduce.8.cloned.1.call-start = ((), (), s32[]{:S(2)}) async-start(), calls=%async_computation.1 | async-start | bytes 2097152 | tf_op jit(solution)/shard_map/psum | solution.py:92
  292.0 15.9 %collective-permute-start.9 = (f32[32,47,128]{2,0,1:T(8,128)S(1)}, f32[32,47,128]{2,0,1:T(8,128)S(1)}, u32[]{:S(2)}, u32[]{:S(2)}) collective-permute-start(f32[32,47,128]{2,0,1:T(8,128)S(1)} %copy.143), channel_id=1, source_target_pairs={{4,0},{5,1},{6,2},{7,3},{8,4},{9,5},{10,6},{11,7},{12,8},{13,9},{1... | collective-permute-start | bytes 2310152 | tf_op jit(solution)/shard_map/ppermute | solution.py:16
  295.2 15.1 %collective-permute-start.8 = (f32[32,47,128]{2,0,1:T(8,128)S(1)}, f32[32,47,128]{2,0,1:T(8,128)S(1)}, u32[]{:S(2)}, u32[]{:S(2)}) collective-permute-start(f32[32,47,128]{2,0,1:T(8,128)S(1)} %copy.142), channel_id=1, source_target_pairs={{0,4},{1,5},{2,6},{3,7},{4,8},{5,9},{6,10},{7,11},{8,12},{9,13},{1... | collective-permute-start | bytes 2310152 | tf_op jit(solution)/shard_map/ppermute | solution.py:16
  319.0 19.8 %collective-permute-start.11 = (f32[32,158,47]{1,0,2:T(8,128)}, f32[32,158,47]{1,0,2:T(8,128)}, u32[]{:S(2)}, u32[]{:S(2)}) collective-permute-start(f32[32,158,47]{1,0,2:T(8,128)} %copy.147), channel_id=1, source_target_pairs={{1,0},{2,1},{3,2},{4,3},{5,4},{6,5},{7,6},{8,7},{9,8},{10,9},{11,1... | collective-permute-start | bytes 2851592 | tf_op jit(solution)/shard_map/ppermute | solution.py:16
  324.7 22.7 %collective-permute-start.10 = (f32[32,158,47]{1,0,2:T(8,128)}, f32[32,158,47]{1,0,2:T(8,128)}, u32[]{:S(2)}, u32[]{:S(2)}) collective-permute-start(f32[32,158,47]{1,0,2:T(8,128)} %copy.146), channel_id=1, source_target_pairs={{0,1},{1,2},{2,3},{3,4},{4,5},{5,6},{6,7},{7,8},{8,9},{9,10},{10,1... | collective-permute-start | bytes 2851592 | tf_op jit(solution)/shard_map/ppermute | solution.py:16
  365.5 13.7 %collective-permute-start.12 = (f32[32,47,128]{2,0,1:T(8,128)S(1)}, f32[32,47,128]{2,0,1:T(8,128)S(1)}, u32[]{:S(2)}, u32[]{:S(2)}) collective-permute-start(f32[32,47,128]{2,0,1:T(8,128)S(1)} %get-tuple-element.15), channel_id=1, source_target_pairs={{0,4},{1,5},{2,6},{3,7},{4,8},{5,9},{6,10},{7,11},{8,12},{9,13},{1... | collective-permute-start | bytes 2310152 | tf_op jit(solution)/shard_map/ppermute | solution.py:16
  368.9 13.7 %collective-permute-start.13 = (f32[32,47,128]{2,0,1:T(8,128)S(1)}, f32[32,47,128]{2,0,1:T(8,128)S(1)}, u32[]{:S(2)}, u32[]{:S(2)}) collective-permute-start(f32[32,47,128]{2,0,1:T(8,128)S(1)} %get-tuple-element.16), channel_id=1, source_target_pairs={{4,0},{5,1},{6,2},{7,3},{8,4},{9,5},{10,6},{11,7},{12,8},{13,9},{1... | collective-permute-start | bytes 2310152 | tf_op jit(solution)/shard_map/ppermute | solution.py:16
  379.2 3.5 copy-start.4
  391.0 21.5 %collective-permute-start.15 = (f32[32,158,47]{1,0,2:T(8,128)}, f32[32,158,47]{1,0,2:T(8,128)}, u32[]{:S(2)}, u32[]{:S(2)}) collective-permute-start(f32[32,158,47]{1,0,2:T(8,128)} %copy.152), channel_id=1, source_target_pairs={{1,0},{2,1},{3,2},{4,3},{5,4},{6,5},{7,6},{8,7},{9,8},{10,9},{11,1... | collective-permute-start | bytes 2851592 | tf_op jit(solution)/shard_map/ppermute | solution.py:16
  397.1 34.6 %collective-permute-start.14 = (f32[32,158,47]{1,0,2:T(8,128)}, f32[32,158,47]{1,0,2:T(8,128)}, u32[]{:S(2)}, u32[]{:S(2)}) collective-permute-start(f32[32,158,47]{1,0,2:T(8,128)} %copy.151), channel_id=1, source_target_pairs={{0,1},{1,2},{2,3},{3,4},{4,5},{5,6},{6,7},{7,8},{8,9},{9,10},{10,1... | collective-permute-start | bytes 2851592 | tf_op jit(solution)/shard_map/ppermute | solution.py:16
  (8 other events, 14.9 us)
Sparse Core Ops, SparseCore 0:
  174.6 113.8 all-reduce.5
  456.1 114.1 all-reduce.7
where the time goes:
time: 585 us; the launch traced here: 580 us
  waiting for transfers between devices  275 us (47%)
  local copies, waits for them, and re-layouts  86.9 us (15%)
  starting transfers between devices  65.5 us (11%)
  matrix products  48.2 us (8%)
  other arithmetic  45.9 us (8%)
  blocking collectives  42.4 us (7%)
  between operations  15.9 us (3%)
    psum x2, waiting for transfers between devices, local(): total = lax.psum(back, 'view')  180 us
    ppermute x16, waiting for transfers between devices, passed_along(): return lax.ppermute(x, axis, pairs)  95.5 us
    ppermute x16, starting transfers between devices, passed_along(): return lax.ppermute(x, axis, pairs)  65.4 us
    slice x8, local copies, waits for them, and re-layouts, full_rims(): left = passed_along(field[:, :, width - margin:], 'blk', 1)  28.7 us
    dot_general x4, matrix products, operator(): along_x = jnp.einsum('xu,zuy->zxy', matrix_x, wide, precision=highest)  28.6 us
    unnamed x1, blocking collectives  24 us
    all_gather x1, blocking collectives, local(): lax.all_gather(prof_y[None], 'view', axis=0, tiled=True)  18.4 us
    slice x4, local copies, waits for them, and re-layouts, full_rims(): right = passed_along(field[:, :, :margin], 'blk', -1)  14.9 us
  transfers between devices with their start and end apart: 18, of which 16 were waited for; matrix products, arithmetic and copies ran while one was open for 10% of the time, Pallas kernels for 0%

commit v1 on v0

v1 whole, which is shorter than its diff:
```python
import functools
import jax
import jax.numpy as jnp
from jax import lax
from jax.experimental import pallas as pl
from jax.experimental.pallas import tpu as pltpu
from jax.sharding import PartitionSpec as P

TAPS = 63
ITERS = 2
Z, BX, BY = 32, 64, 128
HALF_Z = Z // 2
RIM = 32
SHIFT = 16
GRID = 512
F32, BF16 = jnp.float32, jnp.bfloat16
PROF = 8
ORDER = (0, 1, 3, 2)


def split(x):
    hi = x.astype(BF16)
    return hi, (x - hi.astype(F32)).astype(BF16)


def dot(a, b):
    return jnp.dot(a, b, preferred_element_type=F32)


def wrap_of(pos):
    return jnp.where(pos >= GRID, 1, 0) - jnp.where(pos < 0, 1, 0)


def sds(*shape, dtype=F32):
    return jax.ShapeDtypeStruct(shape, dtype)


def call(body, out_shape, *args, smem=(), before=(), after=(), scratch=(), flops=1_000_000):
    specs = [
        pl.BlockSpec(memory_space=pltpu.SMEM if i in smem else pltpu.VMEM)
        for i in range(len(args))
    ]
    count, lead, tail = len(args), len(before), len(after)

    def inner(*refs):
        body(*refs[lead : lead + count], *refs[lead + count + tail :])

    loose = pl.BlockSpec(memory_space=pl.ANY)
    specs = [loose] * lead + specs + [loose] * tail
    size = sum(v.size * v.dtype.itemsize for v in (*args, *out_shape))
    outs = pl.pallas_call(
        inner,
        out_shape=out_shape,
        in_specs=specs,
        out_specs=[pl.BlockSpec(memory_space=pltpu.VMEM) for _ in out_shape],
        scratch_shapes=list(scratch),
        compiler_params=pltpu.CompilerParams(vmem_limit_bytes=40 * 1024 * 1024),
        cost_estimate=pl.CostEstimate(flops=flops, bytes_accessed=size, transcendentals=0),
    )(*before, *args, *after)
    return outs if len(outs) > 1 else outs[0]


def even_column():
    return lax.axis_index("blk") % 2 == 0


def lanes(shape):
    return lax.broadcasted_iota(jnp.int32, shape, len(shape) - 1)


def rows_of(shape):
    return lax.broadcasted_iota(jnp.int32, shape, len(shape) - 2)


def tap_rows(taps, full, rows, depth=True):
    full[...] = jnp.zeros_like(full)
    full[:3, :TAPS] = taps
    x = full[...]
    hi, lo = split(x)
    mid, low = split(x - hi.astype(F32))
    parts = jnp.concatenate([hi, mid, low, jnp.zeros_like(hi)], axis=0)

    def moved(step, flip, width):
        j = lax.broadcasted_iota(jnp.int32, (BY, width), 0)
        target = (TAPS - 1 - j if flip else j) * step
        hot = jnp.where((lanes((BY, width)) == target) & (j < TAPS), 1.0, 0.0).astype(BF16)
        out = dot(parts, hot)
        return out[:8] + (out[8:16] + out[16:24])

    rows[...] = jnp.zeros_like(rows)
    flipped = moved(1, True, BY)
    rows[0:1, :BY] = x[0:1]
    rows[1:2, :BY] = flipped[0:1]
    rows[2:3, :BY] = x[1:2]
    rows[3:4, :BY] = flipped[1:2]
    if depth:
        rows[4:5, :512] = moved(8, False, 512)[2:3]
        rows[5:6, :512] = moved(8, True, 512)[2:3]


def block_start():
    block = lax.axis_index("blk")
    return (block // 4) * BX, (block % 4) * BY


def x_band(rows, row, s, ox, adjoint=False):
    base = jnp.broadcast_to(rows[row : row + 1, :BY], (BX, BY))
    band = pltpu.roll(base, 1, 1, stride=1, stride_axis=0)
    m = s + lanes((BX, BY)) - RIM
    i = s + ox + rows_of((BX, BY))
    keep = (wrap_of(m + ox) == 0) if adjoint else (wrap_of(i) == wrap_of(m))
    return jnp.where(keep, band, 0.0)


def x_band_turned(rows, row, s, ox):
    base = jnp.broadcast_to(rows[row : row + 1, :256], (BY, 256))
    band = pltpu.roll(base, 193, 1, stride=1, stride_axis=0)[:, :BY]
    m = s + rows_of((BY, BY)) - RIM
    i = s + ox + lanes((BY, BY))
    keep = (wrap_of(i) == wrap_of(m)) & (lanes((BY, BY)) < BX)
    return jnp.where(keep, band, 0.0)[:, :BX]


def y_toeplitz(rows, row):
    base = jnp.broadcast_to(rows[row : row + 1, :256], (BY + 2 * RIM, 256))
    return pltpu.roll(base, 193, 1, stride=1, stride_axis=0)[:, :BY]


def y_band(rows, row, cs, oy):
    band = y_toeplitz(rows, row)
    m = cs + rows_of(band.shape)
    j = cs + oy + RIM + lanes(band.shape)
    return jnp.where(wrap_of(j) == wrap_of(m), band, 0.0)


def y_profile(rows, row, cs, oy):
    band = y_toeplitz(rows, row)
    m = cs + rows_of(band.shape) - RIM
    return jnp.sum(jnp.where(wrap_of(m + oy) == 0, band, 0.0), axis=0, keepdims=True)


def z_band(rows, row, shift):
    amount = lax.rem(1024 - 248 - 8 * shift, 1024)
    moved = pltpu.roll(rows[...], amount, 1)[row : row + 1]
    base = jnp.broadcast_to(moved, (256, 1024))
    return pltpu.roll(base, 0, 1, stride=1, stride_axis=0)[:, :256]


def put_x(ref, band):
    hi, lo = split(band)
    top = jnp.concatenate([hi, hi], axis=1)
    bottom = jnp.concatenate([lo, jnp.zeros_like(lo)], axis=1)
    ref[...] = jnp.concatenate([top, bottom], axis=0)


def put_y(main, rims, band):
    hi, lo = split(band[:BY])
    main[...] = jnp.concatenate([hi, lo], axis=1)
    side = band[BY:]
    none = jnp.zeros_like(side)
    whole = jnp.concatenate([jnp.concatenate([side, none], axis=1),
                             jnp.concatenate([none, side], axis=1)], axis=0)
    rims[0], rims[1] = split(whole)


def own_kernel(offs, taps, lxf, wyf, wrf, kzf, kzb, note, full, rows):
    tap_rows(taps[0], full, rows)
    s, cs = block_start()
    ox, oy, oz = offs[0, 0], offs[0, 1], offs[0, 2]
    put_x(lxf, x_band(rows, 1, s, ox))
    put_y(wyf, wrf, y_band(rows, 2, cs, oy))
    front_z = z_band(rows, 5, oz)
    kzf[0], kzf[1] = split(front_z)
    kzb[0], kzb[1] = split(z_band(rows, 4, -oz))
    back_x = x_band(rows, 0, s, ox, True)
    turned = jnp.transpose(jnp.concatenate([back_x, jnp.zeros_like(back_x)], axis=0))
    prof_x = jnp.sum(turned, axis=0, keepdims=True)
    prof_y = y_profile(rows, 3, cs, oy)
    prof_z = jnp.sum(front_z, axis=0, keepdims=True)
    lane = lanes((1, BY))
    shifts = jnp.where(lane == 0, ox, jnp.where(lane == 1, oy, 0)).astype(F32)
    note[...] = jnp.concatenate(
        [full[:3], shifts, prof_x, prof_y, prof_z[:, :128], prof_z[:, 128:]], axis=0)


LX, WY = sds(128, 256, dtype=BF16), sds(128, 256, dtype=BF16)
WR, KZ = sds(2, 128, 256, dtype=BF16), sds(2, 256, 256, dtype=BF16)
LT = sds(2, 128, 256, dtype=BF16)
TAP_SCRATCH = [pltpu.VMEM((8, BY), F32), pltpu.VMEM((8, 1024), F32)]


def own_matrices(offs, taps):
    return call(own_kernel, [LX, WY, WR, KZ, KZ, sds(PROF, 128)], offs, taps, smem=(0,),
                scratch=TAP_SCRATCH)


def group_kernel(n0, n1, n2, n3, lx, wy, wr, lt, full, rows):
    s, cs = block_start()
    for j, note in enumerate((n0, n1, n2, n3)):
        tap_rows(note[:3, :TAPS], full, rows, False)
        shifts = note[3:4]
        ox = shifts[:, 0:1].astype(jnp.int32)
        oy = shifts[:, 1:2].astype(jnp.int32)
        put_x(lx.at[j], x_band(rows, 1, s, ox))
        put_y(wy.at[j], wr.at[j], y_band(rows, 2, cs, oy))
        hi, lo = split(x_band_turned(rows, 0, s, ox))
        lt[0, :, j * BX : (j + 1) * BX] = hi
        lt[1, :, j * BX : (j + 1) * BX] = lo


def group_matrices(notes):
    many = lambda v: sds(4, *v.shape, dtype=v.dtype)
    return call(group_kernel, [many(LX), many(WY), many(WR), LT], *notes, scratch=TAP_SCRATCH)


def row_rims(planes, top, bottom):
    for k, plane in enumerate(planes):
        top[k] = plane[:RIM]
        bottom[k] = plane[BX - RIM :]


def col_rims(planes, out):
    there = lanes(planes[0].shape) >= BY // 2
    for g in range(len(planes) // 2):
        out[g] = jnp.where(there, pltpu.roll(planes[2 * g + 1], BY // 2, 1), planes[2 * g])


ROWS = [sds(HALF_Z, RIM, BY), sds(HALF_Z, RIM, BY)]
COLS = [sds(HALF_Z // 2, BX, BY)]
HALF = sds(HALF_Z, BX, BY)


def planes_of(*refs, half=None):
    planes = []
    for ref in refs:
        if len(ref.shape) == 3:
            skip = 0 if half is None else half * HALF_Z
            stop = ref.shape[0] if half is None else skip + HALF_Z
            planes += [ref[k] for k in range(skip, stop)]
        else:
            planes += [ref[k * BX : (k + 1) * BX] for k in range(ref.shape[0] // BX)]
    return planes


def row_rims_kernel(half, *refs):
    row_rims(planes_of(*refs[:-2], half=half), *refs[-2:])


def col_rims_kernel(half, *refs):
    col_rims(planes_of(*refs[:-1], half=half), refs[-1])


def obs_cols_kernel(obs, out):
    col_rims(planes_of(obs), out)


def x_filter(mat, own, above, below, put):
    for g in range(HALF_Z // 2):
        both = []
        for k in (2 * g, 2 * g + 1):
            both.append(jnp.concatenate([above[k], own[k], below[k]], axis=0))
        o = x_pair(mat, jnp.concatenate(both, axis=1))
        put(2 * g, o[:, :BY])
        put(2 * g + 1, o[:, BY:])


def x_pair(mat, wide):
    hi, lo = split(wide)
    o = dot(mat[...], jnp.concatenate([hi, lo], axis=0))
    return o[:BX] + o[BX:]


def y_filter(main, rims, own, packs, put):
    for g in range(len(own) // 4):
        x = jnp.concatenate([own[4 * g + q] for q in range(4)], axis=0)
        hi, lo = split(x)
        o = dot(hi, main[...])
        o = o[:, :BY] + o[:, BY:] + dot(lo, main[:, :BY])
        hi, lo = split(jnp.concatenate([packs[2 * g], packs[2 * g + 1]], axis=0))
        r = dot(hi, rims[0]) + dot(hi, rims[1]) + dot(lo, rims[0])
        for q in range(4):
            i = q // 2 * BX
            j = q % 2 * BY
            put(4 * g + q, o[q * BX : (q + 1) * BX] + r[i : i + BX, j : j + BY])


def dot_turned(a, b):
    return lax.dot_general(a, b, (((1,), (1,)), ((), ())), preferred_element_type=F32)


def z_filter(mat, tiles):
    hi, lo = split(tiles)
    return dot(mat[0], hi) + dot(mat[0], lo) + dot(mat[1], hi)


def storer(ref, place=lambda k: k):
    def put(k, v):
        ref[place(k)] = v

    return put


def y_first_kernel(count, half, *refs):
    src, (packs, wy, wr, yb, top, bottom) = refs[:count], refs[count:]

    def put(k, v):
        yb[k] = v
        top[k] = v[:RIM]
        bottom[k] = v[BX - RIM :]

    y_filter(wy, wr, planes_of(*src, half=half), packs, put)


def x_first_kernel(count, half, *refs):
    src, (above, below, lx, xa, packs) = refs[:count], refs[count:]
    x_filter(lx, planes_of(*src, half=half), above, below, storer(xa))
    col_rims(planes_of(xa), packs)


def y_first(src, half, cols, wy, wr, **more):
    return call(functools.partial(y_first_kernel, len(src), half), [HALF, *ROWS],
                *src, cols, wy, wr, **more)


def x_first(src, half, rows, lx, **more):
    return call(functools.partial(x_first_kernel, len(src), half), [HALF, *COLS],
                *src, *rows, lx, **more)


def ratio_core(tmp, kf, kb, obs, out, sends):
    for t in range(BX // 16):
        cut = [slice(16 * t, 16 * t + 8), slice(16 * t + 8, 16 * t + 16)]
        blurred = z_filter(kf, jnp.concatenate([tmp[:, c, :].reshape(256, BY) for c in cut], axis=1))
        seen = jnp.concatenate([obs[:, c, :].reshape(256, BY) for c in cut], axis=1)
        back = z_filter(kb, seen / blurred)
        for i, c in enumerate(cut):
            out[:, c, :] = back[:, i * BY : (i + 1) * BY].reshape(Z, 8, BY)
    x = lax.axis_index("view") // 2
    for j, send in zip(ORDER, sends):
        send[...] = out[pl.ds(8 * (x ^ j), 8)]


def ratio_start_kernel(xa, yb, above, below, packs, lx, wy, wr, kf, kb, obs,
                       s0, s1, s3, s2, tmp, out):
    y_filter(wy, wr, planes_of(xa), packs, storer(tmp))
    x_filter(lx, planes_of(yb), above, below, storer(tmp, lambda k: HALF_Z + k))
    ratio_core(tmp, kf, kb, obs, out, (s0, s1, s3, s2))


def ratio_kernel(g1, g3, g2, g0, kf, kb, obs, s0, s1, s3, s2, tmp, out):
    x = lax.axis_index("view") // 2
    for j, got in zip(ORDER, (g0, g1, g3, g2)):
        tmp[pl.ds(8 * (x ^ j), 8)] = got[...]
    ratio_core(tmp, kf, kb, obs, out, (s0, s1, s3, s2))


SHARD = sds(8, BX, BY)
EDGE = sds(8, RIM, BY)
PACK = sds(4, BY, BY)
WHOLE = pltpu.VMEM((Z, BX, BY), F32)


def shard_cols_kernel(own, above, below, out):
    planes = [jnp.concatenate([above[k], own[k * BX : (k + 1) * BX], below[k]], axis=0)
              for k in range(8)]
    col_rims(planes, out)


def spread_kernel(picks, own, above, below, packs, lx, wy, wr, *refs):
    outs, mid = refs[:-1], refs[-1]
    tiles = [jnp.concatenate([above[k], own[k * BX : (k + 1) * BX], below[k]], axis=0)
             for k in range(8)]
    tiles += [packs[k] for k in range(4)]
    for g in range(6):
        hi, lo = split(jnp.concatenate(tiles[2 * g : 2 * g + 2], axis=1))
        both = jnp.concatenate([hi, lo], axis=0)
        for n, j in enumerate(picks):
            o = dot(lx[j], both)
            o = o[:BX] + o[BX:]
            mid[n, 2 * g] = o[:, :BY]
            mid[n, 2 * g + 1] = o[:, BY:]
    for n, j in enumerate(picks):
        y_filter(wy.at[j], wr.at[j], [mid[n, k] for k in range(8)],
                 [mid[n, 8 + k] for k in range(4)], storer(outs[n]))


def spread(picks, new, got, packs, mats, **more):
    return call(functools.partial(spread_kernel, picks), [SHARD] * len(picks),
                new, *got, packs, *mats[:3], **more,
                scratch=[pltpu.VMEM((len(picks), 12, BX, BY), F32)])


def collect_columns(r, w, rims, put):
    for g in range(2):
        planes = [r[4 * g + q] for q in range(4)]
        hi, lo = split(jnp.concatenate(planes, axis=0))
        o = dot_turned(hi, w[:, :BY]) + dot_turned(hi, w[:, BY:]) + dot_turned(lo, w[:, :BY])
        for q in range(4):
            put(4 * g + q, o[q * BX : (q + 1) * BX])
        pairs = [jnp.concatenate(planes[2 * i : 2 * i + 2], axis=1) for i in range(2)]
        hi, lo = split(jnp.concatenate(pairs, axis=0))
        e = dot_turned(hi, rims[0]) + dot_turned(hi, rims[1]) + dot_turned(lo, rims[0])
        for i in range(2):
            put(8 + 2 * g + i, e[i * BX : (i + 1) * BX])


def collect_first_kernel(r0, r1, r3, wy, wr, mid):
    for j, r in enumerate((r0, r1, r3)):
        def put(k, v, j=j):
            mid[k, j * BX : (j + 1) * BX] = v

        collect_columns(r, wy.at[j], wr.at[j], put)


def collect_kernel(part, r2, wy, wr, lt, main, packs, late):
    def put_late(k, v):
        late[k] = v

    collect_columns(r2, wy.at[3], wr.at[3], put_late)
    for g in range(6):
        both = [jnp.concatenate([part[k], late[k]], axis=0) for k in (2 * g, 2 * g + 1)]
        hi, lo = split(jnp.concatenate(both, axis=1))
        o = dot(lt[0], hi) + dot(lt[0], lo) + dot(lt[1], hi)
        for i in range(2):
            k = 2 * g + i
            v = o[:, i * BY : (i + 1) * BY]
            if k < 8:
                main[k] = v
            else:
                packs[k - 8] = v


def add_cols_kernel(main, packs, own, up, down):
    near = lanes((BY, BY)) < BY // 2
    for k in range(8):
        pack = packs[k // 2]
        side = pltpu.roll(pack, BY // 2, 1) if k % 2 else pack
        v = main[k] + jnp.where(near, side, 0.0)
        up[k] = v[:RIM]
        own[k * BX : (k + 1) * BX] = v[RIM : RIM + BX]
        down[k] = v[RIM + BX :]


def add_rows_kernel(own, above, below, *refs):
    out, notes = refs[-1], refs[:-1]
    for k in range(8):
        r = k * BX
        out[r : r + RIM] = own[r : r + RIM] + above[k]
        out[r + RIM : r + BX] = own[r + RIM : r + BX] + below[k]
    for j, note in enumerate(notes):
        out[512 + 8 * j : 520 + 8 * j] = note[...]


def update_kernel(first, *refs):
    if first:
        f, mine, other, out, weight, top, bottom, turned = refs
    else:
        f, mine, other, weight, out = refs
    x = lax.axis_index("view") // 2
    if first:
        every = jnp.concatenate(
            [mine[512:], other[512:], jnp.zeros((64, 128), F32)], axis=0)
        turned[...] = jnp.transpose(every)
        outer = []
        for v in range(8):
            outer.append(turned[:BX, 8 * v + 4 : 8 * v + 5] * every[8 * v + 5 : 8 * v + 6])
        late = x >= 2
        for k in range(8):
            z_row = turned[pl.ds(pl.multiple_of(64 * (x % 2) + 8 * k, 8), 1), :]
            total = None
            for v in range(8):
                c = 8 * v + 6
                term = jnp.where(late, z_row[:, c + 1 : c + 2], z_row[:, c : c + 1]) * outer[v]
                total = term if total is None else total + term
            weight[k * BX : (k + 1) * BX] = total
        old = f[pl.ds(8 * x, 8)].reshape(512, BY)
    else:
        old = f[...]
    new = old * (mine[:512] + other[:512]) / weight[...]
    out[...] = new
    if first:
        for k in range(8):
            top[k] = new[k * BX : k * BX + RIM]
            bottom[k] = new[(k + 1) * BX - RIM : (k + 1) * BX]


def gather_kernel(own, r1, r3, a2, b2, f):
    x = lax.axis_index("view") // 2
    f[pl.ds(8 * x, 8)] = own[...].reshape(8, BX, BY)
    f[pl.ds(8 * (x ^ 1), 8)] = r1[...].reshape(8, BX, BY)
    f[pl.ds(8 * (x ^ 3), 8)] = r3[...].reshape(8, BX, BY)
    f[pl.ds(8 * (x ^ 2), 4)] = a2[...].reshape(4, BX, BY)
    f[pl.ds(8 * (x ^ 2) + 4, 4)] = b2[...].reshape(4, BX, BY)


def cols_kernel(offs, obs, packs, out, top, bottom):
    shift = offs[0, 1] + RIM
    outside = lanes((BX, BY)) + shift >= BY
    for k in range(Z):
        own = pltpu.roll(obs[k], BY - shift, 1)
        side = pltpu.roll(packs[k // 2], lax.rem(2 * BY - shift - BY // 2 * (k % 2), BY), 1)
        v = jnp.where(outside, side, own)
        out[k] = v
        top[k] = v[:SHIFT]
        bottom[k] = v[BX - SHIFT :]


def rows_kernel(offs, obs, above, below, out):
    ox = offs[0, 0]
    total = BX + 2 * SHIFT
    amount = lax.rem(2 * total - SHIFT - ox, total)
    for k in range(Z):
        wide = jnp.concatenate([above[k], obs[k], below[k]], axis=0)
        out[k] = pltpu.roll(wide, amount, 0)[:BX]


def along_rows(x, by):
    return lax.ppermute(x, "blk", [(i, (i + 4 * by) % 32) for i in range(32)])


def along_cols(x, by):
    return lax.ppermute(x, "blk", [(i, i // 4 * 4 + (i + by) % 4) for i in range(32)])


def view_swap(x, mask):
    return lax.ppermute(x, "view", [(i, i ^ mask) for i in range(8)])


def send_rows(top, bottom):
    return along_rows(bottom, 1), along_rows(top, -1)


def trade(own, one, three, two):
    return own, view_swap(one, 2), view_swap(three, 6), view_swap(two, 4)


def local(estimate, observed, kernels, offsets):
    f = estimate[0]
    seen = observed[0, 0]
    cols_b = along_cols(call(functools.partial(col_rims_kernel, 1), COLS, f), -1)
    rows_a = send_rows(*call(functools.partial(row_rims_kernel, 0), ROWS, f))
    lxf, wyf, wrf, kzf, kzb, note = own_matrices(offsets, kernels)
    notes = trade(note, note, note, note)
    yb, *rims = y_first((f,), 1, cols_b, wyf, wrf)
    rows_b = send_rows(*rims)
    xa, packs = x_first((f,), 0, rows_a, lxf, before=(yb,), after=notes[1:])
    cols_a = along_cols(packs, -1)
    obs_cols = along_cols(call(obs_cols_kernel, [sds(Z // 2, BX, BY)], seen), -1)
    obs, top, bottom = call(
        cols_kernel, [sds(Z, BX, BY), sds(Z, SHIFT, BY), sds(Z, SHIFT, BY)],
        offsets, seen, obs_cols, smem=(0,), before=(xa,))
    obs = call(rows_kernel, [sds(Z, BX, BY)], offsets, obs, *send_rows(top, bottom), smem=(0,))
    parts = call(ratio_start_kernel, [SHARD] * 4, xa, yb, *rows_b, cols_a,
                 lxf, wyf, wrf, kzf, kzb, obs, scratch=[WHOLE, WHOLE])
    mats = group_matrices(notes)
    lx, wy, wr, lt = mats
    for step in range(ITERS):
        first = step == 0
        if not first:
            got = send_rows(top, bottom)
            packs = along_cols(call(shard_cols_kernel, [PACK], new, *got), -1)
            one, three = spread((1, 2), new, got, packs, mats)
            two, own = spread((3, 0), new, got, packs, mats, after=(one,))
            own, one, three, two = trade(own, one, three, two)
            parts = call(ratio_kernel, [SHARD] * 4, one, three, two, own, kzf, kzb, obs,
                         scratch=[WHOLE, WHOLE])
        own, one, three, two = trade(*parts)
        part = call(collect_first_kernel, [sds(12, 192, BY)], own, one, three, wy, wr)
        main, packs = call(collect_kernel, [sds(8, BY, BY), PACK], part, two, wy, wr, lt,
                           scratch=[pltpu.VMEM((12, BX, BY), F32)])
        own, up, down = call(add_cols_kernel, [sds(512, BY), EDGE, EDGE],
                             main, along_cols(packs, 1))
        extra = notes if first else ()
        mine = call(add_rows_kernel, [sds(512 + 8 * len(extra), BY)],
                    own, *send_rows(up, down), *extra)
        other = view_swap(mine, 1)
        if first:
            new, weight, top, bottom = call(
                functools.partial(update_kernel, True),
                [sds(512, BY), sds(512, BY), EDGE, EDGE],
                f, mine, other, scratch=[pltpu.VMEM((128, 128), F32)])
        else:
            new = call(functools.partial(update_kernel, False), [sds(512, BY)],
                       new, mine, other, weight)
    r1, r3 = view_swap(new, 2), view_swap(new, 6)
    a2, b2 = view_swap(r3[:256], 2), view_swap(r1[256:], 6)
    return call(gather_kernel, [sds(Z, BX, BY)], new, r1, r3, a2, b2)[None]


def solution(mesh):
    in_specs = (
        P("blk", None, None, None),
        P("view", "blk", None, None, None),
        P("view", None, None),
        P("view", None),
    )
    out_specs = P("blk", None, None, None)
    return jax.shard_map(local, mesh=mesh, in_specs=in_specs, out_specs=out_specs, check_vma=False)
```

time: 585 us -> 163 us (0.28)
  waiting for transfers between devices: 275 us -> 98.5 us
  local copies, waits for them, and re-layouts: 86.9 us -> 1.35 us
  matrix products: 48.2 us -> 0 us
  other arithmetic: 45.9 us -> 0 us
  blocking collectives: 42.4 us -> 0 us
  starting transfers between devices: 65.5 us -> 46.5 us
  between operations: 15.9 us -> 0.27 us
  Pallas kernels: 0 us -> 15.4 us
    psum x2 -> x0, waiting for transfers between devices: 180 us -> none  [local(): total = lax.psum(back, 'view')]
    slice x26 -> x2, local copies, waits for them, and re-layouts: 48.8 us -> 0.02 us  [local(): a2, b2 = (view_swap(r3[:256], 2), view_swap(r1[256:], 6))]
    dot_general x13 -> x0, matrix products: 48.2 us -> none  [the longest x4 28.6 us: operator(): along_x = jnp.einsum('xu,zuy->zxy', matrix_x, wide, precision=highest)]
    mul x8 -> x0, local copies, waits for them, and re-layouts: 27.4 us -> none  [the longest x4 13.7 us: full_rims(): right = right * (column < BLOCKS_Y - 1).astype(jnp.float32)]
    unnamed x1 -> x0, blocking collectives: 24 us -> none
    mul x8 -> x0, other arithmetic: 19.6 us -> none  [the longest x4 9.78 us: full_rims(): right = right * (column < BLOCKS_Y - 1).astype(jnp.float32)]
    ppermute x16 -> x36, starting transfers between devices: 65.4 us -> 46.5 us  [the longest x18 27.2 us: view_swap(): return lax.ppermute(x, 'view', [(i, i ^ mask) for i in range(8)])]
    all_gather x1 -> x0, blocking collectives: 18.4 us -> none  [local(): lax.all_gather(prof_y[None], 'view', axis=0, tiled=True)]
  transfers between devices with their start and end apart: 18 -> 36, of which waited for: 16 -> 27; matrix products, arithmetic and copies ran while one was open for 10% -> 0% of each run, Pallas kernels for 0% -> 3%
where the time goes in v1:
time: 163 us; the launch traced here: 162 us
  waiting for transfers between devices  98.5 us (60%)
  starting transfers between devices  46.5 us (29%)
  Pallas kernels  15.4 us (9%)
    ppermute x18, waiting for transfers between devices, view_swap(): return lax.ppermute(x, 'view', [(i, i ^ mask) for i in range(8)])  60.8 us
    ppermute x18, starting transfers between devices, view_swap(): return lax.ppermute(x, 'view', [(i, i ^ mask) for i in range(8)])  27.2 us
    ppermute x12, waiting for transfers between devices, along_rows(): return lax.ppermute(x, 'blk', [(i, (i + 4 * by) % 32) for i in range(32)])  22.2 us
    ppermute x12, starting transfers between devices, along_rows(): return lax.ppermute(x, 'blk', [(i, (i + 4 * by) % 32) for i in range(32)])  17 us
    ppermute x6, waiting for transfers between devices, along_cols(): lax.ppermute(x, 'blk', [(i, i // 4 * 4 + (i + by) % 4) for i in range(32)])  15.5 us
    pallas_call x25, Pallas kernels, call(): pl.pallas_call(inner, out_shape=out_shape, in_specs=specs, out_specs=[pl....  15.4 us
  transfers between devices with their start and end apart: 36, of which 27 were waited for; matrix products, arithmetic and copies ran while one was open for 0% of the time, Pallas kernels for 3%

profile of v1, /device:TPU:32, one launch (start us, length us, event | category | flops | bytes accessed | tf_op | source)
XLA Modules:
  0.0 162.0 jit_solution(8724558670929821359)
XLA Ops:
  6.7 3.1 %collective-permute-start.5 = (f32[8,128]{1,0:T(8,128)S(1)}, f32[8,128]{1,0:T(8,128)S(1)}, u32[]{:S(2)}, u32[]{:S(2)}) collective-permute-start(f32[8,128]{1,0:T(8,128)S(1)} %get-tuple-element.57.refs_0_.refs_3_), channel_id=1, source_target_pairs={{0,128},{32,160},{64,192},{96,224},{128,0},{160,32},{192,64},{224,... | collective-permute-start | bytes 12296 | tf_op jit(solution)/shard_map/ppermute | solution.py:526
  9.8 2.1 %collective-permute-done.5.refs_7_.refs_3_.refs_6_ = f32[8,128]{1,0:T(8,128)S(1)} collective-permute-done((f32[8,128]{1,0:T(8,128)S(1)}, f32[8,128]{1,0:T(8,128)S(1)}, u32[]{:S(2)}, u32[]{:S(2)}) %collective-permute-start.5) | collective-permute-done | bytes 4128 | tf_op jit(solution)/shard_map/ppermute | solution.py:526
  11.9 2.8 %collective-permute-start.4 = (f32[8,128]{1,0:T(8,128)S(1)}, f32[8,128]{1,0:T(8,128)S(1)}, u32[]{:S(2)}, u32[]{:S(2)}) collective-permute-start(f32[8,128]{1,0:T(8,128)S(1)} %get-tuple-element.57.refs_0_.refs_3_), channel_id=1, source_target_pairs={{0,192},{32,224},{64,128},{96,160},{128,64},{160,96},{192,0},{224,... | collective-permute-start | bytes 12296 | tf_op jit(solution)/shard_map/ppermute | solution.py:526
  21.9 2.2 %collective-permute-start.11 = (f32[32,16,128]{2,1,0:T(8,128)S(1)}, f32[32,16,128]{2,1,0:T(8,128)S(1)}, u32[]{:S(2)}, u32[]{:S(2)}) collective-permute-start(f32[32,16,128]{2,1,0:T(8,128)S(1)} %get-tuple-element.66), channel_id=1, source_target_pairs={{0,28},{1,29},{2,30},{3,31},{4,0},{5,1},{6,2},{7,3},{8,4},{9,5},{1... | collective-permute-start | bytes 786440 | tf_op jit(solution)/shard_map/ppermute | solution.py:518
  24.9 2.3 %collective-permute-start.7 = (f32[16,32,128]{2,1,0:T(8,128)S(1)}, f32[16,32,128]{2,1,0:T(8,128)S(1)}, u32[]{:S(2)}, u32[]{:S(2)}) collective-permute-start(f32[16,32,128]{2,1,0:T(8,128)S(1)} %get-tuple-element.60), channel_id=1, source_target_pairs={{0,28},{1,29},{2,30},{3,31},{4,0},{5,1},{6,2},{7,3},{8,4},{9,5},{1... | collective-permute-start | bytes 786440 | tf_op jit(solution)/shard_map/ppermute | solution.py:518
  30.1 4.1 %collective-permute-done.6.refs_2_ = f32[16,32,128]{2,1,0:T(8,128)S(1)} collective-permute-done((f32[16,32,128]{2,1,0:T(8,128)S(1)}, f32[16,32,128]{2,1,0:T(8,128)S(1)}, u32[]{:S(2)}, u32[]{:S(2)}) %collective-permute-start.6) | collective-permute-done | bytes 262176 | tf_op jit(solution)/shard_map/ppermute | solution.py:518
  34.9 2.1 %shard_map.54 = (f32[8,64,128]{2,1,0:T(8,128)S(1)}, f32[8,64,128]{2,1,0:T(8,128)S(1)}, f32[8,64,128]{2,1,0:T(8,128)S(1)}, f32[8,64,128]{2,1,0:T(8,128)S(1)}) custom-call(f32[16,64,128]{2,1,0:T(8,128)S(1)} %get-tuple-element.58.refs_0_, f32[16,64,128]{2,1,0:T(8,128)S(1)} %get-tuple-element.53.refs_0_.refs_1_, ...), custom_call_target="tpu_custom_call" | custom-call | flops 1000000 | bytes 4718592 | tf_op jit(solution)/shard_map/pallas_call | solution.py:51
  38.9 2.2 %collective-permute-start.14 = (f32[8,64,128]{2,1,0:T(8,128)S(1)}, f32[8,64,128]{2,1,0:T(8,128)S(1)}, u32[]{:S(2)}, u32[]{:S(2)}) collective-permute-start(f32[8,64,128]{2,1,0:T(8,128)S(1)} %get-tuple-element.72), channel_id=1, source_target_pairs={{0,128},{32,160},{64,192},{96,224},{128,0},{160,32},{192,64},{224,... | collective-permute-start | bytes 786440 | tf_op jit(solution)/shard_map/ppermute | solution.py:526
  41.8 4.5 %collective-permute-done.12.refs_1_ = f32[8,64,128]{2,1,0:T(8,128)S(1)} collective-permute-done((f32[8,64,128]{2,1,0:T(8,128)S(1)}, f32[8,64,128]{2,1,0:T(8,128)S(1)}, u32[]{:S(2)}, u32[]{:S(2)}) %collective-permute-start.12) | collective-permute-done | bytes 262176 | tf_op jit(solution)/shard_map/ppermute | solution.py:526
  46.3 5.7 %collective-permute-done.13.refs_2_ = f32[8,64,128]{2,1,0:T(8,128)S(1)} collective-permute-done((f32[8,64,128]{2,1,0:T(8,128)S(1)}, f32[8,64,128]{2,1,0:T(8,128)S(1)}, u32[]{:S(2)}, u32[]{:S(2)}) %collective-permute-start.13) | collective-permute-done | bytes 262176 | tf_op jit(solution)/shard_map/ppermute | solution.py:526
  53.5 5.8 %collective-permute-done.15.refs_1_ = f32[4,128,128]{2,1,0:T(8,128)S(1)} collective-permute-done((f32[4,128,128]{2,1,0:T(8,128)S(1)}, f32[4,128,128]{2,1,0:T(8,128)S(1)}, u32[]{:S(2)}, u32[]{:S(2)}) %collective-permute-start.15) | collective-permute-done | bytes 262176 | tf_op jit(solution)/shard_map/ppermute | solution.py:522
  59.5 3.3 %collective-permute-start.16 = (f32[8,32,128]{2,1,0:T(8,128)S(1)}, f32[8,32,128]{2,1,0:T(8,128)S(1)}, u32[]{:S(2)}, u32[]{:S(2)}) collective-permute-start(f32[8,32,128]{2,1,0:T(8,128)S(1)} %get-tuple-element.77), channel_id=1, source_target_pairs={{0,4},{1,5},{2,6},{3,7},{4,8},{5,9},{6,10},{7,11},{8,12},{9,13},{1... | collective-permute-start | bytes 393224 | tf_op jit(solution)/shard_map/ppermute | solution.py:518
  62.8 2.5 %collective-permute-done.16.refs_1_ = f32[8,32,128]{2,1,0:T(8,128)S(1)} collective-permute-done((f32[8,32,128]{2,1,0:T(8,128)S(1)}, f32[8,32,128]{2,1,0:T(8,128)S(1)}, u32[]{:S(2)}, u32[]{:S(2)}) %collective-permute-start.16) | collective-permute-done | bytes 131104 | tf_op jit(solution)/shard_map/ppermute | solution.py:518
  65.3 3.6 %collective-permute-done.17.refs_2_ = f32[8,32,128]{2,1,0:T(8,128)S(1)} collective-permute-done((f32[8,32,128]{2,1,0:T(8,128)S(1)}, f32[8,32,128]{2,1,0:T(8,128)S(1)}, u32[]{:S(2)}, u32[]{:S(2)}) %collective-permute-start.17) | collective-permute-done | bytes 131104 | tf_op jit(solution)/shard_map/ppermute | solution.py:518
  68.9 3.0 %collective-permute-start.18 = (f32[544,128]{1,0:T(8,128)S(1)}, f32[544,128]{1,0:T(8,128)S(1)}, u32[]{:S(2)}, u32[]{:S(2)}) collective-permute-start(f32[544,128]{1,0:T(8,128)S(1)} %shard_map.59.refs_1_), channel_id=1, source_target_pairs={{0,32},{32,0},{64,96},{96,64},{128,160},{160,128},{192,224},{224,1... | collective-permute-start | bytes 835592 | tf_op jit(solution)/shard_map/ppermute | solution.py:526
  71.9 5.2 %collective-permute-done.18.refs_2_ = f32[544,128]{1,0:T(8,128)S(1)} collective-permute-done((f32[544,128]{1,0:T(8,128)S(1)}, f32[544,128]{1,0:T(8,128)S(1)}, u32[]{:S(2)}, u32[]{:S(2)}) %collective-permute-start.18) | collective-permute-done | bytes 278560 | tf_op jit(solution)/shard_map/ppermute | solution.py:526
  77.6 2.1 %collective-permute-start.19 = (f32[8,32,128]{2,1,0:T(8,128)S(1)}, f32[8,32,128]{2,1,0:T(8,128)S(1)}, u32[]{:S(2)}, u32[]{:S(2)}) collective-permute-start(f32[8,32,128]{2,1,0:T(8,128)S(1)} %get-tuple-element.80), channel_id=1, source_target_pairs={{0,4},{1,5},{2,6},{3,7},{4,8},{5,9},{6,10},{7,11},{8,12},{9,13},{1... | collective-permute-start | bytes 393224 | tf_op jit(solution)/shard_map/ppermute | solution.py:518
  79.7 2.9 %collective-permute-done.19.refs_1_ = f32[8,32,128]{2,1,0:T(8,128)S(1)} collective-permute-done((f32[8,32,128]{2,1,0:T(8,128)S(1)}, f32[8,32,128]{2,1,0:T(8,128)S(1)}, u32[]{:S(2)}, u32[]{:S(2)}) %collective-permute-start.19) | collective-permute-done | bytes 131104 | tf_op jit(solution)/shard_map/ppermute | solution.py:518
  82.7 2.0 %collective-permute-done.20.refs_2_ = f32[8,32,128]{2,1,0:T(8,128)S(1)} collective-permute-done((f32[8,32,128]{2,1,0:T(8,128)S(1)}, f32[8,32,128]{2,1,0:T(8,128)S(1)}, u32[]{:S(2)}, u32[]{:S(2)}) %collective-permute-start.20) | collective-permute-done | bytes 131104 | tf_op jit(solution)/shard_map/ppermute | solution.py:518
  85.1 3.9 %collective-permute-done.21.refs_3_ = f32[4,128,128]{2,1,0:T(8,128)S(1)} collective-permute-done((f32[4,128,128]{2,1,0:T(8,128)S(1)}, f32[4,128,128]{2,1,0:T(8,128)S(1)}, u32[]{:S(2)}, u32[]{:S(2)}) %collective-permute-start.21) | collective-permute-done | bytes 262176 | tf_op jit(solution)/shard_map/ppermute | solution.py:522
  94.4 7.2 %collective-permute-done.24.refs_2_ = f32[8,64,128]{2,1,0:T(8,128)S(1)} collective-permute-done((f32[8,64,128]{2,1,0:T(8,128)S(1)}, f32[8,64,128]{2,1,0:T(8,128)S(1)}, u32[]{:S(2)}, u32[]{:S(2)}) %collective-permute-start.24) | collective-permute-done | bytes 262176 | tf_op jit(solution)/shard_map/ppermute | solution.py:526
  101.6 5.3 %collective-permute-done.23.refs_1_ = f32[8,64,128]{2,1,0:T(8,128)S(1)} collective-permute-done((f32[8,64,128]{2,1,0:T(8,128)S(1)}, f32[8,64,128]{2,1,0:T(8,128)S(1)}, u32[]{:S(2)}, u32[]{:S(2)}) %collective-permute-start.23) | collective-permute-done | bytes 262176 | tf_op jit(solution)/shard_map/ppermute | solution.py:526
  110.2 2.4 %collective-permute-start.27 = (f32[8,64,128]{2,1,0:T(8,128)S(1)}, f32[8,64,128]{2,1,0:T(8,128)S(1)}, u32[]{:S(2)}, u32[]{:S(2)}) collective-permute-start(f32[8,64,128]{2,1,0:T(8,128)S(1)} %get-tuple-element.90), channel_id=1, source_target_pairs={{0,128},{32,160},{64,192},{96,224},{128,0},{160,32},{192,64},{224,... | collective-permute-start | bytes 786440 | tf_op jit(solution)/shard_map/ppermute | solution.py:526
  112.6 5.1 %collective-permute-done.25.refs_1_ = f32[8,64,128]{2,1,0:T(8,128)S(1)} collective-permute-done((f32[8,64,128]{2,1,0:T(8,128)S(1)}, f32[8,64,128]{2,1,0:T(8,128)S(1)}, u32[]{:S(2)}, u32[]{:S(2)}) %collective-permute-start.25) | collective-permute-done | bytes 262176 | tf_op jit(solution)/shard_map/ppermute | solution.py:526
  117.7 6.1 %collective-permute-done.26.refs_2_ = f32[8,64,128]{2,1,0:T(8,128)S(1)} collective-permute-done((f32[8,64,128]{2,1,0:T(8,128)S(1)}, f32[8,64,128]{2,1,0:T(8,128)S(1)}, u32[]{:S(2)}, u32[]{:S(2)}) %collective-permute-start.26) | collective-permute-done | bytes 262176 | tf_op jit(solution)/shard_map/ppermute | solution.py:526
  125.3 5.8 %collective-permute-done.28.refs_1_ = f32[4,128,128]{2,1,0:T(8,128)S(1)} collective-permute-done((f32[4,128,128]{2,1,0:T(8,128)S(1)}, f32[4,128,128]{2,1,0:T(8,128)S(1)}, u32[]{:S(2)}, u32[]{:S(2)}) %collective-permute-start.28) | collective-permute-done | bytes 262176 | tf_op jit(solution)/shard_map/ppermute | solution.py:522
  133.3 2.9 %collective-permute-done.29.refs_1_ = f32[8,32,128]{2,1,0:T(8,128)S(1)} collective-permute-done((f32[8,32,128]{2,1,0:T(8,128)S(1)}, f32[8,32,128]{2,1,0:T(8,128)S(1)}, u32[]{:S(2)}, u32[]{:S(2)}) %collective-permute-start.29) | collective-permute-done | bytes 131104 | tf_op jit(solution)/shard_map/ppermute | solution.py:518
  137.7 3.1 %collective-permute-start.31 = (f32[512,128]{1,0:T(8,128)S(1)}, f32[512,128]{1,0:T(8,128)S(1)}, u32[]{:S(2)}, u32[]{:S(2)}) collective-permute-start(f32[512,128]{1,0:T(8,128)S(1)} %shard_map.68.refs_1_), channel_id=1, source_target_pairs={{0,32},{32,0},{64,96},{96,64},{128,160},{160,128},{192,224},{224,1... | collective-permute-start | bytes 786440 | tf_op jit(solution)/shard_map/ppermute | solution.py:526
  140.8 4.8 %collective-permute-done.31.refs_2_ = f32[512,128]{1,0:T(8,128)S(1)} collective-permute-done((f32[512,128]{1,0:T(8,128)S(1)}, f32[512,128]{1,0:T(8,128)S(1)}, u32[]{:S(2)}, u32[]{:S(2)}) %collective-permute-start.31) | collective-permute-done | bytes 262176 | tf_op jit(solution)/shard_map/ppermute | solution.py:526
  146.5 8.0 %collective-permute-done.33.refs_2_ = f32[512,128]{1,0:T(8,128)S(1)} collective-permute-done((f32[512,128]{1,0:T(8,128)S(1)}, f32[512,128]{1,0:T(8,128)S(1)}, u32[]{:S(2)}, u32[]{:S(2)}) %collective-permute-start.33) | collective-permute-done | bytes 262176 | tf_op jit(solution)/shard_map/ppermute | solution.py:526
  154.6 2.1 %collective-permute-start.35 = (f32[256,128]{1,0:T(8,128)S(1)}, f32[256,128]{1,0:T(8,128)S(1)}, u32[]{:S(2)}, u32[]{:S(2)}) collective-permute-start(f32[256,128]{1,0:T(8,128)S(1)} %slice.9), channel_id=1, source_target_pairs={{0,192},{32,224},{64,128},{96,160},{128,64},{160,96},{192,0},{224,... | collective-permute-start | bytes 393224 | tf_op jit(solution)/shard_map/ppermute | solution.py:526
  156.8 2.8 %collective-permute-done.34.refs_3_ = f32[256,128]{1,0:T(8,128)S(1)} collective-permute-done((f32[256,128]{1,0:T(8,128)S(1)}, f32[256,128]{1,0:T(8,128)S(1)}, u32[]{:S(2)}, u32[]{:S(2)}) %collective-permute-start.34) | collective-permute-done | bytes 131104 | tf_op jit(solution)/shard_map/ppermute | solution.py:526
  (78 shorter events, 40.7 us)
Async XLA Ops:
  1.5 17.2 %collective-permute-start.9 = (f32[16,64,128]{2,1,0:T(8,128)S(1)}, f32[16,64,128]{2,1,0:T(8,128)S(1)}, u32[]{:S(2)}, u32[]{:S(2)}) collective-permute-start(f32[16,64,128]{2,1,0:T(8,128)S(1)} %shard_map.51), channel_id=1, source_target_pairs={{0,3},{1,0},{2,1},{3,2},{4,7},{5,4},{6,5},{7,6},{8,11},{9,8},{10,9... | collective-permute-start | bytes 1572872 | tf_op jit(solution)/shard_map/ppermute | solution.py:522
  2.8 11.9 %collective-permute-start = (f32[8,64,128]{2,1,0:T(8,128)S(1)}, f32[8,64,128]{2,1,0:T(8,128)S(1)}, u32[]{:S(2)}, u32[]{:S(2)}) collective-permute-start(f32[8,64,128]{2,1,0:T(8,128)S(1)} %shard_map.46), channel_id=1, source_target_pairs={{0,3},{1,0},{2,1},{3,2},{4,7},{5,4},{6,5},{7,6},{8,11},{9,8},{10,9... | collective-permute-start | bytes 786440 | tf_op jit(solution)/shard_map/ppermute | solution.py:522
  3.5 14.7 %collective-permute-start.1 = (f32[16,32,128]{2,1,0:T(8,128)S(1)}, f32[16,32,128]{2,1,0:T(8,128)S(1)}, u32[]{:S(2)}, u32[]{:S(2)}) collective-permute-start(f32[16,32,128]{2,1,0:T(8,128)S(1)} %get-tuple-element.54), channel_id=1, source_target_pairs={{0,4},{1,5},{2,6},{3,7},{4,8},{5,9},{6,10},{7,11},{8,12},{9,13},{1... | collective-permute-start | bytes 786440 | tf_op jit(solution)/shard_map/ppermute | solution.py:518
  5.5 12.8 %collective-permute-start.2 = (f32[16,32,128]{2,1,0:T(8,128)S(1)}, f32[16,32,128]{2,1,0:T(8,128)S(1)}, u32[]{:S(2)}, u32[]{:S(2)}) collective-permute-start(f32[16,32,128]{2,1,0:T(8,128)S(1)} %get-tuple-element.55), channel_id=1, source_target_pairs={{0,28},{1,29},{2,30},{3,31},{4,0},{5,1},{6,2},{7,3},{8,4},{9,5},{1... | collective-permute-start | bytes 786440 | tf_op jit(solution)/shard_map/ppermute | solution.py:518
  6.7 5.2 %collective-permute-start.5 = (f32[8,128]{1,0:T(8,128)S(1)}, f32[8,128]{1,0:T(8,128)S(1)}, u32[]{:S(2)}, u32[]{:S(2)}) collective-permute-start(f32[8,128]{1,0:T(8,128)S(1)} %get-tuple-element.57.refs_0_.refs_3_), channel_id=1, source_target_pairs={{0,128},{32,160},{64,192},{96,224},{128,0},{160,32},{192,64},{224,... | collective-permute-start | bytes 12296 | tf_op jit(solution)/shard_map/ppermute | solution.py:526
  19.9 8.5 %collective-permute-start.10 = (f32[32,16,128]{2,1,0:T(8,128)S(1)}, f32[32,16,128]{2,1,0:T(8,128)S(1)}, u32[]{:S(2)}, u32[]{:S(2)}) collective-permute-start(f32[32,16,128]{2,1,0:T(8,128)S(1)} %get-tuple-element.65), channel_id=1, source_target_pairs={{0,4},{1,5},{2,6},{3,7},{4,8},{5,9},{6,10},{7,11},{8,12},{9,13},{1... | collective-permute-start | bytes 786440 | tf_op jit(solution)/shard_map/ppermute | solution.py:518
  21.9 7.4 %collective-permute-start.11 = (f32[32,16,128]{2,1,0:T(8,128)S(1)}, f32[32,16,128]{2,1,0:T(8,128)S(1)}, u32[]{:S(2)}, u32[]{:S(2)}) collective-permute-start(f32[32,16,128]{2,1,0:T(8,128)S(1)} %get-tuple-element.66), channel_id=1, source_target_pairs={{0,28},{1,29},{2,30},{3,31},{4,0},{5,1},{6,2},{7,3},{8,4},{9,5},{1... | collective-permute-start | bytes 786440 | tf_op jit(solution)/shard_map/ppermute | solution.py:518
  24.1 6.0 %collective-permute-start.8 = (f32[8,64,128]{2,1,0:T(8,128)S(1)}, f32[8,64,128]{2,1,0:T(8,128)S(1)}, u32[]{:S(2)}, u32[]{:S(2)}) collective-permute-start(f32[8,64,128]{2,1,0:T(8,128)S(1)} %get-tuple-element.61), channel_id=1, source_target_pairs={{0,3},{1,0},{2,1},{3,2},{4,7},{5,4},{6,5},{7,6},{8,11},{9,8},{10,9... | collective-permute-start | bytes 786440 | tf_op jit(solution)/shard_map/ppermute | solution.py:522
  24.1 10.1 %collective-permute-start.6 = (f32[16,32,128]{2,1,0:T(8,128)S(1)}, f32[16,32,128]{2,1,0:T(8,128)S(1)}, u32[]{:S(2)}, u32[]{:S(2)}) collective-permute-start(f32[16,32,128]{2,1,0:T(8,128)S(1)} %get-tuple-element.59), channel_id=1, source_target_pairs={{0,4},{1,5},{2,6},{3,7},{4,8},{5,9},{6,10},{7,11},{8,12},{9,13},{1... | collective-permute-start | bytes 786440 | tf_op jit(solution)/shard_map/ppermute | solution.py:518
  24.9 10.0 %collective-permute-start.7 = (f32[16,32,128]{2,1,0:T(8,128)S(1)}, f32[16,32,128]{2,1,0:T(8,128)S(1)}, u32[]{:S(2)}, u32[]{:S(2)}) collective-permute-start(f32[16,32,128]{2,1,0:T(8,128)S(1)} %get-tuple-element.60), channel_id=1, source_target_pairs={{0,28},{1,29},{2,30},{3,31},{4,0},{5,1},{6,2},{7,3},{8,4},{9,5},{1... | collective-permute-start | bytes 786440 | tf_op jit(solution)/shard_map/ppermute | solution.py:518
  37.0 9.3 %collective-permute-start.12 = (f32[8,64,128]{2,1,0:T(8,128)S(1)}, f32[8,64,128]{2,1,0:T(8,128)S(1)}, u32[]{:S(2)}, u32[]{:S(2)}) collective-permute-start(f32[8,64,128]{2,1,0:T(8,128)S(1)} %get-tuple-element.68), channel_id=1, source_target_pairs={{0,64},{32,96},{64,0},{96,32},{128,192},{160,224},{192,128},{224,1... | collective-permute-start | bytes 786440 | tf_op jit(solution)/shard_map/ppermute | solution.py:526
  37.3 14.7 %collective-permute-start.13 = (f32[8,64,128]{2,1,0:T(8,128)S(1)}, f32[8,64,128]{2,1,0:T(8,128)S(1)}, u32[]{:S(2)}, u32[]{:S(2)}) collective-permute-start(f32[8,64,128]{2,1,0:T(8,128)S(1)} %get-tuple-element.69), channel_id=1, source_target_pairs={{0,192},{32,224},{64,128},{96,160},{128,64},{160,96},{192,0},{224,... | collective-permute-start | bytes 786440 | tf_op jit(solution)/shard_map/ppermute | solution.py:526
  38.9 13.8 %collective-permute-start.14 = (f32[8,64,128]{2,1,0:T(8,128)S(1)}, f32[8,64,128]{2,1,0:T(8,128)S(1)}, u32[]{:S(2)}, u32[]{:S(2)}) collective-permute-start(f32[8,64,128]{2,1,0:T(8,128)S(1)} %get-tuple-element.72), channel_id=1, source_target_pairs={{0,128},{32,160},{64,192},{96,224},{128,0},{160,32},{192,64},{224,... | collective-permute-start | bytes 786440 | tf_op jit(solution)/shard_map/ppermute | solution.py:526
  53.4 5.9 %collective-permute-start.15 = (f32[4,128,128]{2,1,0:T(8,128)S(1)}, f32[4,128,128]{2,1,0:T(8,128)S(1)}, u32[]{:S(2)}, u32[]{:S(2)}) collective-permute-start(f32[4,128,128]{2,1,0:T(8,128)S(1)} %get-tuple-element.75), channel_id=1, source_target_pairs={{0,1},{1,2},{2,3},{3,0},{4,5},{5,6},{6,7},{7,4},{8,9},{9,10},{10,1... | collective-permute-start | bytes 786440 | tf_op jit(solution)/shard_map/ppermute | solution.py:522
  59.5 5.8 %collective-permute-start.16 = (f32[8,32,128]{2,1,0:T(8,128)S(1)}, f32[8,32,128]{2,1,0:T(8,128)S(1)}, u32[]{:S(2)}, u32[]{:S(2)}) collective-permute-start(f32[8,32,128]{2,1,0:T(8,128)S(1)} %get-tuple-element.77), channel_id=1, source_target_pairs={{0,4},{1,5},{2,6},{3,7},{4,8},{5,9},{6,10},{7,11},{8,12},{9,13},{1... | collective-permute-start | bytes 393224 | tf_op jit(solution)/shard_map/ppermute | solution.py:518
  62.8 6.1 %collective-permute-start.17 = (f32[8,32,128]{2,1,0:T(8,128)S(1)}, f32[8,32,128]{2,1,0:T(8,128)S(1)}, u32[]{:S(2)}, u32[]{:S(2)}) collective-permute-start(f32[8,32,128]{2,1,0:T(8,128)S(1)} %get-tuple-element.78), channel_id=1, source_target_pairs={{0,28},{1,29},{2,30},{3,31},{4,0},{5,1},{6,2},{7,3},{8,4},{9,5},{1... | collective-permute-start | bytes 393224 | tf_op jit(solution)/shard_map/ppermute | solution.py:518
  68.9 8.1 %collective-permute-start.18 = (f32[544,128]{1,0:T(8,128)S(1)}, f32[544,128]{1,0:T(8,128)S(1)}, u32[]{:S(2)}, u32[]{:S(2)}) collective-permute-start(f32[544,128]{1,0:T(8,128)S(1)} %shard_map.59.refs_1_), channel_id=1, source_target_pairs={{0,32},{32,0},{64,96},{96,64},{128,160},{160,128},{192,224},{224,1... | collective-permute-start | bytes 835592 | tf_op jit(solution)/shard_map/ppermute | solution.py:526
  77.6 5.0 %collective-permute-start.19 = (f32[8,32,128]{2,1,0:T(8,128)S(1)}, f32[8,32,128]{2,1,0:T(8,128)S(1)}, u32[]{:S(2)}, u32[]{:S(2)}) collective-permute-start(f32[8,32,128]{2,1,0:T(8,128)S(1)} %get-tuple-element.80), channel_id=1, source_target_pairs={{0,4},{1,5},{2,6},{3,7},{4,8},{5,9},{6,10},{7,11},{8,12},{9,13},{1... | collective-permute-start | bytes 393224 | tf_op jit(solution)/shard_map/ppermute | solution.py:518
  79.7 5.0 %collective-permute-start.20 = (f32[8,32,128]{2,1,0:T(8,128)S(1)}, f32[8,32,128]{2,1,0:T(8,128)S(1)}, u32[]{:S(2)}, u32[]{:S(2)}) collective-permute-start(f32[8,32,128]{2,1,0:T(8,128)S(1)} %get-tuple-element.81), channel_id=1, source_target_pairs={{0,28},{1,29},{2,30},{3,31},{4,0},{5,1},{6,2},{7,3},{8,4},{9,5},{1... | collective-permute-start | bytes 393224 | tf_op jit(solution)/shard_map/ppermute | solution.py:518
  90.8 10.8 %collective-permute-start.24 = (f32[8,64,128]{2,1,0:T(8,128)S(1)}, f32[8,64,128]{2,1,0:T(8,128)S(1)}, u32[]{:S(2)}, u32[]{:S(2)}) collective-permute-start(f32[8,64,128]{2,1,0:T(8,128)S(1)} %get-tuple-element.85), channel_id=1, source_target_pairs={{0,128},{32,160},{64,192},{96,224},{128,0},{160,32},{192,64},{224,... | collective-permute-start | bytes 786440 | tf_op jit(solution)/shard_map/ppermute | solution.py:526
  92.0 15.0 %collective-permute-start.23 = (f32[8,64,128]{2,1,0:T(8,128)S(1)}, f32[8,64,128]{2,1,0:T(8,128)S(1)}, u32[]{:S(2)}, u32[]{:S(2)}) collective-permute-start(f32[8,64,128]{2,1,0:T(8,128)S(1)} %get-tuple-element.84), channel_id=1, source_target_pairs={{0,192},{32,224},{64,128},{96,160},{128,64},{160,96},{192,0},{224,... | collective-permute-start | bytes 786440 | tf_op jit(solution)/shard_map/ppermute | solution.py:526
  94.0 13.0 %collective-permute-start.22 = (f32[8,64,128]{2,1,0:T(8,128)S(1)}, f32[8,64,128]{2,1,0:T(8,128)S(1)}, u32[]{:S(2)}, u32[]{:S(2)}) collective-permute-start(f32[8,64,128]{2,1,0:T(8,128)S(1)} %get-tuple-element.83.refs_7_), channel_id=1, source_target_pairs={{0,64},{32,96},{64,0},{96,32},{128,192},{160,224},{192,128},{224,1... | collective-permute-start | bytes 786440 | tf_op jit(solution)/shard_map/ppermute | solution.py:526
  108.4 9.2 %collective-permute-start.25 = (f32[8,64,128]{2,1,0:T(8,128)S(1)}, f32[8,64,128]{2,1,0:T(8,128)S(1)}, u32[]{:S(2)}, u32[]{:S(2)}) collective-permute-start(f32[8,64,128]{2,1,0:T(8,128)S(1)} %get-tuple-element.88), channel_id=1, source_target_pairs={{0,64},{32,96},{64,0},{96,32},{128,192},{160,224},{192,128},{224,1... | collective-permute-start | bytes 786440 | tf_op jit(solution)/shard_map/ppermute | solution.py:526
  108.5 15.2 %collective-permute-start.26 = (f32[8,64,128]{2,1,0:T(8,128)S(1)}, f32[8,64,128]{2,1,0:T(8,128)S(1)}, u32[]{:S(2)}, u32[]{:S(2)}) collective-permute-start(f32[8,64,128]{2,1,0:T(8,128)S(1)} %get-tuple-element.89), channel_id=1, source_target_pairs={{0,192},{32,224},{64,128},{96,160},{128,64},{160,96},{192,0},{224,... | collective-permute-start | bytes 786440 | tf_op jit(solution)/shard_map/ppermute | solution.py:526
  110.2 14.3 %collective-permute-start.27 = (f32[8,64,128]{2,1,0:T(8,128)S(1)}, f32[8,64,128]{2,1,0:T(8,128)S(1)}, u32[]{:S(2)}, u32[]{:S(2)}) collective-permute-start(f32[8,64,128]{2,1,0:T(8,128)S(1)} %get-tuple-element.90), channel_id=1, source_target_pairs={{0,128},{32,160},{64,192},{96,224},{128,0},{160,32},{192,64},{224,... | collective-permute-start | bytes 786440 | tf_op jit(solution)/shard_map/ppermute | solution.py:526
  125.2 5.9 %collective-permute-start.28 = (f32[4,128,128]{2,1,0:T(8,128)S(1)}, f32[4,128,128]{2,1,0:T(8,128)S(1)}, u32[]{:S(2)}, u32[]{:S(2)}) collective-permute-start(f32[4,128,128]{2,1,0:T(8,128)S(1)} %get-tuple-element.92), channel_id=1, source_target_pairs={{0,1},{1,2},{2,3},{3,0},{4,5},{5,6},{6,7},{7,4},{8,9},{9,10},{10,1... | collective-permute-start | bytes 786440 | tf_op jit(solution)/shard_map/ppermute | solution.py:522
  131.2 5.0 %collective-permute-start.29 = (f32[8,32,128]{2,1,0:T(8,128)S(1)}, f32[8,32,128]{2,1,0:T(8,128)S(1)}, u32[]{:S(2)}, u32[]{:S(2)}) collective-permute-start(f32[8,32,128]{2,1,0:T(8,128)S(1)} %get-tuple-element.94), channel_id=1, source_target_pairs={{0,4},{1,5},{2,6},{3,7},{4,8},{5,9},{6,10},{7,11},{8,12},{9,13},{1... | collective-permute-start | bytes 393224 | tf_op jit(solution)/shard_map/ppermute | solution.py:518
  137.7 8.0 %collective-permute-start.31 = (f32[512,128]{1,0:T(8,128)S(1)}, f32[512,128]{1,0:T(8,128)S(1)}, u32[]{:S(2)}, u32[]{:S(2)}) collective-permute-start(f32[512,128]{1,0:T(8,128)S(1)} %shard_map.68.refs_1_), channel_id=1, source_target_pairs={{0,32},{32,0},{64,96},{96,64},{128,160},{160,128},{192,224},{224,1... | collective-permute-start | bytes 786440 | tf_op jit(solution)/shard_map/ppermute | solution.py:526
  145.7 8.8 %collective-permute-start.33 = (f32[512,128]{1,0:T(8,128)S(1)}, f32[512,128]{1,0:T(8,128)S(1)}, u32[]{:S(2)}, u32[]{:S(2)}) collective-permute-start(f32[512,128]{1,0:T(8,128)S(1)} %shard_map.69.refs_0_), channel_id=1, source_target_pairs={{0,192},{32,224},{64,128},{96,160},{128,64},{160,96},{192,0},{224,... | collective-permute-start | bytes 786440 | tf_op jit(solution)/shard_map/ppermute | solution.py:526
  146.4 8.2 %collective-permute-start.32 = (f32[512,128]{1,0:T(8,128)S(1)}, f32[512,128]{1,0:T(8,128)S(1)}, u32[]{:S(2)}, u32[]{:S(2)}) collective-permute-start(f32[512,128]{1,0:T(8,128)S(1)} %shard_map.69.refs_0_), channel_id=1, source_target_pairs={{0,64},{32,96},{64,0},{96,32},{128,192},{160,224},{192,128},{224,1... | collective-permute-start | bytes 786440 | tf_op jit(solution)/shard_map/ppermute | solution.py:526
  154.5 5.1 %collective-permute-start.34 = (f32[256,128]{1,0:T(8,128)S(1)}, f32[256,128]{1,0:T(8,128)S(1)}, u32[]{:S(2)}, u32[]{:S(2)}) collective-permute-start(f32[256,128]{1,0:T(8,128)S(1)} %slice.8), channel_id=1, source_target_pairs={{0,64},{32,96},{64,0},{96,32},{128,192},{160,224},{192,128},{224,1... | collective-permute-start | bytes 393224 | tf_op jit(solution)/shard_map/ppermute | solution.py:526
  154.6 6.3 %collective-permute-start.35 = (f32[256,128]{1,0:T(8,128)S(1)}, f32[256,128]{1,0:T(8,128)S(1)}, u32[]{:S(2)}, u32[]{:S(2)}) collective-permute-start(f32[256,128]{1,0:T(8,128)S(1)} %slice.9), channel_id=1, source_target_pairs={{0,192},{32,224},{64,128},{96,160},{128,64},{160,96},{192,0},{224,... | collective-permute-start | bytes 393224 | tf_op jit(solution)/shard_map/ppermute | solution.py:526
  (9 other events, 30.8 us)

commit v2 on v1

--- a/solution.py
+++ b/solution.py
@@ -189,28 +189,38 @@
 TAP_SCRATCH = [pltpu.VMEM((8, BY), F32), pltpu.VMEM((8, 1024), F32)]
 
 
-def own_matrices(offs, taps):
+def own_matrices(offs, taps, **more):
     return call(own_kernel, [LX, WY, WR, KZ, KZ, sds(PROF, 128)], offs, taps, smem=(0,),
-                scratch=TAP_SCRATCH)
-
-
-def group_kernel(n0, n1, n2, n3, lx, wy, wr, lt, full, rows):
+                scratch=TAP_SCRATCH, **more)
+
+
+def view_matrices(note, lx, wy, wr, lt, j, full, rows):
     s, cs = block_start()
-    for j, note in enumerate((n0, n1, n2, n3)):
-        tap_rows(note[:3, :TAPS], full, rows, False)
-        shifts = note[3:4]
-        ox = shifts[:, 0:1].astype(jnp.int32)
-        oy = shifts[:, 1:2].astype(jnp.int32)
-        put_x(lx.at[j], x_band(rows, 1, s, ox))
-        put_y(wy.at[j], wr.at[j], y_band(rows, 2, cs, oy))
-        hi, lo = split(x_band_turned(rows, 0, s, ox))
-        lt[0, :, j * BX : (j + 1) * BX] = hi
-        lt[1, :, j * BX : (j + 1) * BX] = lo
-
-
-def group_matrices(notes):
-    many = lambda v: sds(4, *v.shape, dtype=v.dtype)
-    return call(group_kernel, [many(LX), many(WY), many(WR), LT], *notes, scratch=TAP_SCRATCH)
+    tap_rows(note[:3, :TAPS], full, rows, False)
+    shifts = note[3:4]
+    ox = shifts[:, 0:1].astype(jnp.int32)
+    oy = shifts[:, 1:2].astype(jnp.int32)
+    put_x(lx, x_band(rows, 1, s, ox))
+    put_y(wy, wr, y_band(rows, 2, cs, oy))
+    hi, lo = split(x_band_turned(rows, 0, s, ox))
+    lt[0, :, j * BX : (j + 1) * BX] = hi
+    lt[1, :, j * BX : (j + 1) * BX] = lo
+
+
+def near_matrices_kernel(note, m1, m3, lx, wy, wr, lt, full, rows):
+    lt[...] = jnp.zeros_like(lt)
+    for j, ref in enumerate((note, m1, m3)):
+        one = ref[...] if j == 0 else ref[512:]
+        view_matrices(one, lx.at[j], wy.at[j], wr.at[j], lt, j, full, rows)
+
+
+def far_matrices_kernel(m2, old, lx, wy, wr, lt, full, rows):
+    lt[...] = old[...]
+    view_matrices(m2[512:], lx.at[0], wy.at[0], wr.at[0], lt, 3, full, rows)
+
+
+def many(count):
+    return [sds(count, *v.shape, dtype=v.dtype) for v in (LX, WY, WR)] + [LT]
 
 
 def row_rims(planes, top, bottom):
@@ -327,34 +337,44 @@
                 *src, *rows, lx, **more)
 
 
-def ratio_core(tmp, kf, kb, obs, out, sends):
+def ratio_core(load, kf, kb, obs, out, sends):
     for t in range(BX // 16):
         cut = [slice(16 * t, 16 * t + 8), slice(16 * t + 8, 16 * t + 16)]
-        blurred = z_filter(kf, jnp.concatenate([tmp[:, c, :].reshape(256, BY) for c in cut], axis=1))
+        blurred = z_filter(kf, jnp.concatenate([load(c) for c in cut], axis=1))
         seen = jnp.concatenate([obs[:, c, :].reshape(256, BY) for c in cut], axis=1)
         back = z_filter(kb, seen / blurred)
         for i, c in enumerate(cut):
             out[:, c, :] = back[:, i * BY : (i + 1) * BY].reshape(Z, 8, BY)
     x = lax.axis_index("view") // 2
     for j, send in zip(ORDER, sends):
-        send[...] = out[pl.ds(8 * (x ^ j), 8)]
-
-
-def ratio_start_kernel(xa, yb, above, below, packs, lx, wy, wr, kf, kb, obs,
-                       s0, s1, s3, s2, tmp, out):
-    y_filter(wy, wr, planes_of(xa), packs, storer(tmp))
-    x_filter(lx, planes_of(yb), above, below, storer(tmp, lambda k: HALF_Z + k))
-    ratio_core(tmp, kf, kb, obs, out, (s0, s1, s3, s2))
+        send[:512] = out[pl.ds(8 * (x ^ j), 8)].reshape(512, BY)
+
+
+def second_x_kernel(yb, above, below, lx, out):
+    x_filter(lx, planes_of(yb), above, below, storer(out))
+
+
+def second_y_kernel(xa, packs, wy, wr, out):
+    y_filter(wy, wr, planes_of(xa), packs, storer(out))
+
+
+def ratio_start_kernel(ga, gb, kf, kb, obs, note, s0, s1, s3, s2, out):
+    def load(c):
+        return jnp.concatenate([ga[:, c, :], gb[:, c, :]], axis=0).reshape(256, BY)
+
+    ratio_core(load, kf, kb, obs, out, (s0, s1, s3, s2))
+    for send in (s1, s3, s2):
+        send[512:] = note[...]
 
 
 def ratio_kernel(g1, g3, g2, g0, kf, kb, obs, s0, s1, s3, s2, tmp, out):
     x = lax.axis_index("view") // 2
     for j, got in zip(ORDER, (g0, g1, g3, g2)):
-        tmp[pl.ds(8 * (x ^ j), 8)] = got[...]
-    ratio_core(tmp, kf, kb, obs, out, (s0, s1, s3, s2))
-
-
-SHARD = sds(8, BX, BY)
+        tmp[pl.ds(8 * (x ^ j), 8)] = got[...].reshape(8, BX, BY)
+    ratio_core(lambda c: tmp[:, c, :].reshape(256, BY), kf, kb, obs, out, (s0, s1, s3, s2))
+
+
+SHARD, NOTED = sds(512, BY), sds(520, BY)
 EDGE = sds(8, RIM, BY)
 PACK = sds(4, BY, BY)
 WHOLE = pltpu.VMEM((Z, BX, BY), F32)
@@ -366,33 +386,39 @@
     col_rims(planes, out)
 
 
-def spread_kernel(picks, own, above, below, packs, lx, wy, wr, *refs):
-    outs, mid = refs[:-1], refs[-1]
+def spread_kernel(picks, own, above, below, packs, *refs):
+    count = len(picks)
+    mats, outs, mid = refs[: 3 * count], refs[3 * count : -1], refs[-1]
     tiles = [jnp.concatenate([above[k], own[k * BX : (k + 1) * BX], below[k]], axis=0)
              for k in range(8)]
     tiles += [packs[k] for k in range(4)]
     for g in range(6):
         hi, lo = split(jnp.concatenate(tiles[2 * g : 2 * g + 2], axis=1))
         both = jnp.concatenate([hi, lo], axis=0)
-        for n, j in enumerate(picks):
-            o = dot(lx[j], both)
+        for n in range(count):
+            o = dot(mats[3 * n][picks[n]], both)
             o = o[:BX] + o[BX:]
             mid[n, 2 * g] = o[:, :BY]
             mid[n, 2 * g + 1] = o[:, BY:]
-    for n, j in enumerate(picks):
-        y_filter(wy.at[j], wr.at[j], [mid[n, k] for k in range(8)],
-                 [mid[n, 8 + k] for k in range(4)], storer(outs[n]))
+    for n in range(count):
+        out = outs[n]
+
+        def put(k, v, out=out):
+            out[k * BX : (k + 1) * BX] = v
+
+        y_filter(mats[3 * n + 1].at[picks[n]], mats[3 * n + 2].at[picks[n]],
+                 [mid[n, k] for k in range(8)], [mid[n, 8 + k] for k in range(4)], put)
 
 
 def spread(picks, new, got, packs, mats, **more):
     return call(functools.partial(spread_kernel, picks), [SHARD] * len(picks),
-                new, *got, packs, *mats[:3], **more,
+                new, *got, packs, *mats, **more,
                 scratch=[pltpu.VMEM((len(picks), 12, BX, BY), F32)])
 
 
 def collect_columns(r, w, rims, put):
     for g in range(2):
-        planes = [r[4 * g + q] for q in range(4)]
+        planes = [r[(4 * g + q) * BX : (4 * g + q + 1) * BX] for q in range(4)]
         hi, lo = split(jnp.concatenate(planes, axis=0))
         o = dot_turned(hi, w[:, :BY]) + dot_turned(hi, w[:, BY:]) + dot_turned(lo, w[:, :BY])
         for q in range(4):
@@ -416,7 +442,7 @@
     def put_late(k, v):
         late[k] = v
 
-    collect_columns(r2, wy.at[3], wr.at[3], put_late)
+    collect_columns(r2, wy.at[0], wr.at[0], put_late)
     for g in range(6):
         both = [jnp.concatenate([part[k], late[k]], axis=0) for k in (2 * g, 2 * g + 1)]
         hi, lo = split(jnp.concatenate(both, axis=1))
@@ -448,7 +474,11 @@
         out[r : r + RIM] = own[r : r + RIM] + above[k]
         out[r + RIM : r + BX] = own[r + RIM : r + BX] + below[k]
     for j, note in enumerate(notes):
-        out[512 + 8 * j : 520 + 8 * j] = note[...]
+        out[512 + 8 * j : 520 + 8 * j] = note[...] if j == 0 else note[512:]
+
+
+def touch_kernel(out):
+    out[...] = jnp.zeros_like(out)
 
 
 def update_kernel(first, *refs):
@@ -484,13 +514,10 @@
             bottom[k] = new[(k + 1) * BX - RIM : (k + 1) * BX]
 
 
-def gather_kernel(own, r1, r3, a2, b2, f):
+def gather_kernel(own, one, three, two, f):
     x = lax.axis_index("view") // 2
-    f[pl.ds(8 * x, 8)] = own[...].reshape(8, BX, BY)
-    f[pl.ds(8 * (x ^ 1), 8)] = r1[...].reshape(8, BX, BY)
-    f[pl.ds(8 * (x ^ 3), 8)] = r3[...].reshape(8, BX, BY)
-    f[pl.ds(8 * (x ^ 2), 4)] = a2[...].reshape(4, BX, BY)
-    f[pl.ds(8 * (x ^ 2) + 4, 4)] = b2[...].reshape(4, BX, BY)
+    for j, ref in zip(ORDER, (own, one, three, two)):
+        f[pl.ds(8 * (x ^ j), 8)] = ref[...].reshape(8, BX, BY)
 
 
 def cols_kernel(offs, obs, packs, out, top, bottom):
@@ -530,43 +557,52 @@
     return along_rows(bottom, 1), along_rows(top, -1)
 
 
-def trade(own, one, three, two):
-    return own, view_swap(one, 2), view_swap(three, 6), view_swap(two, 4)
+def trade(*parts):
+    return [p if j == 0 else view_swap(p, 2 * j) for j, p in zip(ORDER, parts)]
 
 
 def local(estimate, observed, kernels, offsets):
     f = estimate[0]
     seen = observed[0, 0]
-    cols_b = along_cols(call(functools.partial(col_rims_kernel, 1), COLS, f), -1)
-    rows_a = send_rows(*call(functools.partial(row_rims_kernel, 0), ROWS, f))
-    lxf, wyf, wrf, kzf, kzb, note = own_matrices(offsets, kernels)
-    notes = trade(note, note, note, note)
-    yb, *rims = y_first((f,), 1, cols_b, wyf, wrf)
-    rows_b = send_rows(*rims)
-    xa, packs = x_first((f,), 0, rows_a, lxf, before=(yb,), after=notes[1:])
-    cols_a = along_cols(packs, -1)
-    obs_cols = along_cols(call(obs_cols_kernel, [sds(Z // 2, BX, BY)], seen), -1)
+    packs = call(functools.partial(col_rims_kernel, 1), COLS, f)
+    cols_b = along_cols(packs, -1)
+    edges = call(functools.partial(row_rims_kernel, 0), ROWS, f, before=(packs,))
+    rows_a = send_rows(*edges)
+    lxf, wyf, wrf, kzf, kzb, note = own_matrices(offsets, kernels, before=edges[:1])
+    obs_packs = call(obs_cols_kernel, [sds(Z // 2, BX, BY)], seen, before=edges[:1])
+    obs_cols = along_cols(obs_packs, -1)
     obs, top, bottom = call(
         cols_kernel, [sds(Z, BX, BY), sds(Z, SHIFT, BY), sds(Z, SHIFT, BY)],
-        offsets, seen, obs_cols, smem=(0,), before=(xa,))
-    obs = call(rows_kernel, [sds(Z, BX, BY)], offsets, obs, *send_rows(top, bottom), smem=(0,))
-    parts = call(ratio_start_kernel, [SHARD] * 4, xa, yb, *rows_b, cols_a,
-                 lxf, wyf, wrf, kzf, kzb, obs, scratch=[WHOLE, WHOLE])
-    mats = group_matrices(notes)
-    lx, wy, wr, lt = mats
+        offsets, seen, obs_cols, smem=(0,))
+    above, below = send_rows(top, bottom)
+    xa, packs = x_first((f,), 0, rows_a, lxf, before=(obs,))
+    cols_a = along_cols(packs, -1)
+    yb, *rims = y_first((f,), 1, cols_b, wyf, wrf, before=(xa,))
+    rows_b = send_rows(*rims)
+    obs = call(rows_kernel, [sds(Z, BX, BY)], offsets, obs, above, below, smem=(0,),
+               before=(yb,))
+    ga = call(second_y_kernel, [HALF], xa, cols_a, wyf, wrf, before=(obs,))
+    gb = call(second_x_kernel, [HALF], yb, *rows_b, lxf, before=(ga,))
+    parts = call(ratio_start_kernel, [SHARD] + [NOTED] * 3, ga, gb, kzf, kzb, obs, note,
+                 scratch=[WHOLE])
     for step in range(ITERS):
         first = step == 0
         if not first:
             got = send_rows(top, bottom)
             packs = along_cols(call(shard_cols_kernel, [PACK], new, *got), -1)
-            one, three = spread((1, 2), new, got, packs, mats)
-            two, own = spread((3, 0), new, got, packs, mats, after=(one,))
+            one, three = spread((1, 2), new, got, packs, [*near[:3], *near[:3]])
+            two, own = spread((0, 0), new, got, packs, [*far[:3], *near[:3]], after=(one,))
             own, one, three, two = trade(own, one, three, two)
+            mark = call(touch_kernel, [sds(8, BY)], before=(one, three))
             parts = call(ratio_kernel, [SHARD] * 4, one, three, two, own, kzf, kzb, obs,
-                         scratch=[WHOLE, WHOLE])
+                         before=(mark,), scratch=[WHOLE, WHOLE])
         own, one, three, two = trade(*parts)
-        part = call(collect_first_kernel, [sds(12, 192, BY)], own, one, three, wy, wr)
-        main, packs = call(collect_kernel, [sds(8, BY, BY), PACK], part, two, wy, wr, lt,
+        if first:
+            near = call(near_matrices_kernel, many(3), note, one, three, scratch=TAP_SCRATCH)
+            far = call(far_matrices_kernel, many(1), two, near[3], scratch=TAP_SCRATCH)
+            notes = (note, one, three, two)
+        part = call(collect_first_kernel, [sds(12, 192, BY)], own, one, three, *near[1:3])
+        main, packs = call(collect_kernel, [sds(8, BY, BY), PACK], part, two, *far[1:],
                            scratch=[pltpu.VMEM((12, BX, BY), F32)])
         own, up, down = call(add_cols_kernel, [sds(512, BY), EDGE, EDGE],
                              main, along_cols(packs, 1))
@@ -582,9 +618,7 @@
         else:
             new = call(functools.partial(update_kernel, False), [sds(512, BY)],
                        new, mine, other, weight)
-    r1, r3 = view_swap(new, 2), view_swap(new, 6)
-    a2, b2 = view_swap(r3[:256], 2), view_swap(r1[256:], 6)
-    return call(gather_kernel, [sds(Z, BX, BY)], new, r1, r3, a2, b2)[None]
+    return call(gather_kernel, [sds(Z, BX, BY)], *trade(new, new, new, new))[None]
 
 
 def solution(mesh):

time: 163 us -> 155 us (0.951)
  starting transfers between devices: 46.5 us -> 39.7 us
    ppermute x18 -> x14, waiting for transfers between devices: 60.8 us -> 53.1 us  [view_swap(): return lax.ppermute(x, 'view', [(i, i ^ mask) for i in range(8)])]
    ppermute x18 -> x14, starting transfers between devices: 27.2 us -> 22.8 us  [view_swap(): return lax.ppermute(x, 'view', [(i, i ^ mask) for i in range(8)])]
    ppermute x6, waiting for transfers between devices: 15.5 us -> 18.8 us  [along_cols(): lax.ppermute(x, 'blk', [(i, i // 4 * 4 + (i + by) % 4) for i in range(32)])]
    ppermute x12, waiting for transfers between devices: 22.2 us -> 25.2 us  [along_rows(): return lax.ppermute(x, 'blk', [(i, (i + 4 * by) % 32) for i in range(32)])]
    ppermute x12, starting transfers between devices: 17 us -> 14.5 us  [along_rows(): return lax.ppermute(x, 'blk', [(i, (i + 4 * by) % 32) for i in range(32)])]
    pallas_call x25 -> x29, Pallas kernels: 15.4 us -> 15.6 us  [call(): pl.pallas_call(inner, out_shape=out_shape, in_specs=specs, out_specs=[pl....]
  transfers between devices with their start and end apart: 36 -> 32, of which waited for: 27 -> 26; matrix products, arithmetic and copies ran while one was open for 0% -> 0% of each run, Pallas kernels for 3% -> 4%
where the time goes in v2:
time: 155 us
  waiting for transfers between devices  97 us (63%)
  starting transfers between devices  39.7 us (26%)
  Pallas kernels  15.6 us (10%)
  local copies, waits for them, and re-layouts  2.27 us (1%)
    ppermute x14, waiting for transfers between devices, view_swap(): return lax.ppermute(x, 'view', [(i, i ^ mask) for i in range(8)])  53.1 us
    ppermute x12, waiting for transfers between devices, along_rows(): return lax.ppermute(x, 'blk', [(i, (i + 4 * by) % 32) for i in range(32)])  25.2 us
    ppermute x14, starting transfers between devices, view_swap(): return lax.ppermute(x, 'view', [(i, i ^ mask) for i in range(8)])  22.8 us
    ppermute x6, waiting for transfers between devices, along_cols(): lax.ppermute(x, 'blk', [(i, i // 4 * 4 + (i + by) % 4) for i in range(32)])  18.8 us
    pallas_call x29, Pallas kernels, call(): pl.pallas_call(inner, out_shape=out_shape, in_specs=specs, out_specs=[pl....  15.6 us
    ppermute x12, starting transfers between devices, along_rows(): return lax.ppermute(x, 'blk', [(i, (i + 4 * by) % 32) for i in range(32)])  14.5 us
  transfers between devices with their start and end apart: 32, of which 26 were waited for; matrix products, arithmetic and copies ran while one was open for 0% of the time, Pallas kernels for 4%

profile of v2, /device:TPU:32, one launch (start us, length us, event | category | flops | bytes accessed | tf_op | source)
XLA Modules:
  0.0 154.9 jit_solution(16930862475487770302)
XLA Ops:
  3.8 1.9 %collective-permute-start.1 = (f32[16,32,128]{2,1,0:T(8,128)S(1)}, f32[16,32,128]{2,1,0:T(8,128)S(1)}, u32[]{:S(2)}, u32[]{:S(2)}) collective-permute-start(f32[16,32,128]{2,1,0:T(8,128)S(1)} %get-tuple-element.57), channel_id=1, source_target_pairs={{0,4},{1,5},{2,6},{3,7},{4,8},{5,9},{6,10},{7,11},{8,12},{9,13},{1... | collective-permute-start | bytes 786440 | tf_op jit(solution)/shard_map/ppermute | solution.py:545
  7.2 3.3 %collective-permute-done.refs_2_ = f32[16,64,128]{2,1,0:T(8,128)S(1)} collective-permute-done((f32[16,64,128]{2,1,0:T(8,128)S(1)}, f32[16,64,128]{2,1,0:T(8,128)S(1)}, u32[]{:S(2)}, u32[]{:S(2)}) %collective-permute-start) | collective-permute-done | bytes 524320 | tf_op jit(solution)/shard_map/ppermute | solution.py:549
  14.5 3.3 %collective-permute-start.4 = (f32[32,16,128]{2,1,0:T(8,128)S(1)}, f32[32,16,128]{2,1,0:T(8,128)S(1)}, u32[]{:S(2)}, u32[]{:S(2)}) collective-permute-start(f32[32,16,128]{2,1,0:T(8,128)S(1)} %get-tuple-element.63), channel_id=1, source_target_pairs={{0,4},{1,5},{2,6},{3,7},{4,8},{5,9},{6,10},{7,11},{8,12},{9,13},{1... | collective-permute-start | bytes 786440 | tf_op jit(solution)/shard_map/ppermute | solution.py:545
  18.3 2.7 %collective-permute-start.7 = (f32[16,32,128]{2,1,0:T(8,128)S(1)}, f32[16,32,128]{2,1,0:T(8,128)S(1)}, u32[]{:S(2)}, u32[]{:S(2)}) collective-permute-start(f32[16,32,128]{2,1,0:T(8,128)S(1)} %get-tuple-element.66), channel_id=1, source_target_pairs={{0,4},{1,5},{2,6},{3,7},{4,8},{5,9},{6,10},{7,11},{8,12},{9,13},{1... | collective-permute-start | bytes 786440 | tf_op jit(solution)/shard_map/ppermute | solution.py:545
  21.2 3.3 %collective-permute-done.4.refs_3_ = f32[32,16,128]{2,1,0:T(8,128)S(1)} collective-permute-done((f32[32,16,128]{2,1,0:T(8,128)S(1)}, f32[32,16,128]{2,1,0:T(8,128)S(1)}, u32[]{:S(2)}, u32[]{:S(2)}) %collective-permute-start.4) | collective-permute-done | bytes 262176 | tf_op jit(solution)/shard_map/ppermute | solution.py:545
  24.5 3.0 %collective-permute-done.5.refs_4_ = f32[32,16,128]{2,1,0:T(8,128)S(1)} collective-permute-done((f32[32,16,128]{2,1,0:T(8,128)S(1)}, f32[32,16,128]{2,1,0:T(8,128)S(1)}, u32[]{:S(2)}, u32[]{:S(2)}) %collective-permute-start.5) | collective-permute-done | bytes 262176 | tf_op jit(solution)/shard_map/ppermute | solution.py:545
  29.0 3.2 %collective-permute-done.8.refs_3_ = f32[16,32,128]{2,1,0:T(8,128)S(1)} collective-permute-done((f32[16,32,128]{2,1,0:T(8,128)S(1)}, f32[16,32,128]{2,1,0:T(8,128)S(1)}, u32[]{:S(2)}, u32[]{:S(2)}) %collective-permute-start.8) | collective-permute-done | bytes 262176 | tf_op jit(solution)/shard_map/ppermute | solution.py:545
  35.4 2.1 %collective-permute-start.10 = (f32[520,128]{1,0:T(8,128)S(1)}, f32[520,128]{1,0:T(8,128)S(1)}, u32[]{:S(2)}, u32[]{:S(2)}) collective-permute-start(f32[520,128]{1,0:T(8,128)S(1)} %get-tuple-element.73), channel_id=1, source_target_pairs={{0,192},{32,224},{64,128},{96,160},{128,64},{160,96},{192,0},{224,... | collective-permute-start | bytes 798728 | tf_op jit(solution)/shard_map/ppermute | solution.py:553
  38.1 5.1 %collective-permute-done.9.refs_1_.refs_4_ = f32[520,128]{1,0:T(8,128)S(1)} collective-permute-done((f32[520,128]{1,0:T(8,128)S(1)}, f32[520,128]{1,0:T(8,128)S(1)}, u32[]{:S(2)}, u32[]{:S(2)}) %collective-permute-start.9) | collective-permute-done | bytes 266272 | tf_op jit(solution)/shard_map/ppermute | solution.py:553
  43.3 6.2 %collective-permute-done.10.refs_2_.refs_5_ = f32[520,128]{1,0:T(8,128)S(1)} collective-permute-done((f32[520,128]{1,0:T(8,128)S(1)}, f32[520,128]{1,0:T(8,128)S(1)}, u32[]{:S(2)}, u32[]{:S(2)}) %collective-permute-start.10) | collective-permute-done | bytes 266272 | tf_op jit(solution)/shard_map/ppermute | solution.py:553
  51.8 5.8 %collective-permute-done.12.refs_1_ = f32[4,128,128]{2,1,0:T(8,128)S(1)} collective-permute-done((f32[4,128,128]{2,1,0:T(8,128)S(1)}, f32[4,128,128]{2,1,0:T(8,128)S(1)}, u32[]{:S(2)}, u32[]{:S(2)}) %collective-permute-start.12) | collective-permute-done | bytes 262176 | tf_op jit(solution)/shard_map/ppermute | solution.py:549
  59.8 3.1 %collective-permute-done.13.refs_1_ = f32[8,32,128]{2,1,0:T(8,128)S(1)} collective-permute-done((f32[8,32,128]{2,1,0:T(8,128)S(1)}, f32[8,32,128]{2,1,0:T(8,128)S(1)}, u32[]{:S(2)}, u32[]{:S(2)}) %collective-permute-start.13) | collective-permute-done | bytes 131104 | tf_op jit(solution)/shard_map/ppermute | solution.py:545
  64.2 3.8 %collective-permute-start.15 = (f32[544,128]{1,0:T(8,128)S(1)}, f32[544,128]{1,0:T(8,128)S(1)}, u32[]{:S(2)}, u32[]{:S(2)}) collective-permute-start(f32[544,128]{1,0:T(8,128)S(1)} %shard_map.62.refs_1_), channel_id=1, source_target_pairs={{0,32},{32,0},{64,96},{96,64},{128,160},{160,128},{192,224},{224,1... | collective-permute-start | bytes 835592 | tf_op jit(solution)/shard_map/ppermute | solution.py:553
  68.0 5.0 %collective-permute-done.15.refs_2_ = f32[544,128]{1,0:T(8,128)S(1)} collective-permute-done((f32[544,128]{1,0:T(8,128)S(1)}, f32[544,128]{1,0:T(8,128)S(1)}, u32[]{:S(2)}, u32[]{:S(2)}) %collective-permute-start.15) | collective-permute-done | bytes 278560 | tf_op jit(solution)/shard_map/ppermute | solution.py:553
  73.5 1.9 %collective-permute-start.16 = (f32[8,32,128]{2,1,0:T(8,128)S(1)}, f32[8,32,128]{2,1,0:T(8,128)S(1)}, u32[]{:S(2)}, u32[]{:S(2)}) collective-permute-start(f32[8,32,128]{2,1,0:T(8,128)S(1)} %get-tuple-element.87), channel_id=1, source_target_pairs={{0,4},{1,5},{2,6},{3,7},{4,8},{5,9},{6,10},{7,11},{8,12},{9,13},{1... | collective-permute-start | bytes 393224 | tf_op jit(solution)/shard_map/ppermute | solution.py:545
  75.6 2.9 %collective-permute-done.16.refs_1_ = f32[8,32,128]{2,1,0:T(8,128)S(1)} collective-permute-done((f32[8,32,128]{2,1,0:T(8,128)S(1)}, f32[8,32,128]{2,1,0:T(8,128)S(1)}, u32[]{:S(2)}, u32[]{:S(2)}) %collective-permute-start.16) | collective-permute-done | bytes 131104 | tf_op jit(solution)/shard_map/ppermute | solution.py:545
  80.7 3.9 %collective-permute-done.18.refs_3_ = f32[4,128,128]{2,1,0:T(8,128)S(1)} collective-permute-done((f32[4,128,128]{2,1,0:T(8,128)S(1)}, f32[4,128,128]{2,1,0:T(8,128)S(1)}, u32[]{:S(2)}, u32[]{:S(2)}) %collective-permute-start.18) | collective-permute-done | bytes 262176 | tf_op jit(solution)/shard_map/ppermute | solution.py:549
  85.5 2.2 %collective-permute-start.20 = (f32[512,128]{1,0:T(8,128)S(1)}, f32[512,128]{1,0:T(8,128)S(1)}, u32[]{:S(2)}, u32[]{:S(2)}) collective-permute-start(f32[512,128]{1,0:T(8,128)S(1)} %get-tuple-element.91), channel_id=1, source_target_pairs={{0,192},{32,224},{64,128},{96,160},{128,64},{160,96},{192,0},{224,... | collective-permute-start | bytes 786440 | tf_op jit(solution)/shard_map/ppermute | solution.py:553
  88.5 2.7 %collective-permute-start.21 = (f32[512,128]{1,0:T(8,128)S(1)}, f32[512,128]{1,0:T(8,128)S(1)}, u32[]{:S(2)}, u32[]{:S(2)}) collective-permute-start(f32[512,128]{1,0:T(8,128)S(1)} %get-tuple-element.93), channel_id=1, source_target_pairs={{0,128},{32,160},{64,192},{96,224},{128,0},{160,32},{192,64},{224,... | collective-permute-start | bytes 786440 | tf_op jit(solution)/shard_map/ppermute | solution.py:553
  91.2 4.4 %collective-permute-done.20.refs_1_.refs_2_ = f32[512,128]{1,0:T(8,128)S(1)} collective-permute-done((f32[512,128]{1,0:T(8,128)S(1)}, f32[512,128]{1,0:T(8,128)S(1)}, u32[]{:S(2)}, u32[]{:S(2)}) %collective-permute-start.20) | collective-permute-done | bytes 262176 | tf_op jit(solution)/shard_map/ppermute | solution.py:553
  96.8 6.2 %collective-permute-done.21.refs_3_ = f32[512,128]{1,0:T(8,128)S(1)} collective-permute-done((f32[512,128]{1,0:T(8,128)S(1)}, f32[512,128]{1,0:T(8,128)S(1)}, u32[]{:S(2)}, u32[]{:S(2)}) %collective-permute-start.21) | collective-permute-done | bytes 262176 | tf_op jit(solution)/shard_map/ppermute | solution.py:553
  104.8 2.2 %collective-permute-start.23 = (f32[512,128]{1,0:T(8,128)S(1)}, f32[512,128]{1,0:T(8,128)S(1)}, u32[]{:S(2)}, u32[]{:S(2)}) collective-permute-start(f32[512,128]{1,0:T(8,128)S(1)} %get-tuple-element.97), channel_id=1, source_target_pairs={{0,192},{32,224},{64,128},{96,160},{128,64},{160,96},{192,0},{224,... | collective-permute-start | bytes 786440 | tf_op jit(solution)/shard_map/ppermute | solution.py:553
  106.9 1.9 %collective-permute-start.24 = (f32[512,128]{1,0:T(8,128)S(1)}, f32[512,128]{1,0:T(8,128)S(1)}, u32[]{:S(2)}, u32[]{:S(2)}) collective-permute-start(f32[512,128]{1,0:T(8,128)S(1)} %get-tuple-element.98), channel_id=1, source_target_pairs={{0,128},{32,160},{64,192},{96,224},{128,0},{160,32},{192,64},{224,... | collective-permute-start | bytes 786440 | tf_op jit(solution)/shard_map/ppermute | solution.py:553
  108.8 5.1 %collective-permute-done.22.refs_1_ = f32[512,128]{1,0:T(8,128)S(1)} collective-permute-done((f32[512,128]{1,0:T(8,128)S(1)}, f32[512,128]{1,0:T(8,128)S(1)}, u32[]{:S(2)}, u32[]{:S(2)}) %collective-permute-start.22) | collective-permute-done | bytes 262176 | tf_op jit(solution)/shard_map/ppermute | solution.py:553
  113.9 4.5 %collective-permute-done.23.refs_2_ = f32[512,128]{1,0:T(8,128)S(1)} collective-permute-done((f32[512,128]{1,0:T(8,128)S(1)}, f32[512,128]{1,0:T(8,128)S(1)}, u32[]{:S(2)}, u32[]{:S(2)}) %collective-permute-start.23) | collective-permute-done | bytes 262176 | tf_op jit(solution)/shard_map/ppermute | solution.py:553
  121.0 5.8 %collective-permute-done.25.refs_1_ = f32[4,128,128]{2,1,0:T(8,128)S(1)} collective-permute-done((f32[4,128,128]{2,1,0:T(8,128)S(1)}, f32[4,128,128]{2,1,0:T(8,128)S(1)}, u32[]{:S(2)}, u32[]{:S(2)}) %collective-permute-start.25) | collective-permute-done | bytes 262176 | tf_op jit(solution)/shard_map/ppermute | solution.py:549
  126.9 2.0 %collective-permute-start.26 = (f32[8,32,128]{2,1,0:T(8,128)S(1)}, f32[8,32,128]{2,1,0:T(8,128)S(1)}, u32[]{:S(2)}, u32[]{:S(2)}) collective-permute-start(f32[8,32,128]{2,1,0:T(8,128)S(1)} %get-tuple-element.102), channel_id=1, source_target_pairs={{0,4},{1,5},{2,6},{3,7},{4,8},{5,9},{6,10},{7,11},{8,12},{9,13},{1... | collective-permute-start | bytes 393224 | tf_op jit(solution)/shard_map/ppermute | solution.py:545
  129.0 2.9 %collective-permute-done.26.refs_1_ = f32[8,32,128]{2,1,0:T(8,128)S(1)} collective-permute-done((f32[8,32,128]{2,1,0:T(8,128)S(1)}, f32[8,32,128]{2,1,0:T(8,128)S(1)}, u32[]{:S(2)}, u32[]{:S(2)}) %collective-permute-start.26) | collective-permute-done | bytes 131104 | tf_op jit(solution)/shard_map/ppermute | solution.py:545
  135.6 6.3 %collective-permute-done.28.refs_2_ = f32[512,128]{1,0:T(8,128)S(1)} collective-permute-done((f32[512,128]{1,0:T(8,128)S(1)}, f32[512,128]{1,0:T(8,128)S(1)}, u32[]{:S(2)}, u32[]{:S(2)}) %collective-permute-start.28) | collective-permute-done | bytes 262176 | tf_op jit(solution)/shard_map/ppermute | solution.py:553
  141.9 2.6 %collective-permute-start.31 = (f32[512,128]{1,0:T(8,128)S(1)}, f32[512,128]{1,0:T(8,128)S(1)}, u32[]{:S(2)}, u32[]{:S(2)}) collective-permute-start(f32[512,128]{1,0:T(8,128)S(1)} %shard_map.73.refs_0_), channel_id=1, source_target_pairs={{0,128},{32,160},{64,192},{96,224},{128,0},{160,32},{192,64},{224,... | collective-permute-start | bytes 786440 | tf_op jit(solution)/shard_map/ppermute | solution.py:553
  145.7 5.5 %collective-permute-done.31.refs_3_ = f32[512,128]{1,0:T(8,128)S(1)} collective-permute-done((f32[512,128]{1,0:T(8,128)S(1)}, f32[512,128]{1,0:T(8,128)S(1)}, u32[]{:S(2)}, u32[]{:S(2)}) %collective-permute-start.31) | collective-permute-done | bytes 262176 | tf_op jit(solution)/shard_map/ppermute | solution.py:553
  151.2 2.6 %collective-permute-done.30.refs_2_ = f32[512,128]{1,0:T(8,128)S(1)} collective-permute-done((f32[512,128]{1,0:T(8,128)S(1)}, f32[512,128]{1,0:T(8,128)S(1)}, u32[]{:S(2)}, u32[]{:S(2)}) %collective-permute-start.30) | collective-permute-done | bytes 262176 | tf_op jit(solution)/shard_map/ppermute | solution.py:553
  (72 shorter events, 37.2 us)
Async XLA Ops:
  2.7 7.8 %collective-permute-start = (f32[16,64,128]{2,1,0:T(8,128)S(1)}, f32[16,64,128]{2,1,0:T(8,128)S(1)}, u32[]{:S(2)}, u32[]{:S(2)}) collective-permute-start(f32[16,64,128]{2,1,0:T(8,128)S(1)} %shard_map.48), channel_id=1, source_target_pairs={{0,3},{1,0},{2,1},{3,2},{4,7},{5,4},{6,5},{7,6},{8,11},{9,8},{10,9... | collective-permute-start | bytes 1572872 | tf_op jit(solution)/shard_map/ppermute | solution.py:549
  3.8 7.9 %collective-permute-start.1 = (f32[16,32,128]{2,1,0:T(8,128)S(1)}, f32[16,32,128]{2,1,0:T(8,128)S(1)}, u32[]{:S(2)}, u32[]{:S(2)}) collective-permute-start(f32[16,32,128]{2,1,0:T(8,128)S(1)} %get-tuple-element.57), channel_id=1, source_target_pairs={{0,4},{1,5},{2,6},{3,7},{4,8},{5,9},{6,10},{7,11},{8,12},{9,13},{1... | collective-permute-start | bytes 786440 | tf_op jit(solution)/shard_map/ppermute | solution.py:545
  5.7 7.6 %collective-permute-start.2 = (f32[16,32,128]{2,1,0:T(8,128)S(1)}, f32[16,32,128]{2,1,0:T(8,128)S(1)}, u32[]{:S(2)}, u32[]{:S(2)}) collective-permute-start(f32[16,32,128]{2,1,0:T(8,128)S(1)} %get-tuple-element.55.refs_0_), channel_id=1, source_target_pairs={{0,28},{1,29},{2,30},{3,31},{4,0},{5,1},{6,2},{7,3},{8,4},{9,5},{1... | collective-permute-start | bytes 786440 | tf_op jit(solution)/shard_map/ppermute | solution.py:545
  5.8 11.9 %collective-permute-start.3 = (f32[8,64,128]{2,1,0:T(8,128)S(1)}, f32[8,64,128]{2,1,0:T(8,128)S(1)}, u32[]{:S(2)}, u32[]{:S(2)}) collective-permute-start(f32[8,64,128]{2,1,0:T(8,128)S(1)} %shard_map.46.refs_0_), channel_id=1, source_target_pairs={{0,3},{1,0},{2,1},{3,2},{4,7},{5,4},{6,5},{7,6},{8,11},{9,8},{10,9... | collective-permute-start | bytes 786440 | tf_op jit(solution)/shard_map/ppermute | solution.py:549
  13.7 14.7 %collective-permute-start.6 = (f32[8,64,128]{2,1,0:T(8,128)S(1)}, f32[8,64,128]{2,1,0:T(8,128)S(1)}, u32[]{:S(2)}, u32[]{:S(2)}) collective-permute-start(f32[8,64,128]{2,1,0:T(8,128)S(1)} %get-tuple-element.65), channel_id=1, source_target_pairs={{0,3},{1,0},{2,1},{3,2},{4,7},{5,4},{6,5},{7,6},{8,11},{9,8},{10,9... | collective-permute-start | bytes 786440 | tf_op jit(solution)/shard_map/ppermute | solution.py:549
  14.5 10.0 %collective-permute-start.4 = (f32[32,16,128]{2,1,0:T(8,128)S(1)}, f32[32,16,128]{2,1,0:T(8,128)S(1)}, u32[]{:S(2)}, u32[]{:S(2)}) collective-permute-start(f32[32,16,128]{2,1,0:T(8,128)S(1)} %get-tuple-element.63), channel_id=1, source_target_pairs={{0,4},{1,5},{2,6},{3,7},{4,8},{5,9},{6,10},{7,11},{8,12},{9,13},{1... | collective-permute-start | bytes 786440 | tf_op jit(solution)/shard_map/ppermute | solution.py:545
  17.7 9.8 %collective-permute-start.5 = (f32[32,16,128]{2,1,0:T(8,128)S(1)}, f32[32,16,128]{2,1,0:T(8,128)S(1)}, u32[]{:S(2)}, u32[]{:S(2)}) collective-permute-start(f32[32,16,128]{2,1,0:T(8,128)S(1)} %get-tuple-element.64), channel_id=1, source_target_pairs={{0,28},{1,29},{2,30},{3,31},{4,0},{5,1},{6,2},{7,3},{8,4},{9,5},{1... | collective-permute-start | bytes 786440 | tf_op jit(solution)/shard_map/ppermute | solution.py:545
  18.3 10.7 %collective-permute-start.7 = (f32[16,32,128]{2,1,0:T(8,128)S(1)}, f32[16,32,128]{2,1,0:T(8,128)S(1)}, u32[]{:S(2)}, u32[]{:S(2)}) collective-permute-start(f32[16,32,128]{2,1,0:T(8,128)S(1)} %get-tuple-element.66), channel_id=1, source_target_pairs={{0,4},{1,5},{2,6},{3,7},{4,8},{5,9},{6,10},{7,11},{8,12},{9,13},{1... | collective-permute-start | bytes 786440 | tf_op jit(solution)/shard_map/ppermute | solution.py:545
  21.0 11.1 %collective-permute-start.8 = (f32[16,32,128]{2,1,0:T(8,128)S(1)}, f32[16,32,128]{2,1,0:T(8,128)S(1)}, u32[]{:S(2)}, u32[]{:S(2)}) collective-permute-start(f32[16,32,128]{2,1,0:T(8,128)S(1)} %get-tuple-element.67), channel_id=1, source_target_pairs={{0,28},{1,29},{2,30},{3,31},{4,0},{5,1},{6,2},{7,3},{8,4},{9,5},{1... | collective-permute-start | bytes 786440 | tf_op jit(solution)/shard_map/ppermute | solution.py:545
  33.8 9.4 %collective-permute-start.9 = (f32[520,128]{1,0:T(8,128)S(1)}, f32[520,128]{1,0:T(8,128)S(1)}, u32[]{:S(2)}, u32[]{:S(2)}) collective-permute-start(f32[520,128]{1,0:T(8,128)S(1)} %get-tuple-element.72), channel_id=1, source_target_pairs={{0,64},{32,96},{64,0},{96,32},{128,192},{160,224},{192,128},{224,1... | collective-permute-start | bytes 798728 | tf_op jit(solution)/shard_map/ppermute | solution.py:553
  35.4 14.1 %collective-permute-start.10 = (f32[520,128]{1,0:T(8,128)S(1)}, f32[520,128]{1,0:T(8,128)S(1)}, u32[]{:S(2)}, u32[]{:S(2)}) collective-permute-start(f32[520,128]{1,0:T(8,128)S(1)} %get-tuple-element.73), channel_id=1, source_target_pairs={{0,192},{32,224},{64,128},{96,160},{128,64},{160,96},{192,0},{224,... | collective-permute-start | bytes 798728 | tf_op jit(solution)/shard_map/ppermute | solution.py:553
  37.5 12.5 %collective-permute-start.11 = (f32[520,128]{1,0:T(8,128)S(1)}, f32[520,128]{1,0:T(8,128)S(1)}, u32[]{:S(2)}, u32[]{:S(2)}) collective-permute-start(f32[520,128]{1,0:T(8,128)S(1)} %get-tuple-element.76), channel_id=1, source_target_pairs={{0,128},{32,160},{64,192},{96,224},{128,0},{160,32},{192,64},{224,... | collective-permute-start | bytes 798728 | tf_op jit(solution)/shard_map/ppermute | solution.py:553
  51.7 5.9 %collective-permute-start.12 = (f32[4,128,128]{2,1,0:T(8,128)S(1)}, f32[4,128,128]{2,1,0:T(8,128)S(1)}, u32[]{:S(2)}, u32[]{:S(2)}) collective-permute-start(f32[4,128,128]{2,1,0:T(8,128)S(1)} %get-tuple-element.82), channel_id=1, source_target_pairs={{0,1},{1,2},{2,3},{3,0},{4,5},{5,6},{6,7},{7,4},{8,9},{9,10},{10,1... | collective-permute-start | bytes 786440 | tf_op jit(solution)/shard_map/ppermute | solution.py:549
  57.7 5.2 %collective-permute-start.13 = (f32[8,32,128]{2,1,0:T(8,128)S(1)}, f32[8,32,128]{2,1,0:T(8,128)S(1)}, u32[]{:S(2)}, u32[]{:S(2)}) collective-permute-start(f32[8,32,128]{2,1,0:T(8,128)S(1)} %get-tuple-element.84), channel_id=1, source_target_pairs={{0,4},{1,5},{2,6},{3,7},{4,8},{5,9},{6,10},{7,11},{8,12},{9,13},{1... | collective-permute-start | bytes 393224 | tf_op jit(solution)/shard_map/ppermute | solution.py:545
  59.2 5.0 %collective-permute-start.14 = (f32[8,32,128]{2,1,0:T(8,128)S(1)}, f32[8,32,128]{2,1,0:T(8,128)S(1)}, u32[]{:S(2)}, u32[]{:S(2)}) collective-permute-start(f32[8,32,128]{2,1,0:T(8,128)S(1)} %get-tuple-element.85), channel_id=1, source_target_pairs={{0,28},{1,29},{2,30},{3,31},{4,0},{5,1},{6,2},{7,3},{8,4},{9,5},{1... | collective-permute-start | bytes 393224 | tf_op jit(solution)/shard_map/ppermute | solution.py:545
  64.2 8.8 %collective-permute-start.15 = (f32[544,128]{1,0:T(8,128)S(1)}, f32[544,128]{1,0:T(8,128)S(1)}, u32[]{:S(2)}, u32[]{:S(2)}) collective-permute-start(f32[544,128]{1,0:T(8,128)S(1)} %shard_map.62.refs_1_), channel_id=1, source_target_pairs={{0,32},{32,0},{64,96},{96,64},{128,160},{160,128},{192,224},{224,1... | collective-permute-start | bytes 835592 | tf_op jit(solution)/shard_map/ppermute | solution.py:553
  73.5 5.0 %collective-permute-start.16 = (f32[8,32,128]{2,1,0:T(8,128)S(1)}, f32[8,32,128]{2,1,0:T(8,128)S(1)}, u32[]{:S(2)}, u32[]{:S(2)}) collective-permute-start(f32[8,32,128]{2,1,0:T(8,128)S(1)} %get-tuple-element.87), channel_id=1, source_target_pairs={{0,4},{1,5},{2,6},{3,7},{4,8},{5,9},{6,10},{7,11},{8,12},{9,13},{1... | collective-permute-start | bytes 393224 | tf_op jit(solution)/shard_map/ppermute | solution.py:545
  75.5 5.0 %collective-permute-start.17 = (f32[8,32,128]{2,1,0:T(8,128)S(1)}, f32[8,32,128]{2,1,0:T(8,128)S(1)}, u32[]{:S(2)}, u32[]{:S(2)}) collective-permute-start(f32[8,32,128]{2,1,0:T(8,128)S(1)} %get-tuple-element.88), channel_id=1, source_target_pairs={{0,28},{1,29},{2,30},{3,31},{4,0},{5,1},{6,2},{7,3},{8,4},{9,5},{1... | collective-permute-start | bytes 393224 | tf_op jit(solution)/shard_map/ppermute | solution.py:545
  80.6 4.0 %collective-permute-start.18 = (f32[4,128,128]{2,1,0:T(8,128)S(1)}, f32[4,128,128]{2,1,0:T(8,128)S(1)}, u32[]{:S(2)}, u32[]{:S(2)}) collective-permute-start(f32[4,128,128]{2,1,0:T(8,128)S(1)} %shard_map.64), channel_id=1, source_target_pairs={{0,3},{1,0},{2,1},{3,2},{4,7},{5,4},{6,5},{7,6},{8,11},{9,8},{10,9... | collective-permute-start | bytes 786440 | tf_op jit(solution)/shard_map/ppermute | solution.py:549
  85.5 10.2 %collective-permute-start.20 = (f32[512,128]{1,0:T(8,128)S(1)}, f32[512,128]{1,0:T(8,128)S(1)}, u32[]{:S(2)}, u32[]{:S(2)}) collective-permute-start(f32[512,128]{1,0:T(8,128)S(1)} %get-tuple-element.91), channel_id=1, source_target_pairs={{0,192},{32,224},{64,128},{96,160},{128,64},{160,96},{192,0},{224,... | collective-permute-start | bytes 786440 | tf_op jit(solution)/shard_map/ppermute | solution.py:553
  87.6 9.1 %collective-permute-start.19 = (f32[512,128]{1,0:T(8,128)S(1)}, f32[512,128]{1,0:T(8,128)S(1)}, u32[]{:S(2)}, u32[]{:S(2)}) collective-permute-start(f32[512,128]{1,0:T(8,128)S(1)} %get-tuple-element.90.refs_10_), channel_id=1, source_target_pairs={{0,64},{32,96},{64,0},{96,32},{128,192},{160,224},{192,128},{224,1... | collective-permute-start | bytes 786440 | tf_op jit(solution)/shard_map/ppermute | solution.py:553
  88.5 14.4 %collective-permute-start.21 = (f32[512,128]{1,0:T(8,128)S(1)}, f32[512,128]{1,0:T(8,128)S(1)}, u32[]{:S(2)}, u32[]{:S(2)}) collective-permute-start(f32[512,128]{1,0:T(8,128)S(1)} %get-tuple-element.93), channel_id=1, source_target_pairs={{0,128},{32,160},{64,192},{96,224},{128,0},{160,32},{192,64},{224,... | collective-permute-start | bytes 786440 | tf_op jit(solution)/shard_map/ppermute | solution.py:553
  104.4 9.5 %collective-permute-start.22 = (f32[512,128]{1,0:T(8,128)S(1)}, f32[512,128]{1,0:T(8,128)S(1)}, u32[]{:S(2)}, u32[]{:S(2)}) collective-permute-start(f32[512,128]{1,0:T(8,128)S(1)} %get-tuple-element.96), channel_id=1, source_target_pairs={{0,64},{32,96},{64,0},{96,32},{128,192},{160,224},{192,128},{224,1... | collective-permute-start | bytes 786440 | tf_op jit(solution)/shard_map/ppermute | solution.py:553
  104.8 13.7 %collective-permute-start.23 = (f32[512,128]{1,0:T(8,128)S(1)}, f32[512,128]{1,0:T(8,128)S(1)}, u32[]{:S(2)}, u32[]{:S(2)}) collective-permute-start(f32[512,128]{1,0:T(8,128)S(1)} %get-tuple-element.97), channel_id=1, source_target_pairs={{0,192},{32,224},{64,128},{96,160},{128,64},{160,96},{192,0},{224,... | collective-permute-start | bytes 786440 | tf_op jit(solution)/shard_map/ppermute | solution.py:553
  106.9 13.3 %collective-permute-start.24 = (f32[512,128]{1,0:T(8,128)S(1)}, f32[512,128]{1,0:T(8,128)S(1)}, u32[]{:S(2)}, u32[]{:S(2)}) collective-permute-start(f32[512,128]{1,0:T(8,128)S(1)} %get-tuple-element.98), channel_id=1, source_target_pairs={{0,128},{32,160},{64,192},{96,224},{128,0},{160,32},{192,64},{224,... | collective-permute-start | bytes 786440 | tf_op jit(solution)/shard_map/ppermute | solution.py:553
  120.9 5.9 %collective-permute-start.25 = (f32[4,128,128]{2,1,0:T(8,128)S(1)}, f32[4,128,128]{2,1,0:T(8,128)S(1)}, u32[]{:S(2)}, u32[]{:S(2)}) collective-permute-start(f32[4,128,128]{2,1,0:T(8,128)S(1)} %get-tuple-element.100), channel_id=1, source_target_pairs={{0,1},{1,2},{2,3},{3,0},{4,5},{5,6},{6,7},{7,4},{8,9},{9,10},{10,1... | collective-permute-start | bytes 786440 | tf_op jit(solution)/shard_map/ppermute | solution.py:549
  126.9 5.0 %collective-permute-start.26 = (f32[8,32,128]{2,1,0:T(8,128)S(1)}, f32[8,32,128]{2,1,0:T(8,128)S(1)}, u32[]{:S(2)}, u32[]{:S(2)}) collective-permute-start(f32[8,32,128]{2,1,0:T(8,128)S(1)} %get-tuple-element.102), channel_id=1, source_target_pairs={{0,4},{1,5},{2,6},{3,7},{4,8},{5,9},{6,10},{7,11},{8,12},{9,13},{1... | collective-permute-start | bytes 393224 | tf_op jit(solution)/shard_map/ppermute | solution.py:545
  128.9 5.0 %collective-permute-start.27 = (f32[8,32,128]{2,1,0:T(8,128)S(1)}, f32[8,32,128]{2,1,0:T(8,128)S(1)}, u32[]{:S(2)}, u32[]{:S(2)}) collective-permute-start(f32[8,32,128]{2,1,0:T(8,128)S(1)} %get-tuple-element.103), channel_id=1, source_target_pairs={{0,28},{1,29},{2,30},{3,31},{4,0},{5,1},{6,2},{7,3},{8,4},{9,5},{1... | collective-permute-start | bytes 393224 | tf_op jit(solution)/shard_map/ppermute | solution.py:545
  133.9 8.0 %collective-permute-start.28 = (f32[512,128]{1,0:T(8,128)S(1)}, f32[512,128]{1,0:T(8,128)S(1)}, u32[]{:S(2)}, u32[]{:S(2)}) collective-permute-start(f32[512,128]{1,0:T(8,128)S(1)} %shard_map.72.refs_1_), channel_id=1, source_target_pairs={{0,32},{32,0},{64,96},{96,64},{128,160},{160,128},{192,224},{224,1... | collective-permute-start | bytes 786440 | tf_op jit(solution)/shard_map/ppermute | solution.py:553
  141.9 9.3 %collective-permute-start.31 = (f32[512,128]{1,0:T(8,128)S(1)}, f32[512,128]{1,0:T(8,128)S(1)}, u32[]{:S(2)}, u32[]{:S(2)}) collective-permute-start(f32[512,128]{1,0:T(8,128)S(1)} %shard_map.73.refs_0_), channel_id=1, source_target_pairs={{0,128},{32,160},{64,192},{96,224},{128,0},{160,32},{192,64},{224,... | collective-permute-start | bytes 786440 | tf_op jit(solution)/shard_map/ppermute | solution.py:553
  144.5 9.3 %collective-permute-start.30 = (f32[512,128]{1,0:T(8,128)S(1)}, f32[512,128]{1,0:T(8,128)S(1)}, u32[]{:S(2)}, u32[]{:S(2)}) collective-permute-start(f32[512,128]{1,0:T(8,128)S(1)} %shard_map.73.refs_0_), channel_id=1, source_target_pairs={{0,192},{32,224},{64,128},{96,160},{128,64},{160,96},{192,0},{224,... | collective-permute-start | bytes 786440 | tf_op jit(solution)/shard_map/ppermute | solution.py:553
  145.7 8.2 %collective-permute-start.29 = (f32[512,128]{1,0:T(8,128)S(1)}, f32[512,128]{1,0:T(8,128)S(1)}, u32[]{:S(2)}, u32[]{:S(2)}) collective-permute-start(f32[512,128]{1,0:T(8,128)S(1)} %shard_map.73.refs_0_), channel_id=1, source_target_pairs={{0,64},{32,96},{64,0},{96,32},{128,192},{160,224},{192,128},{224,1... | collective-permute-start | bytes 786440 | tf_op jit(solution)/shard_map/ppermute | solution.py:553
  (5 other events, 22.4 us)

commit v3 on v2

--- a/solution.py
+++ b/solution.py
@@ -15,7 +15,6 @@
 GRID = 512
 F32, BF16 = jnp.float32, jnp.bfloat16
 PROF = 8
-ORDER = (0, 1, 3, 2)
 
 
 def split(x):
@@ -62,6 +61,11 @@
 
 def even_column():
     return lax.axis_index("blk") % 2 == 0
+
+
+def partners():
+    core = lax.axis_index("blk") % 2
+    return 0, 1 + 2 * core, 3 - 2 * core, 2
 
 
 def lanes(shape):
@@ -346,7 +350,7 @@
         for i, c in enumerate(cut):
             out[:, c, :] = back[:, i * BY : (i + 1) * BY].reshape(Z, 8, BY)
     x = lax.axis_index("view") // 2
-    for j, send in zip(ORDER, sends):
+    for j, send in zip(partners(), sends):
         send[:512] = out[pl.ds(8 * (x ^ j), 8)].reshape(512, BY)
 
 
@@ -369,7 +373,7 @@
 
 def ratio_kernel(g1, g3, g2, g0, kf, kb, obs, s0, s1, s3, s2, tmp, out):
     x = lax.axis_index("view") // 2
-    for j, got in zip(ORDER, (g0, g1, g3, g2)):
+    for j, got in zip(partners(), (g0, g1, g3, g2)):
         tmp[pl.ds(8 * (x ^ j), 8)] = got[...].reshape(8, BX, BY)
     ratio_core(lambda c: tmp[:, c, :].reshape(256, BY), kf, kb, obs, out, (s0, s1, s3, s2))
 
@@ -516,7 +520,7 @@
 
 def gather_kernel(own, one, three, two, f):
     x = lax.axis_index("view") // 2
-    for j, ref in zip(ORDER, (own, one, three, two)):
+    for j, ref in zip(partners(), (own, one, three, two)):
         f[pl.ds(8 * (x ^ j), 8)] = ref[...].reshape(8, BX, BY)
 
 
@@ -557,8 +561,13 @@
     return along_rows(bottom, 1), along_rows(top, -1)
 
 
-def trade(*parts):
-    return [p if j == 0 else view_swap(p, 2 * j) for j, p in zip(ORDER, parts)]
+def trade(own, one, three, two):
+    def swap(x, even, odd):
+        pairs = [(v * 32 + b, (v ^ (2 * (odd if b % 2 else even))) * 32 + b)
+                 for v in range(8) for b in range(32)]
+        return lax.ppermute(x, ("view", "blk"), pairs)
+
+    return own, swap(one, 1, 3), swap(three, 3, 1), swap(two, 2, 2)
 
 
 def local(estimate, observed, kernels, offsets):

time: 155 us -> 153 us (0.987)
  waiting for transfers between devices: 97 us -> 94.1 us
    ppermute x14 -> x2, waiting for transfers between devices: 53.1 us -> 10.8 us  [view_swap(): return lax.ppermute(x, 'view', [(i, i ^ mask) for i in range(8)])]
    ppermute x0 -> x12, waiting for transfers between devices: none -> 39.7 us  [swap(): return lax.ppermute(x, ('view', 'blk'), pairs)]
    ppermute x0 -> x12, starting transfers between devices: none -> 17.2 us  [swap(): return lax.ppermute(x, ('view', 'blk'), pairs)]
    ppermute x14 -> x2, starting transfers between devices: 22.8 us -> 5.9 us  [view_swap(): return lax.ppermute(x, 'view', [(i, i ^ mask) for i in range(8)])]
where the time goes in v3:
time: 153 us
  waiting for transfers between devices  94.1 us (62%)
  starting transfers between devices  40.6 us (27%)
  Pallas kernels  15.6 us (10%)
  local copies, waits for them, and re-layouts  2.27 us (1%)
    ppermute x12, waiting for transfers between devices, swap(): return lax.ppermute(x, ('view', 'blk'), pairs)  39.7 us
    ppermute x12, waiting for transfers between devices, along_rows(): return lax.ppermute(x, 'blk', [(i, (i + 4 * by) % 32) for i in range(32)])  24.9 us
    ppermute x6, waiting for transfers between devices, along_cols(): lax.ppermute(x, 'blk', [(i, i // 4 * 4 + (i + by) % 4) for i in range(32)])  18.8 us
    ppermute x12, starting transfers between devices, swap(): return lax.ppermute(x, ('view', 'blk'), pairs)  17.2 us
    pallas_call x29, Pallas kernels, call(): pl.pallas_call(inner, out_shape=out_shape, in_specs=specs, out_specs=[pl....  15.6 us
    ppermute x12, starting transfers between devices, along_rows(): return lax.ppermute(x, 'blk', [(i, (i + 4 * by) % 32) for i in range(32)])  15.1 us
    ppermute x2, waiting for transfers between devices, view_swap(): return lax.ppermute(x, 'view', [(i, i ^ mask) for i in range(8)])  10.8 us
    ppermute x2, starting transfers between devices, view_swap(): return lax.ppermute(x, 'view', [(i, i ^ mask) for i in range(8)])  5.9 us
  transfers between devices with their start and end apart: 32, of which 26 were waited for; matrix products, arithmetic and copies ran while one was open for 0% of the time, Pallas kernels for 4%

profile of v3, /device:TPU:32, one launch (start us, length us, event | category | flops | bytes accessed | tf_op | source)
XLA Modules:
  0.0 152.9 jit_solution(6001942280196576467)
XLA Ops:
  3.8 1.9 %collective-permute-start.1 = (f32[16,32,128]{2,1,0:T(8,128)S(1)}, f32[16,32,128]{2,1,0:T(8,128)S(1)}, u32[]{:S(2)}, u32[]{:S(2)}) collective-permute-start(f32[16,32,128]{2,1,0:T(8,128)S(1)} %get-tuple-element.57), channel_id=1, source_target_pairs={{0,4},{1,5},{2,6},{3,7},{4,8},{5,9},{6,10},{7,11},{8,12},{9,13},{1... | collective-permute-start | bytes 786440 | tf_op jit(solution)/shard_map/ppermute | solution.py:549
  7.2 3.3 %collective-permute-done.refs_2_ = f32[16,64,128]{2,1,0:T(8,128)S(1)} collective-permute-done((f32[16,64,128]{2,1,0:T(8,128)S(1)}, f32[16,64,128]{2,1,0:T(8,128)S(1)}, u32[]{:S(2)}, u32[]{:S(2)}) %collective-permute-start) | collective-permute-done | bytes 524320 | tf_op jit(solution)/shard_map/ppermute | solution.py:553
  11.6 1.7 %collective-permute-done.2.refs_3_ = f32[16,32,128]{2,1,0:T(8,128)S(1)} collective-permute-done((f32[16,32,128]{2,1,0:T(8,128)S(1)}, f32[16,32,128]{2,1,0:T(8,128)S(1)}, u32[]{:S(2)}, u32[]{:S(2)}) %collective-permute-start.2) | collective-permute-done | bytes 262176 | tf_op jit(solution)/shard_map/ppermute | solution.py:549
  14.5 3.3 %collective-permute-start.4 = (f32[32,16,128]{2,1,0:T(8,128)S(1)}, f32[32,16,128]{2,1,0:T(8,128)S(1)}, u32[]{:S(2)}, u32[]{:S(2)}) collective-permute-start(f32[32,16,128]{2,1,0:T(8,128)S(1)} %get-tuple-element.63), channel_id=1, source_target_pairs={{0,4},{1,5},{2,6},{3,7},{4,8},{5,9},{6,10},{7,11},{8,12},{9,13},{1... | collective-permute-start | bytes 786440 | tf_op jit(solution)/shard_map/ppermute | solution.py:549
  18.3 2.7 %collective-permute-start.7 = (f32[16,32,128]{2,1,0:T(8,128)S(1)}, f32[16,32,128]{2,1,0:T(8,128)S(1)}, u32[]{:S(2)}, u32[]{:S(2)}) collective-permute-start(f32[16,32,128]{2,1,0:T(8,128)S(1)} %get-tuple-element.66), channel_id=1, source_target_pairs={{0,4},{1,5},{2,6},{3,7},{4,8},{5,9},{6,10},{7,11},{8,12},{9,13},{1... | collective-permute-start | bytes 786440 | tf_op jit(solution)/shard_map/ppermute | solution.py:549
  21.2 3.3 %collective-permute-done.4.refs_3_ = f32[32,16,128]{2,1,0:T(8,128)S(1)} collective-permute-done((f32[32,16,128]{2,1,0:T(8,128)S(1)}, f32[32,16,128]{2,1,0:T(8,128)S(1)}, u32[]{:S(2)}, u32[]{:S(2)}) %collective-permute-start.4) | collective-permute-done | bytes 262176 | tf_op jit(solution)/shard_map/ppermute | solution.py:549
  24.5 3.0 %collective-permute-done.5.refs_4_ = f32[32,16,128]{2,1,0:T(8,128)S(1)} collective-permute-done((f32[32,16,128]{2,1,0:T(8,128)S(1)}, f32[32,16,128]{2,1,0:T(8,128)S(1)}, u32[]{:S(2)}, u32[]{:S(2)}) %collective-permute-start.5) | collective-permute-done | bytes 262176 | tf_op jit(solution)/shard_map/ppermute | solution.py:549
  29.0 3.2 %collective-permute-done.8.refs_3_ = f32[16,32,128]{2,1,0:T(8,128)S(1)} collective-permute-done((f32[16,32,128]{2,1,0:T(8,128)S(1)}, f32[16,32,128]{2,1,0:T(8,128)S(1)}, u32[]{:S(2)}, u32[]{:S(2)}) %collective-permute-start.8) | collective-permute-done | bytes 262176 | tf_op jit(solution)/shard_map/ppermute | solution.py:549
  35.4 2.1 %collective-permute-start.10 = (f32[520,128]{1,0:T(8,128)S(1)}, f32[520,128]{1,0:T(8,128)S(1)}, u32[]{:S(2)}, u32[]{:S(2)}) collective-permute-start(f32[520,128]{1,0:T(8,128)S(1)} %get-tuple-element.73), channel_id=1, source_target_pairs={{0,192},{1,65},{2,194},{3,67},{4,196},{5,69},{6,198},{7,71},{8,200... | collective-permute-start | bytes 798728 | tf_op jit(solution)/shard_map/ppermute | solution.py:568
  38.1 4.4 %collective-permute-done.9.refs_1_.refs_4_ = f32[520,128]{1,0:T(8,128)S(1)} collective-permute-done((f32[520,128]{1,0:T(8,128)S(1)}, f32[520,128]{1,0:T(8,128)S(1)}, u32[]{:S(2)}, u32[]{:S(2)}) %collective-permute-start.9) | collective-permute-done | bytes 266272 | tf_op jit(solution)/shard_map/ppermute | solution.py:568
  44.5 5.0 %collective-permute-done.11.refs_0_.refs_1_.refs_6_ = f32[520,128]{1,0:T(8,128)S(1)} collective-permute-done((f32[520,128]{1,0:T(8,128)S(1)}, f32[520,128]{1,0:T(8,128)S(1)}, u32[]{:S(2)}, u32[]{:S(2)}) %collective-permute-start.11) | collective-permute-done | bytes 266272 | tf_op jit(solution)/shard_map/ppermute | solution.py:568
  51.3 5.8 %collective-permute-done.12.refs_1_ = f32[4,128,128]{2,1,0:T(8,128)S(1)} collective-permute-done((f32[4,128,128]{2,1,0:T(8,128)S(1)}, f32[4,128,128]{2,1,0:T(8,128)S(1)}, u32[]{:S(2)}, u32[]{:S(2)}) %collective-permute-start.12) | collective-permute-done | bytes 262176 | tf_op jit(solution)/shard_map/ppermute | solution.py:553
  59.3 3.1 %collective-permute-done.13.refs_1_ = f32[8,32,128]{2,1,0:T(8,128)S(1)} collective-permute-done((f32[8,32,128]{2,1,0:T(8,128)S(1)}, f32[8,32,128]{2,1,0:T(8,128)S(1)}, u32[]{:S(2)}, u32[]{:S(2)}) %collective-permute-start.13) | collective-permute-done | bytes 131104 | tf_op jit(solution)/shard_map/ppermute | solution.py:549
  63.7 3.8 %collective-permute-start.15 = (f32[544,128]{1,0:T(8,128)S(1)}, f32[544,128]{1,0:T(8,128)S(1)}, u32[]{:S(2)}, u32[]{:S(2)}) collective-permute-start(f32[544,128]{1,0:T(8,128)S(1)} %shard_map.62.refs_1_), channel_id=1, source_target_pairs={{0,32},{32,0},{64,96},{96,64},{128,160},{160,128},{192,224},{224,1... | collective-permute-start | bytes 835592 | tf_op jit(solution)/shard_map/ppermute | solution.py:557
  67.5 5.0 %collective-permute-done.15.refs_2_ = f32[544,128]{1,0:T(8,128)S(1)} collective-permute-done((f32[544,128]{1,0:T(8,128)S(1)}, f32[544,128]{1,0:T(8,128)S(1)}, u32[]{:S(2)}, u32[]{:S(2)}) %collective-permute-start.15) | collective-permute-done | bytes 278560 | tf_op jit(solution)/shard_map/ppermute | solution.py:557
  75.1 2.9 %collective-permute-done.16.refs_1_ = f32[8,32,128]{2,1,0:T(8,128)S(1)} collective-permute-done((f32[8,32,128]{2,1,0:T(8,128)S(1)}, f32[8,32,128]{2,1,0:T(8,128)S(1)}, u32[]{:S(2)}, u32[]{:S(2)}) %collective-permute-start.16) | collective-permute-done | bytes 131104 | tf_op jit(solution)/shard_map/ppermute | solution.py:549
  79.7 3.9 %collective-permute-done.18.refs_3_ = f32[4,128,128]{2,1,0:T(8,128)S(1)} collective-permute-done((f32[4,128,128]{2,1,0:T(8,128)S(1)}, f32[4,128,128]{2,1,0:T(8,128)S(1)}, u32[]{:S(2)}, u32[]{:S(2)}) %collective-permute-start.18) | collective-permute-done | bytes 262176 | tf_op jit(solution)/shard_map/ppermute | solution.py:553
  84.5 1.6 %collective-permute-start.20 = (f32[512,128]{1,0:T(8,128)S(1)}, f32[512,128]{1,0:T(8,128)S(1)}, u32[]{:S(2)}, u32[]{:S(2)}) collective-permute-start(f32[512,128]{1,0:T(8,128)S(1)} %get-tuple-element.91), channel_id=1, source_target_pairs={{0,192},{1,65},{2,194},{3,67},{4,196},{5,69},{6,198},{7,71},{8,200... | collective-permute-start | bytes 786440 | tf_op jit(solution)/shard_map/ppermute | solution.py:568
  87.4 2.8 %collective-permute-start.21 = (f32[512,128]{1,0:T(8,128)S(1)}, f32[512,128]{1,0:T(8,128)S(1)}, u32[]{:S(2)}, u32[]{:S(2)}) collective-permute-start(f32[512,128]{1,0:T(8,128)S(1)} %get-tuple-element.93), channel_id=1, source_target_pairs={{0,128},{1,129},{2,130},{3,131},{4,132},{5,133},{6,134},{7,135},{8... | collective-permute-start | bytes 786440 | tf_op jit(solution)/shard_map/ppermute | solution.py:568
  90.3 4.0 %collective-permute-done.20.refs_1_.refs_2_ = f32[512,128]{1,0:T(8,128)S(1)} collective-permute-done((f32[512,128]{1,0:T(8,128)S(1)}, f32[512,128]{1,0:T(8,128)S(1)}, u32[]{:S(2)}, u32[]{:S(2)}) %collective-permute-start.20) | collective-permute-done | bytes 262176 | tf_op jit(solution)/shard_map/ppermute | solution.py:568
  95.3 5.6 %collective-permute-done.21.refs_3_ = f32[512,128]{1,0:T(8,128)S(1)} collective-permute-done((f32[512,128]{1,0:T(8,128)S(1)}, f32[512,128]{1,0:T(8,128)S(1)}, u32[]{:S(2)}, u32[]{:S(2)}) %collective-permute-start.21) | collective-permute-done | bytes 262176 | tf_op jit(solution)/shard_map/ppermute | solution.py:568
  104.7 2.1 %collective-permute-start.24 = (f32[512,128]{1,0:T(8,128)S(1)}, f32[512,128]{1,0:T(8,128)S(1)}, u32[]{:S(2)}, u32[]{:S(2)}) collective-permute-start(f32[512,128]{1,0:T(8,128)S(1)} %get-tuple-element.98), channel_id=1, source_target_pairs={{0,128},{1,129},{2,130},{3,131},{4,132},{5,133},{6,134},{7,135},{8... | collective-permute-start | bytes 786440 | tf_op jit(solution)/shard_map/ppermute | solution.py:568
  106.8 5.0 %collective-permute-done.22.refs_1_ = f32[512,128]{1,0:T(8,128)S(1)} collective-permute-done((f32[512,128]{1,0:T(8,128)S(1)}, f32[512,128]{1,0:T(8,128)S(1)}, u32[]{:S(2)}, u32[]{:S(2)}) %collective-permute-start.22) | collective-permute-done | bytes 262176 | tf_op jit(solution)/shard_map/ppermute | solution.py:568
  112.6 5.2 %collective-permute-done.24.refs_1_ = f32[512,128]{1,0:T(8,128)S(1)} collective-permute-done((f32[512,128]{1,0:T(8,128)S(1)}, f32[512,128]{1,0:T(8,128)S(1)}, u32[]{:S(2)}, u32[]{:S(2)}) %collective-permute-start.24) | collective-permute-done | bytes 262176 | tf_op jit(solution)/shard_map/ppermute | solution.py:568
  118.6 5.8 %collective-permute-done.25.refs_1_ = f32[4,128,128]{2,1,0:T(8,128)S(1)} collective-permute-done((f32[4,128,128]{2,1,0:T(8,128)S(1)}, f32[4,128,128]{2,1,0:T(8,128)S(1)}, u32[]{:S(2)}, u32[]{:S(2)}) %collective-permute-start.25) | collective-permute-done | bytes 262176 | tf_op jit(solution)/shard_map/ppermute | solution.py:553
  124.5 2.7 %collective-permute-start.26 = (f32[8,32,128]{2,1,0:T(8,128)S(1)}, f32[8,32,128]{2,1,0:T(8,128)S(1)}, u32[]{:S(2)}, u32[]{:S(2)}) collective-permute-start(f32[8,32,128]{2,1,0:T(8,128)S(1)} %get-tuple-element.102), channel_id=1, source_target_pairs={{0,4},{1,5},{2,6},{3,7},{4,8},{5,9},{6,10},{7,11},{8,12},{9,13},{1... | collective-permute-start | bytes 393224 | tf_op jit(solution)/shard_map/ppermute | solution.py:549
  127.2 2.5 %collective-permute-done.26.refs_1_ = f32[8,32,128]{2,1,0:T(8,128)S(1)} collective-permute-done((f32[8,32,128]{2,1,0:T(8,128)S(1)}, f32[8,32,128]{2,1,0:T(8,128)S(1)}, u32[]{:S(2)}, u32[]{:S(2)}) %collective-permute-start.26) | collective-permute-done | bytes 131104 | tf_op jit(solution)/shard_map/ppermute | solution.py:549
  129.8 2.4 %collective-permute-done.27.refs_2_ = f32[8,32,128]{2,1,0:T(8,128)S(1)} collective-permute-done((f32[8,32,128]{2,1,0:T(8,128)S(1)}, f32[8,32,128]{2,1,0:T(8,128)S(1)}, u32[]{:S(2)}, u32[]{:S(2)}) %collective-permute-start.27) | collective-permute-done | bytes 131104 | tf_op jit(solution)/shard_map/ppermute | solution.py:549
  132.2 2.1 %collective-permute-start.28 = (f32[512,128]{1,0:T(8,128)S(1)}, f32[512,128]{1,0:T(8,128)S(1)}, u32[]{:S(2)}, u32[]{:S(2)}) collective-permute-start(f32[512,128]{1,0:T(8,128)S(1)} %shard_map.72.refs_1_), channel_id=1, source_target_pairs={{0,32},{32,0},{64,96},{96,64},{128,160},{160,128},{192,224},{224,1... | collective-permute-start | bytes 786440 | tf_op jit(solution)/shard_map/ppermute | solution.py:557
  134.3 5.9 %collective-permute-done.28.refs_2_ = f32[512,128]{1,0:T(8,128)S(1)} collective-permute-done((f32[512,128]{1,0:T(8,128)S(1)}, f32[512,128]{1,0:T(8,128)S(1)}, u32[]{:S(2)}, u32[]{:S(2)}) %collective-permute-start.28) | collective-permute-done | bytes 262176 | tf_op jit(solution)/shard_map/ppermute | solution.py:557
  143.8 5.3 %collective-permute-done.31.refs_3_ = f32[512,128]{1,0:T(8,128)S(1)} collective-permute-done((f32[512,128]{1,0:T(8,128)S(1)}, f32[512,128]{1,0:T(8,128)S(1)}, u32[]{:S(2)}, u32[]{:S(2)}) %collective-permute-start.31) | collective-permute-done | bytes 262176 | tf_op jit(solution)/shard_map/ppermute | solution.py:568
  149.1 2.7 %collective-permute-done.30.refs_2_ = f32[512,128]{1,0:T(8,128)S(1)} collective-permute-done((f32[512,128]{1,0:T(8,128)S(1)}, f32[512,128]{1,0:T(8,128)S(1)}, u32[]{:S(2)}, u32[]{:S(2)}) %collective-permute-start.30) | collective-permute-done | bytes 262176 | tf_op jit(solution)/shard_map/ppermute | solution.py:568
  (72 shorter events, 38.5 us)
Async XLA Ops:
  2.7 7.8 %collective-permute-start = (f32[16,64,128]{2,1,0:T(8,128)S(1)}, f32[16,64,128]{2,1,0:T(8,128)S(1)}, u32[]{:S(2)}, u32[]{:S(2)}) collective-permute-start(f32[16,64,128]{2,1,0:T(8,128)S(1)} %shard_map.48), channel_id=1, source_target_pairs={{0,3},{1,0},{2,1},{3,2},{4,7},{5,4},{6,5},{7,6},{8,11},{9,8},{10,9... | collective-permute-start | bytes 1572872 | tf_op jit(solution)/shard_map/ppermute | solution.py:553
  3.8 7.9 %collective-permute-start.1 = (f32[16,32,128]{2,1,0:T(8,128)S(1)}, f32[16,32,128]{2,1,0:T(8,128)S(1)}, u32[]{:S(2)}, u32[]{:S(2)}) collective-permute-start(f32[16,32,128]{2,1,0:T(8,128)S(1)} %get-tuple-element.57), channel_id=1, source_target_pairs={{0,4},{1,5},{2,6},{3,7},{4,8},{5,9},{6,10},{7,11},{8,12},{9,13},{1... | collective-permute-start | bytes 786440 | tf_op jit(solution)/shard_map/ppermute | solution.py:549
  5.7 7.6 %collective-permute-start.2 = (f32[16,32,128]{2,1,0:T(8,128)S(1)}, f32[16,32,128]{2,1,0:T(8,128)S(1)}, u32[]{:S(2)}, u32[]{:S(2)}) collective-permute-start(f32[16,32,128]{2,1,0:T(8,128)S(1)} %get-tuple-element.55.refs_0_), channel_id=1, source_target_pairs={{0,28},{1,29},{2,30},{3,31},{4,0},{5,1},{6,2},{7,3},{8,4},{9,5},{1... | collective-permute-start | bytes 786440 | tf_op jit(solution)/shard_map/ppermute | solution.py:549
  5.8 11.9 %collective-permute-start.3 = (f32[8,64,128]{2,1,0:T(8,128)S(1)}, f32[8,64,128]{2,1,0:T(8,128)S(1)}, u32[]{:S(2)}, u32[]{:S(2)}) collective-permute-start(f32[8,64,128]{2,1,0:T(8,128)S(1)} %shard_map.46.refs_0_), channel_id=1, source_target_pairs={{0,3},{1,0},{2,1},{3,2},{4,7},{5,4},{6,5},{7,6},{8,11},{9,8},{10,9... | collective-permute-start | bytes 786440 | tf_op jit(solution)/shard_map/ppermute | solution.py:553
  13.7 14.7 %collective-permute-start.6 = (f32[8,64,128]{2,1,0:T(8,128)S(1)}, f32[8,64,128]{2,1,0:T(8,128)S(1)}, u32[]{:S(2)}, u32[]{:S(2)}) collective-permute-start(f32[8,64,128]{2,1,0:T(8,128)S(1)} %get-tuple-element.65), channel_id=1, source_target_pairs={{0,3},{1,0},{2,1},{3,2},{4,7},{5,4},{6,5},{7,6},{8,11},{9,8},{10,9... | collective-permute-start | bytes 786440 | tf_op jit(solution)/shard_map/ppermute | solution.py:553
  14.5 10.0 %collective-permute-start.4 = (f32[32,16,128]{2,1,0:T(8,128)S(1)}, f32[32,16,128]{2,1,0:T(8,128)S(1)}, u32[]{:S(2)}, u32[]{:S(2)}) collective-permute-start(f32[32,16,128]{2,1,0:T(8,128)S(1)} %get-tuple-element.63), channel_id=1, source_target_pairs={{0,4},{1,5},{2,6},{3,7},{4,8},{5,9},{6,10},{7,11},{8,12},{9,13},{1... | collective-permute-start | bytes 786440 | tf_op jit(solution)/shard_map/ppermute | solution.py:549
  17.7 9.8 %collective-permute-start.5 = (f32[32,16,128]{2,1,0:T(8,128)S(1)}, f32[32,16,128]{2,1,0:T(8,128)S(1)}, u32[]{:S(2)}, u32[]{:S(2)}) collective-permute-start(f32[32,16,128]{2,1,0:T(8,128)S(1)} %get-tuple-element.64), channel_id=1, source_target_pairs={{0,28},{1,29},{2,30},{3,31},{4,0},{5,1},{6,2},{7,3},{8,4},{9,5},{1... | collective-permute-start | bytes 786440 | tf_op jit(solution)/shard_map/ppermute | solution.py:549
  18.3 10.7 %collective-permute-start.7 = (f32[16,32,128]{2,1,0:T(8,128)S(1)}, f32[16,32,128]{2,1,0:T(8,128)S(1)}, u32[]{:S(2)}, u32[]{:S(2)}) collective-permute-start(f32[16,32,128]{2,1,0:T(8,128)S(1)} %get-tuple-element.66), channel_id=1, source_target_pairs={{0,4},{1,5},{2,6},{3,7},{4,8},{5,9},{6,10},{7,11},{8,12},{9,13},{1... | collective-permute-start | bytes 786440 | tf_op jit(solution)/shard_map/ppermute | solution.py:549
  21.0 11.1 %collective-permute-start.8 = (f32[16,32,128]{2,1,0:T(8,128)S(1)}, f32[16,32,128]{2,1,0:T(8,128)S(1)}, u32[]{:S(2)}, u32[]{:S(2)}) collective-permute-start(f32[16,32,128]{2,1,0:T(8,128)S(1)} %get-tuple-element.67), channel_id=1, source_target_pairs={{0,28},{1,29},{2,30},{3,31},{4,0},{5,1},{6,2},{7,3},{8,4},{9,5},{1... | collective-permute-start | bytes 786440 | tf_op jit(solution)/shard_map/ppermute | solution.py:549
  33.8 8.8 %collective-permute-start.9 = (f32[520,128]{1,0:T(8,128)S(1)}, f32[520,128]{1,0:T(8,128)S(1)}, u32[]{:S(2)}, u32[]{:S(2)}) collective-permute-start(f32[520,128]{1,0:T(8,128)S(1)} %get-tuple-element.72), channel_id=1, source_target_pairs={{0,64},{1,193},{2,66},{3,195},{4,68},{5,197},{6,70},{7,199},{8,72}... | collective-permute-start | bytes 798728 | tf_op jit(solution)/shard_map/ppermute | solution.py:568
  35.4 8.6 %collective-permute-start.10 = (f32[520,128]{1,0:T(8,128)S(1)}, f32[520,128]{1,0:T(8,128)S(1)}, u32[]{:S(2)}, u32[]{:S(2)}) collective-permute-start(f32[520,128]{1,0:T(8,128)S(1)} %get-tuple-element.73), channel_id=1, source_target_pairs={{0,192},{1,65},{2,194},{3,67},{4,196},{5,69},{6,198},{7,71},{8,200... | collective-permute-start | bytes 798728 | tf_op jit(solution)/shard_map/ppermute | solution.py:568
  37.5 12.0 %collective-permute-start.11 = (f32[520,128]{1,0:T(8,128)S(1)}, f32[520,128]{1,0:T(8,128)S(1)}, u32[]{:S(2)}, u32[]{:S(2)}) collective-permute-start(f32[520,128]{1,0:T(8,128)S(1)} %get-tuple-element.76), channel_id=1, source_target_pairs={{0,128},{1,129},{2,130},{3,131},{4,132},{5,133},{6,134},{7,135},{8... | collective-permute-start | bytes 798728 | tf_op jit(solution)/shard_map/ppermute | solution.py:568
  51.2 5.9 %collective-permute-start.12 = (f32[4,128,128]{2,1,0:T(8,128)S(1)}, f32[4,128,128]{2,1,0:T(8,128)S(1)}, u32[]{:S(2)}, u32[]{:S(2)}) collective-permute-start(f32[4,128,128]{2,1,0:T(8,128)S(1)} %get-tuple-element.82), channel_id=1, source_target_pairs={{0,1},{1,2},{2,3},{3,0},{4,5},{5,6},{6,7},{7,4},{8,9},{9,10},{10,1... | collective-permute-start | bytes 786440 | tf_op jit(solution)/shard_map/ppermute | solution.py:553
  57.2 5.2 %collective-permute-start.13 = (f32[8,32,128]{2,1,0:T(8,128)S(1)}, f32[8,32,128]{2,1,0:T(8,128)S(1)}, u32[]{:S(2)}, u32[]{:S(2)}) collective-permute-start(f32[8,32,128]{2,1,0:T(8,128)S(1)} %get-tuple-element.84), channel_id=1, source_target_pairs={{0,4},{1,5},{2,6},{3,7},{4,8},{5,9},{6,10},{7,11},{8,12},{9,13},{1... | collective-permute-start | bytes 393224 | tf_op jit(solution)/shard_map/ppermute | solution.py:549
  58.7 5.0 %collective-permute-start.14 = (f32[8,32,128]{2,1,0:T(8,128)S(1)}, f32[8,32,128]{2,1,0:T(8,128)S(1)}, u32[]{:S(2)}, u32[]{:S(2)}) collective-permute-start(f32[8,32,128]{2,1,0:T(8,128)S(1)} %get-tuple-element.85), channel_id=1, source_target_pairs={{0,28},{1,29},{2,30},{3,31},{4,0},{5,1},{6,2},{7,3},{8,4},{9,5},{1... | collective-permute-start | bytes 393224 | tf_op jit(solution)/shard_map/ppermute | solution.py:549
  63.7 8.8 %collective-permute-start.15 = (f32[544,128]{1,0:T(8,128)S(1)}, f32[544,128]{1,0:T(8,128)S(1)}, u32[]{:S(2)}, u32[]{:S(2)}) collective-permute-start(f32[544,128]{1,0:T(8,128)S(1)} %shard_map.62.refs_1_), channel_id=1, source_target_pairs={{0,32},{32,0},{64,96},{96,64},{128,160},{160,128},{192,224},{224,1... | collective-permute-start | bytes 835592 | tf_op jit(solution)/shard_map/ppermute | solution.py:557
  73.0 5.0 %collective-permute-start.16 = (f32[8,32,128]{2,1,0:T(8,128)S(1)}, f32[8,32,128]{2,1,0:T(8,128)S(1)}, u32[]{:S(2)}, u32[]{:S(2)}) collective-permute-start(f32[8,32,128]{2,1,0:T(8,128)S(1)} %get-tuple-element.87), channel_id=1, source_target_pairs={{0,4},{1,5},{2,6},{3,7},{4,8},{5,9},{6,10},{7,11},{8,12},{9,13},{1... | collective-permute-start | bytes 393224 | tf_op jit(solution)/shard_map/ppermute | solution.py:549
  74.5 5.0 %collective-permute-start.17 = (f32[8,32,128]{2,1,0:T(8,128)S(1)}, f32[8,32,128]{2,1,0:T(8,128)S(1)}, u32[]{:S(2)}, u32[]{:S(2)}) collective-permute-start(f32[8,32,128]{2,1,0:T(8,128)S(1)} %get-tuple-element.88), channel_id=1, source_target_pairs={{0,28},{1,29},{2,30},{3,31},{4,0},{5,1},{6,2},{7,3},{8,4},{9,5},{1... | collective-permute-start | bytes 393224 | tf_op jit(solution)/shard_map/ppermute | solution.py:549
  79.6 4.0 %collective-permute-start.18 = (f32[4,128,128]{2,1,0:T(8,128)S(1)}, f32[4,128,128]{2,1,0:T(8,128)S(1)}, u32[]{:S(2)}, u32[]{:S(2)}) collective-permute-start(f32[4,128,128]{2,1,0:T(8,128)S(1)} %shard_map.64), channel_id=1, source_target_pairs={{0,3},{1,0},{2,1},{3,2},{4,7},{5,4},{6,5},{7,6},{8,11},{9,8},{10,9... | collective-permute-start | bytes 786440 | tf_op jit(solution)/shard_map/ppermute | solution.py:553
  84.5 9.8 %collective-permute-start.20 = (f32[512,128]{1,0:T(8,128)S(1)}, f32[512,128]{1,0:T(8,128)S(1)}, u32[]{:S(2)}, u32[]{:S(2)}) collective-permute-start(f32[512,128]{1,0:T(8,128)S(1)} %get-tuple-element.91), channel_id=1, source_target_pairs={{0,192},{1,65},{2,194},{3,67},{4,196},{5,69},{6,198},{7,71},{8,200... | collective-permute-start | bytes 786440 | tf_op jit(solution)/shard_map/ppermute | solution.py:568
  86.1 9.1 %collective-permute-start.19 = (f32[512,128]{1,0:T(8,128)S(1)}, f32[512,128]{1,0:T(8,128)S(1)}, u32[]{:S(2)}, u32[]{:S(2)}) collective-permute-start(f32[512,128]{1,0:T(8,128)S(1)} %get-tuple-element.90.refs_10_), channel_id=1, source_target_pairs={{0,64},{1,193},{2,66},{3,195},{4,68},{5,197},{6,70},{7,199},{8,72}... | collective-permute-start | bytes 786440 | tf_op jit(solution)/shard_map/ppermute | solution.py:568
  87.4 13.5 %collective-permute-start.21 = (f32[512,128]{1,0:T(8,128)S(1)}, f32[512,128]{1,0:T(8,128)S(1)}, u32[]{:S(2)}, u32[]{:S(2)}) collective-permute-start(f32[512,128]{1,0:T(8,128)S(1)} %get-tuple-element.93), channel_id=1, source_target_pairs={{0,128},{1,129},{2,130},{3,131},{4,132},{5,133},{6,134},{7,135},{8... | collective-permute-start | bytes 786440 | tf_op jit(solution)/shard_map/ppermute | solution.py:568
  102.4 9.4 %collective-permute-start.22 = (f32[512,128]{1,0:T(8,128)S(1)}, f32[512,128]{1,0:T(8,128)S(1)}, u32[]{:S(2)}, u32[]{:S(2)}) collective-permute-start(f32[512,128]{1,0:T(8,128)S(1)} %get-tuple-element.96), channel_id=1, source_target_pairs={{0,64},{1,193},{2,66},{3,195},{4,68},{5,197},{6,70},{7,199},{8,72}... | collective-permute-start | bytes 786440 | tf_op jit(solution)/shard_map/ppermute | solution.py:568
  103.2 8.6 %collective-permute-start.23 = (f32[512,128]{1,0:T(8,128)S(1)}, f32[512,128]{1,0:T(8,128)S(1)}, u32[]{:S(2)}, u32[]{:S(2)}) collective-permute-start(f32[512,128]{1,0:T(8,128)S(1)} %get-tuple-element.97), channel_id=1, source_target_pairs={{0,192},{1,65},{2,194},{3,67},{4,196},{5,69},{6,198},{7,71},{8,200... | collective-permute-start | bytes 786440 | tf_op jit(solution)/shard_map/ppermute | solution.py:568
  104.7 13.1 %collective-permute-start.24 = (f32[512,128]{1,0:T(8,128)S(1)}, f32[512,128]{1,0:T(8,128)S(1)}, u32[]{:S(2)}, u32[]{:S(2)}) collective-permute-start(f32[512,128]{1,0:T(8,128)S(1)} %get-tuple-element.98), channel_id=1, source_target_pairs={{0,128},{1,129},{2,130},{3,131},{4,132},{5,133},{6,134},{7,135},{8... | collective-permute-start | bytes 786440 | tf_op jit(solution)/shard_map/ppermute | solution.py:568
  118.5 5.9 %collective-permute-start.25 = (f32[4,128,128]{2,1,0:T(8,128)S(1)}, f32[4,128,128]{2,1,0:T(8,128)S(1)}, u32[]{:S(2)}, u32[]{:S(2)}) collective-permute-start(f32[4,128,128]{2,1,0:T(8,128)S(1)} %get-tuple-element.100), channel_id=1, source_target_pairs={{0,1},{1,2},{2,3},{3,0},{4,5},{5,6},{6,7},{7,4},{8,9},{9,10},{10,1... | collective-permute-start | bytes 786440 | tf_op jit(solution)/shard_map/ppermute | solution.py:553
  124.5 5.3 %collective-permute-start.26 = (f32[8,32,128]{2,1,0:T(8,128)S(1)}, f32[8,32,128]{2,1,0:T(8,128)S(1)}, u32[]{:S(2)}, u32[]{:S(2)}) collective-permute-start(f32[8,32,128]{2,1,0:T(8,128)S(1)} %get-tuple-element.102), channel_id=1, source_target_pairs={{0,4},{1,5},{2,6},{3,7},{4,8},{5,9},{6,10},{7,11},{8,12},{9,13},{1... | collective-permute-start | bytes 393224 | tf_op jit(solution)/shard_map/ppermute | solution.py:549
  127.2 5.0 %collective-permute-start.27 = (f32[8,32,128]{2,1,0:T(8,128)S(1)}, f32[8,32,128]{2,1,0:T(8,128)S(1)}, u32[]{:S(2)}, u32[]{:S(2)}) collective-permute-start(f32[8,32,128]{2,1,0:T(8,128)S(1)} %get-tuple-element.103), channel_id=1, source_target_pairs={{0,28},{1,29},{2,30},{3,31},{4,0},{5,1},{6,2},{7,3},{8,4},{9,5},{1... | collective-permute-start | bytes 393224 | tf_op jit(solution)/shard_map/ppermute | solution.py:549
  132.2 8.0 %collective-permute-start.28 = (f32[512,128]{1,0:T(8,128)S(1)}, f32[512,128]{1,0:T(8,128)S(1)}, u32[]{:S(2)}, u32[]{:S(2)}) collective-permute-start(f32[512,128]{1,0:T(8,128)S(1)} %shard_map.72.refs_1_), channel_id=1, source_target_pairs={{0,32},{32,0},{64,96},{96,64},{128,160},{160,128},{192,224},{224,1... | collective-permute-start | bytes 786440 | tf_op jit(solution)/shard_map/ppermute | solution.py:557
  140.3 8.8 %collective-permute-start.31 = (f32[512,128]{1,0:T(8,128)S(1)}, f32[512,128]{1,0:T(8,128)S(1)}, u32[]{:S(2)}, u32[]{:S(2)}) collective-permute-start(f32[512,128]{1,0:T(8,128)S(1)} %shard_map.73.refs_0_), channel_id=1, source_target_pairs={{0,128},{1,129},{2,130},{3,131},{4,132},{5,133},{6,134},{7,135},{8... | collective-permute-start | bytes 786440 | tf_op jit(solution)/shard_map/ppermute | solution.py:568
  141.0 10.8 %collective-permute-start.30 = (f32[512,128]{1,0:T(8,128)S(1)}, f32[512,128]{1,0:T(8,128)S(1)}, u32[]{:S(2)}, u32[]{:S(2)}) collective-permute-start(f32[512,128]{1,0:T(8,128)S(1)} %shard_map.73.refs_0_), channel_id=1, source_target_pairs={{0,192},{1,65},{2,194},{3,67},{4,196},{5,69},{6,198},{7,71},{8,200... | collective-permute-start | bytes 786440 | tf_op jit(solution)/shard_map/ppermute | solution.py:568
  142.5 9.3 %collective-permute-start.29 = (f32[512,128]{1,0:T(8,128)S(1)}, f32[512,128]{1,0:T(8,128)S(1)}, u32[]{:S(2)}, u32[]{:S(2)}) collective-permute-start(f32[512,128]{1,0:T(8,128)S(1)} %shard_map.73.refs_0_), channel_id=1, source_target_pairs={{0,64},{1,193},{2,66},{3,195},{4,68},{5,197},{6,70},{7,199},{8,72}... | collective-permute-start | bytes 786440 | tf_op jit(solution)/shard_map/ppermute | solution.py:568
  (5 other events, 22.4 us)

commit v4 on v3

--- a/solution.py
+++ b/solution.py
@@ -354,15 +354,13 @@
         send[:512] = out[pl.ds(8 * (x ^ j), 8)].reshape(512, BY)
 
 
-def second_x_kernel(yb, above, below, lx, out):
-    x_filter(lx, planes_of(yb), above, below, storer(out))
-
-
 def second_y_kernel(xa, packs, wy, wr, out):
     y_filter(wy, wr, planes_of(xa), packs, storer(out))
 
 
-def ratio_start_kernel(ga, gb, kf, kb, obs, note, s0, s1, s3, s2, out):
+def ratio_start_kernel(ga, yb, above, below, lx, kf, kb, obs, note, s0, s1, s3, s2, out, gb):
+    x_filter(lx, planes_of(yb), above, below, storer(gb))
+
     def load(c):
         return jnp.concatenate([ga[:, c, :], gb[:, c, :]], axis=0).reshape(256, BY)
 
@@ -591,9 +589,8 @@
     obs = call(rows_kernel, [sds(Z, BX, BY)], offsets, obs, above, below, smem=(0,),
                before=(yb,))
     ga = call(second_y_kernel, [HALF], xa, cols_a, wyf, wrf, before=(obs,))
-    gb = call(second_x_kernel, [HALF], yb, *rows_b, lxf, before=(ga,))
-    parts = call(ratio_start_kernel, [SHARD] + [NOTED] * 3, ga, gb, kzf, kzb, obs, note,
-                 scratch=[WHOLE])
+    parts = call(ratio_start_kernel, [SHARD] + [NOTED] * 3, ga, yb, *rows_b, lxf, kzf, kzb,
+                 obs, note, scratch=[WHOLE, pltpu.VMEM((HALF_Z, BX, BY), F32)])
     for step in range(ITERS):
         first = step == 0
         if not first:
@@ -608,9 +605,11 @@
         own, one, three, two = trade(*parts)
         if first:
             near = call(near_matrices_kernel, many(3), note, one, three, scratch=TAP_SCRATCH)
-            far = call(far_matrices_kernel, many(1), two, near[3], scratch=TAP_SCRATCH)
             notes = (note, one, three, two)
         part = call(collect_first_kernel, [sds(12, 192, BY)], own, one, three, *near[1:3])
+        if first:
+            far = call(far_matrices_kernel, many(1), two, near[3], before=(part,),
+                       scratch=TAP_SCRATCH)
         main, packs = call(collect_kernel, [sds(8, BY, BY), PACK], part, two, *far[1:],
                            scratch=[pltpu.VMEM((12, BX, BY), F32)])
         own, up, down = call(add_cols_kernel, [sds(512, BY), EDGE, EDGE],

time: 153 us -> 152 us (level)
  waiting for transfers between devices: 94.1 us -> 92.5 us
    ppermute x12, waiting for transfers between devices: 39.7 us -> 38.1 us  [swap(): return lax.ppermute(x, ('view', 'blk'), pairs)]
    pallas_call x29 -> x28, Pallas kernels: 15.6 us -> 15.6 us  [call(): pl.pallas_call(inner, out_shape=out_shape, in_specs=specs, out_specs=[pl....]
  transfers between devices with their start and end apart: 32 -> 32, of which waited for: 26 -> 25; matrix products, arithmetic and copies ran while one was open for 0% -> 0% of each run, Pallas kernels for 4% -> 5%
where the time goes in v4:
time: 152 us; the launch traced here: 151 us
  waiting for transfers between devices  92.5 us (61%)
  starting transfers between devices  40.4 us (27%)
  Pallas kernels  15.6 us (10%)
  local copies, waits for them, and re-layouts  2.27 us (1%)
    ppermute x12, waiting for transfers between devices, swap(): return lax.ppermute(x, ('view', 'blk'), pairs)  38.1 us
    ppermute x12, waiting for transfers between devices, along_rows(): return lax.ppermute(x, 'blk', [(i, (i + 4 * by) % 32) for i in range(32)])  25.5 us
    ppermute x6, waiting for transfers between devices, along_cols(): lax.ppermute(x, 'blk', [(i, i // 4 * 4 + (i + by) % 4) for i in range(32)])  18.8 us
    ppermute x12, starting transfers between devices, swap(): return lax.ppermute(x, ('view', 'blk'), pairs)  17.2 us
    pallas_call x28, Pallas kernels, call(): pl.pallas_call(inner, out_shape=out_shape, in_specs=specs, out_specs=[pl....  15.6 us
    ppermute x12, starting transfers between devices, along_rows(): return lax.ppermute(x, 'blk', [(i, (i + 4 * by) % 32) for i in range(32)])  14.5 us
    ppermute x2, waiting for transfers between devices, view_swap(): return lax.ppermute(x, 'view', [(i, i ^ mask) for i in range(8)])  10.1 us
    ppermute x2, starting transfers between devices, view_swap(): return lax.ppermute(x, 'view', [(i, i ^ mask) for i in range(8)])  6.37 us
  transfers between devices with their start and end apart: 32, of which 25 were waited for; matrix products, arithmetic and copies ran while one was open for 0% of the time, Pallas kernels for 5%

profile of v4, /device:TPU:32, one launch (start us, length us, event | category | flops | bytes accessed | tf_op | source)
XLA Modules:
  0.0 151.1 jit_solution(14580970816170390099)
XLA Ops:
  3.8 1.9 %collective-permute-start.1 = (f32[16,32,128]{2,1,0:T(8,128)S(1)}, f32[16,32,128]{2,1,0:T(8,128)S(1)}, u32[]{:S(2)}, u32[]{:S(2)}) collective-permute-start(f32[16,32,128]{2,1,0:T(8,128)S(1)} %get-tuple-element.57), channel_id=1, source_target_pairs={{0,4},{1,5},{2,6},{3,7},{4,8},{5,9},{6,10},{7,11},{8,12},{9,13},{1... | collective-permute-start | bytes 786440 | tf_op jit(solution)/shard_map/ppermute | solution.py:547
  7.2 3.3 %collective-permute-done.refs_2_ = f32[16,64,128]{2,1,0:T(8,128)S(1)} collective-permute-done((f32[16,64,128]{2,1,0:T(8,128)S(1)}, f32[16,64,128]{2,1,0:T(8,128)S(1)}, u32[]{:S(2)}, u32[]{:S(2)}) %collective-permute-start) | collective-permute-done | bytes 524320 | tf_op jit(solution)/shard_map/ppermute | solution.py:551
  14.5 3.3 %collective-permute-start.4 = (f32[32,16,128]{2,1,0:T(8,128)S(1)}, f32[32,16,128]{2,1,0:T(8,128)S(1)}, u32[]{:S(2)}, u32[]{:S(2)}) collective-permute-start(f32[32,16,128]{2,1,0:T(8,128)S(1)} %get-tuple-element.63), channel_id=1, source_target_pairs={{0,4},{1,5},{2,6},{3,7},{4,8},{5,9},{6,10},{7,11},{8,12},{9,13},{1... | collective-permute-start | bytes 786440 | tf_op jit(solution)/shard_map/ppermute | solution.py:547
  18.3 2.7 %collective-permute-start.7 = (f32[16,32,128]{2,1,0:T(8,128)S(1)}, f32[16,32,128]{2,1,0:T(8,128)S(1)}, u32[]{:S(2)}, u32[]{:S(2)}) collective-permute-start(f32[16,32,128]{2,1,0:T(8,128)S(1)} %get-tuple-element.66), channel_id=1, source_target_pairs={{0,4},{1,5},{2,6},{3,7},{4,8},{5,9},{6,10},{7,11},{8,12},{9,13},{1... | collective-permute-start | bytes 786440 | tf_op jit(solution)/shard_map/ppermute | solution.py:547
  21.2 3.3 %collective-permute-done.4.refs_3_ = f32[32,16,128]{2,1,0:T(8,128)S(1)} collective-permute-done((f32[32,16,128]{2,1,0:T(8,128)S(1)}, f32[32,16,128]{2,1,0:T(8,128)S(1)}, u32[]{:S(2)}, u32[]{:S(2)}) %collective-permute-start.4) | collective-permute-done | bytes 262176 | tf_op jit(solution)/shard_map/ppermute | solution.py:547
  24.5 3.0 %collective-permute-done.5.refs_4_ = f32[32,16,128]{2,1,0:T(8,128)S(1)} collective-permute-done((f32[32,16,128]{2,1,0:T(8,128)S(1)}, f32[32,16,128]{2,1,0:T(8,128)S(1)}, u32[]{:S(2)}, u32[]{:S(2)}) %collective-permute-start.5) | collective-permute-done | bytes 262176 | tf_op jit(solution)/shard_map/ppermute | solution.py:547
  29.0 3.2 %collective-permute-done.8.refs_3_ = f32[16,32,128]{2,1,0:T(8,128)S(1)} collective-permute-done((f32[16,32,128]{2,1,0:T(8,128)S(1)}, f32[16,32,128]{2,1,0:T(8,128)S(1)}, u32[]{:S(2)}, u32[]{:S(2)}) %collective-permute-start.8) | collective-permute-done | bytes 262176 | tf_op jit(solution)/shard_map/ppermute | solution.py:547
  35.4 2.1 %collective-permute-start.10 = (f32[520,128]{1,0:T(8,128)S(1)}, f32[520,128]{1,0:T(8,128)S(1)}, u32[]{:S(2)}, u32[]{:S(2)}) collective-permute-start(f32[520,128]{1,0:T(8,128)S(1)} %get-tuple-element.73), channel_id=1, source_target_pairs={{0,192},{1,65},{2,194},{3,67},{4,196},{5,69},{6,198},{7,71},{8,200... | collective-permute-start | bytes 798728 | tf_op jit(solution)/shard_map/ppermute | solution.py:566
  38.1 4.4 %collective-permute-done.9.refs_1_.refs_4_ = f32[520,128]{1,0:T(8,128)S(1)} collective-permute-done((f32[520,128]{1,0:T(8,128)S(1)}, f32[520,128]{1,0:T(8,128)S(1)}, u32[]{:S(2)}, u32[]{:S(2)}) %collective-permute-start.9) | collective-permute-done | bytes 266272 | tf_op jit(solution)/shard_map/ppermute | solution.py:566
  45.3 4.1 %collective-permute-done.11.refs_1_.refs_6_ = f32[520,128]{1,0:T(8,128)S(1)} collective-permute-done((f32[520,128]{1,0:T(8,128)S(1)}, f32[520,128]{1,0:T(8,128)S(1)}, u32[]{:S(2)}, u32[]{:S(2)}) %collective-permute-start.11) | collective-permute-done | bytes 266272 | tf_op jit(solution)/shard_map/ppermute | solution.py:566
  50.5 5.8 %collective-permute-done.12.refs_1_ = f32[4,128,128]{2,1,0:T(8,128)S(1)} collective-permute-done((f32[4,128,128]{2,1,0:T(8,128)S(1)}, f32[4,128,128]{2,1,0:T(8,128)S(1)}, u32[]{:S(2)}, u32[]{:S(2)}) %collective-permute-start.12) | collective-permute-done | bytes 262176 | tf_op jit(solution)/shard_map/ppermute | solution.py:551
  58.5 3.1 %collective-permute-done.13.refs_1_ = f32[8,32,128]{2,1,0:T(8,128)S(1)} collective-permute-done((f32[8,32,128]{2,1,0:T(8,128)S(1)}, f32[8,32,128]{2,1,0:T(8,128)S(1)}, u32[]{:S(2)}, u32[]{:S(2)}) %collective-permute-start.13) | collective-permute-done | bytes 131104 | tf_op jit(solution)/shard_map/ppermute | solution.py:547
  63.2 3.5 %collective-permute-start.15 = (f32[544,128]{1,0:T(8,128)S(1)}, f32[544,128]{1,0:T(8,128)S(1)}, u32[]{:S(2)}, u32[]{:S(2)}) collective-permute-start(f32[544,128]{1,0:T(8,128)S(1)} %shard_map.61.refs_1_), channel_id=1, source_target_pairs={{0,32},{32,0},{64,96},{96,64},{128,160},{160,128},{192,224},{224,1... | collective-permute-start | bytes 835592 | tf_op jit(solution)/shard_map/ppermute | solution.py:555
  66.7 5.0 %collective-permute-done.15.refs_2_ = f32[544,128]{1,0:T(8,128)S(1)} collective-permute-done((f32[544,128]{1,0:T(8,128)S(1)}, f32[544,128]{1,0:T(8,128)S(1)}, u32[]{:S(2)}, u32[]{:S(2)}) %collective-permute-start.15) | collective-permute-done | bytes 278560 | tf_op jit(solution)/shard_map/ppermute | solution.py:555
  72.2 1.8 %collective-permute-start.16 = (f32[8,32,128]{2,1,0:T(8,128)S(1)}, f32[8,32,128]{2,1,0:T(8,128)S(1)}, u32[]{:S(2)}, u32[]{:S(2)}) collective-permute-start(f32[8,32,128]{2,1,0:T(8,128)S(1)} %get-tuple-element.87), channel_id=1, source_target_pairs={{0,4},{1,5},{2,6},{3,7},{4,8},{5,9},{6,10},{7,11},{8,12},{9,13},{1... | collective-permute-start | bytes 393224 | tf_op jit(solution)/shard_map/ppermute | solution.py:547
  74.3 2.9 %collective-permute-done.16.refs_1_ = f32[8,32,128]{2,1,0:T(8,128)S(1)} collective-permute-done((f32[8,32,128]{2,1,0:T(8,128)S(1)}, f32[8,32,128]{2,1,0:T(8,128)S(1)}, u32[]{:S(2)}, u32[]{:S(2)}) %collective-permute-start.16) | collective-permute-done | bytes 131104 | tf_op jit(solution)/shard_map/ppermute | solution.py:547
  77.3 1.7 %collective-permute-done.17.refs_2_ = f32[8,32,128]{2,1,0:T(8,128)S(1)} collective-permute-done((f32[8,32,128]{2,1,0:T(8,128)S(1)}, f32[8,32,128]{2,1,0:T(8,128)S(1)}, u32[]{:S(2)}, u32[]{:S(2)}) %collective-permute-start.17) | collective-permute-done | bytes 131104 | tf_op jit(solution)/shard_map/ppermute | solution.py:547
  79.2 3.9 %collective-permute-done.18.refs_3_ = f32[4,128,128]{2,1,0:T(8,128)S(1)} collective-permute-done((f32[4,128,128]{2,1,0:T(8,128)S(1)}, f32[4,128,128]{2,1,0:T(8,128)S(1)}, u32[]{:S(2)}, u32[]{:S(2)}) %collective-permute-start.18) | collective-permute-done | bytes 262176 | tf_op jit(solution)/shard_map/ppermute | solution.py:551
  86.7 3.1 %collective-permute-start.21 = (f32[512,128]{1,0:T(8,128)S(1)}, f32[512,128]{1,0:T(8,128)S(1)}, u32[]{:S(2)}, u32[]{:S(2)}) collective-permute-start(f32[512,128]{1,0:T(8,128)S(1)} %get-tuple-element.93), channel_id=1, source_target_pairs={{0,128},{1,129},{2,130},{3,131},{4,132},{5,133},{6,134},{7,135},{8... | collective-permute-start | bytes 786440 | tf_op jit(solution)/shard_map/ppermute | solution.py:566
  89.7 5.1 %collective-permute-done.20.refs_1_.refs_2_ = f32[512,128]{1,0:T(8,128)S(1)} collective-permute-done((f32[512,128]{1,0:T(8,128)S(1)}, f32[512,128]{1,0:T(8,128)S(1)}, u32[]{:S(2)}, u32[]{:S(2)}) %collective-permute-start.20) | collective-permute-done | bytes 262176 | tf_op jit(solution)/shard_map/ppermute | solution.py:566
  94.8 5.3 %collective-permute-done.21.refs_3_ = f32[512,128]{1,0:T(8,128)S(1)} collective-permute-done((f32[512,128]{1,0:T(8,128)S(1)}, f32[512,128]{1,0:T(8,128)S(1)}, u32[]{:S(2)}, u32[]{:S(2)}) %collective-permute-start.21) | collective-permute-done | bytes 262176 | tf_op jit(solution)/shard_map/ppermute | solution.py:566
  103.9 2.0 %collective-permute-start.24 = (f32[512,128]{1,0:T(8,128)S(1)}, f32[512,128]{1,0:T(8,128)S(1)}, u32[]{:S(2)}, u32[]{:S(2)}) collective-permute-start(f32[512,128]{1,0:T(8,128)S(1)} %get-tuple-element.98), channel_id=1, source_target_pairs={{0,128},{1,129},{2,130},{3,131},{4,132},{5,133},{6,134},{7,135},{8... | collective-permute-start | bytes 786440 | tf_op jit(solution)/shard_map/ppermute | solution.py:566
  106.0 5.0 %collective-permute-done.22.refs_1_ = f32[512,128]{1,0:T(8,128)S(1)} collective-permute-done((f32[512,128]{1,0:T(8,128)S(1)}, f32[512,128]{1,0:T(8,128)S(1)}, u32[]{:S(2)}, u32[]{:S(2)}) %collective-permute-start.22) | collective-permute-done | bytes 262176 | tf_op jit(solution)/shard_map/ppermute | solution.py:566
  111.7 4.9 %collective-permute-done.24.refs_1_ = f32[512,128]{1,0:T(8,128)S(1)} collective-permute-done((f32[512,128]{1,0:T(8,128)S(1)}, f32[512,128]{1,0:T(8,128)S(1)}, u32[]{:S(2)}, u32[]{:S(2)}) %collective-permute-start.24) | collective-permute-done | bytes 262176 | tf_op jit(solution)/shard_map/ppermute | solution.py:566
  117.5 5.8 %collective-permute-done.25.refs_1_ = f32[4,128,128]{2,1,0:T(8,128)S(1)} collective-permute-done((f32[4,128,128]{2,1,0:T(8,128)S(1)}, f32[4,128,128]{2,1,0:T(8,128)S(1)}, u32[]{:S(2)}, u32[]{:S(2)}) %collective-permute-start.25) | collective-permute-done | bytes 262176 | tf_op jit(solution)/shard_map/ppermute | solution.py:551
  123.4 1.8 %collective-permute-start.26 = (f32[8,32,128]{2,1,0:T(8,128)S(1)}, f32[8,32,128]{2,1,0:T(8,128)S(1)}, u32[]{:S(2)}, u32[]{:S(2)}) collective-permute-start(f32[8,32,128]{2,1,0:T(8,128)S(1)} %get-tuple-element.102), channel_id=1, source_target_pairs={{0,4},{1,5},{2,6},{3,7},{4,8},{5,9},{6,10},{7,11},{8,12},{9,13},{1... | collective-permute-start | bytes 393224 | tf_op jit(solution)/shard_map/ppermute | solution.py:547
  125.5 3.0 %collective-permute-done.26.refs_1_ = f32[8,32,128]{2,1,0:T(8,128)S(1)} collective-permute-done((f32[8,32,128]{2,1,0:T(8,128)S(1)}, f32[8,32,128]{2,1,0:T(8,128)S(1)}, u32[]{:S(2)}, u32[]{:S(2)}) %collective-permute-start.26) | collective-permute-done | bytes 131104 | tf_op jit(solution)/shard_map/ppermute | solution.py:547
  128.5 2.1 %collective-permute-done.27.refs_2_ = f32[8,32,128]{2,1,0:T(8,128)S(1)} collective-permute-done((f32[8,32,128]{2,1,0:T(8,128)S(1)}, f32[8,32,128]{2,1,0:T(8,128)S(1)}, u32[]{:S(2)}, u32[]{:S(2)}) %collective-permute-start.27) | collective-permute-done | bytes 131104 | tf_op jit(solution)/shard_map/ppermute | solution.py:547
  130.6 2.9 %collective-permute-start.28 = (f32[512,128]{1,0:T(8,128)S(1)}, f32[512,128]{1,0:T(8,128)S(1)}, u32[]{:S(2)}, u32[]{:S(2)}) collective-permute-start(f32[512,128]{1,0:T(8,128)S(1)} %shard_map.71.refs_1_), channel_id=1, source_target_pairs={{0,32},{32,0},{64,96},{96,64},{128,160},{160,128},{192,224},{224,1... | collective-permute-start | bytes 786440 | tf_op jit(solution)/shard_map/ppermute | solution.py:555
  133.5 5.1 %collective-permute-done.28.refs_2_ = f32[512,128]{1,0:T(8,128)S(1)} collective-permute-done((f32[512,128]{1,0:T(8,128)S(1)}, f32[512,128]{1,0:T(8,128)S(1)}, u32[]{:S(2)}, u32[]{:S(2)}) %collective-permute-start.28) | collective-permute-done | bytes 262176 | tf_op jit(solution)/shard_map/ppermute | solution.py:555
  142.2 5.1 %collective-permute-done.31.refs_3_ = f32[512,128]{1,0:T(8,128)S(1)} collective-permute-done((f32[512,128]{1,0:T(8,128)S(1)}, f32[512,128]{1,0:T(8,128)S(1)}, u32[]{:S(2)}, u32[]{:S(2)}) %collective-permute-start.31) | collective-permute-done | bytes 262176 | tf_op jit(solution)/shard_map/ppermute | solution.py:566
  147.3 2.7 %collective-permute-done.30.refs_2_ = f32[512,128]{1,0:T(8,128)S(1)} collective-permute-done((f32[512,128]{1,0:T(8,128)S(1)}, f32[512,128]{1,0:T(8,128)S(1)}, u32[]{:S(2)}, u32[]{:S(2)}) %collective-permute-start.30) | collective-permute-done | bytes 262176 | tf_op jit(solution)/shard_map/ppermute | solution.py:566
  (71 shorter events, 38.0 us)
Async XLA Ops:
  2.7 7.8 %collective-permute-start = (f32[16,64,128]{2,1,0:T(8,128)S(1)}, f32[16,64,128]{2,1,0:T(8,128)S(1)}, u32[]{:S(2)}, u32[]{:S(2)}) collective-permute-start(f32[16,64,128]{2,1,0:T(8,128)S(1)} %shard_map.48), channel_id=1, source_target_pairs={{0,3},{1,0},{2,1},{3,2},{4,7},{5,4},{6,5},{7,6},{8,11},{9,8},{10,9... | collective-permute-start | bytes 1572872 | tf_op jit(solution)/shard_map/ppermute | solution.py:551
  3.8 7.8 %collective-permute-start.1 = (f32[16,32,128]{2,1,0:T(8,128)S(1)}, f32[16,32,128]{2,1,0:T(8,128)S(1)}, u32[]{:S(2)}, u32[]{:S(2)}) collective-permute-start(f32[16,32,128]{2,1,0:T(8,128)S(1)} %get-tuple-element.57), channel_id=1, source_target_pairs={{0,4},{1,5},{2,6},{3,7},{4,8},{5,9},{6,10},{7,11},{8,12},{9,13},{1... | collective-permute-start | bytes 786440 | tf_op jit(solution)/shard_map/ppermute | solution.py:547
  5.7 7.6 %collective-permute-start.2 = (f32[16,32,128]{2,1,0:T(8,128)S(1)}, f32[16,32,128]{2,1,0:T(8,128)S(1)}, u32[]{:S(2)}, u32[]{:S(2)}) collective-permute-start(f32[16,32,128]{2,1,0:T(8,128)S(1)} %get-tuple-element.55.refs_0_), channel_id=1, source_target_pairs={{0,28},{1,29},{2,30},{3,31},{4,0},{5,1},{6,2},{7,3},{8,4},{9,5},{1... | collective-permute-start | bytes 786440 | tf_op jit(solution)/shard_map/ppermute | solution.py:547
  5.8 11.9 %collective-permute-start.3 = (f32[8,64,128]{2,1,0:T(8,128)S(1)}, f32[8,64,128]{2,1,0:T(8,128)S(1)}, u32[]{:S(2)}, u32[]{:S(2)}) collective-permute-start(f32[8,64,128]{2,1,0:T(8,128)S(1)} %shard_map.46.refs_0_), channel_id=1, source_target_pairs={{0,3},{1,0},{2,1},{3,2},{4,7},{5,4},{6,5},{7,6},{8,11},{9,8},{10,9... | collective-permute-start | bytes 786440 | tf_op jit(solution)/shard_map/ppermute | solution.py:551
  13.7 14.7 %collective-permute-start.6 = (f32[8,64,128]{2,1,0:T(8,128)S(1)}, f32[8,64,128]{2,1,0:T(8,128)S(1)}, u32[]{:S(2)}, u32[]{:S(2)}) collective-permute-start(f32[8,64,128]{2,1,0:T(8,128)S(1)} %get-tuple-element.65), channel_id=1, source_target_pairs={{0,3},{1,0},{2,1},{3,2},{4,7},{5,4},{6,5},{7,6},{8,11},{9,8},{10,9... | collective-permute-start | bytes 786440 | tf_op jit(solution)/shard_map/ppermute | solution.py:551
  14.5 10.0 %collective-permute-start.4 = (f32[32,16,128]{2,1,0:T(8,128)S(1)}, f32[32,16,128]{2,1,0:T(8,128)S(1)}, u32[]{:S(2)}, u32[]{:S(2)}) collective-permute-start(f32[32,16,128]{2,1,0:T(8,128)S(1)} %get-tuple-element.63), channel_id=1, source_target_pairs={{0,4},{1,5},{2,6},{3,7},{4,8},{5,9},{6,10},{7,11},{8,12},{9,13},{1... | collective-permute-start | bytes 786440 | tf_op jit(solution)/shard_map/ppermute | solution.py:547
  17.7 9.8 %collective-permute-start.5 = (f32[32,16,128]{2,1,0:T(8,128)S(1)}, f32[32,16,128]{2,1,0:T(8,128)S(1)}, u32[]{:S(2)}, u32[]{:S(2)}) collective-permute-start(f32[32,16,128]{2,1,0:T(8,128)S(1)} %get-tuple-element.64), channel_id=1, source_target_pairs={{0,28},{1,29},{2,30},{3,31},{4,0},{5,1},{6,2},{7,3},{8,4},{9,5},{1... | collective-permute-start | bytes 786440 | tf_op jit(solution)/shard_map/ppermute | solution.py:547
  18.3 10.7 %collective-permute-start.7 = (f32[16,32,128]{2,1,0:T(8,128)S(1)}, f32[16,32,128]{2,1,0:T(8,128)S(1)}, u32[]{:S(2)}, u32[]{:S(2)}) collective-permute-start(f32[16,32,128]{2,1,0:T(8,128)S(1)} %get-tuple-element.66), channel_id=1, source_target_pairs={{0,4},{1,5},{2,6},{3,7},{4,8},{5,9},{6,10},{7,11},{8,12},{9,13},{1... | collective-permute-start | bytes 786440 | tf_op jit(solution)/shard_map/ppermute | solution.py:547
  21.0 11.1 %collective-permute-start.8 = (f32[16,32,128]{2,1,0:T(8,128)S(1)}, f32[16,32,128]{2,1,0:T(8,128)S(1)}, u32[]{:S(2)}, u32[]{:S(2)}) collective-permute-start(f32[16,32,128]{2,1,0:T(8,128)S(1)} %get-tuple-element.67), channel_id=1, source_target_pairs={{0,28},{1,29},{2,30},{3,31},{4,0},{5,1},{6,2},{7,3},{8,4},{9,5},{1... | collective-permute-start | bytes 786440 | tf_op jit(solution)/shard_map/ppermute | solution.py:547
  33.8 8.8 %collective-permute-start.9 = (f32[520,128]{1,0:T(8,128)S(1)}, f32[520,128]{1,0:T(8,128)S(1)}, u32[]{:S(2)}, u32[]{:S(2)}) collective-permute-start(f32[520,128]{1,0:T(8,128)S(1)} %get-tuple-element.72), channel_id=1, source_target_pairs={{0,64},{1,193},{2,66},{3,195},{4,68},{5,197},{6,70},{7,199},{8,72}... | collective-permute-start | bytes 798728 | tf_op jit(solution)/shard_map/ppermute | solution.py:566
  35.4 8.6 %collective-permute-start.10 = (f32[520,128]{1,0:T(8,128)S(1)}, f32[520,128]{1,0:T(8,128)S(1)}, u32[]{:S(2)}, u32[]{:S(2)}) collective-permute-start(f32[520,128]{1,0:T(8,128)S(1)} %get-tuple-element.73), channel_id=1, source_target_pairs={{0,192},{1,65},{2,194},{3,67},{4,196},{5,69},{6,198},{7,71},{8,200... | collective-permute-start | bytes 798728 | tf_op jit(solution)/shard_map/ppermute | solution.py:566
  37.5 12.0 %collective-permute-start.11 = (f32[520,128]{1,0:T(8,128)S(1)}, f32[520,128]{1,0:T(8,128)S(1)}, u32[]{:S(2)}, u32[]{:S(2)}) collective-permute-start(f32[520,128]{1,0:T(8,128)S(1)} %get-tuple-element.76), channel_id=1, source_target_pairs={{0,128},{1,129},{2,130},{3,131},{4,132},{5,133},{6,134},{7,135},{8... | collective-permute-start | bytes 798728 | tf_op jit(solution)/shard_map/ppermute | solution.py:566
  50.4 5.9 %collective-permute-start.12 = (f32[4,128,128]{2,1,0:T(8,128)S(1)}, f32[4,128,128]{2,1,0:T(8,128)S(1)}, u32[]{:S(2)}, u32[]{:S(2)}) collective-permute-start(f32[4,128,128]{2,1,0:T(8,128)S(1)} %get-tuple-element.82), channel_id=1, source_target_pairs={{0,1},{1,2},{2,3},{3,0},{4,5},{5,6},{6,7},{7,4},{8,9},{9,10},{10,1... | collective-permute-start | bytes 786440 | tf_op jit(solution)/shard_map/ppermute | solution.py:551
  56.4 5.2 %collective-permute-start.13 = (f32[8,32,128]{2,1,0:T(8,128)S(1)}, f32[8,32,128]{2,1,0:T(8,128)S(1)}, u32[]{:S(2)}, u32[]{:S(2)}) collective-permute-start(f32[8,32,128]{2,1,0:T(8,128)S(1)} %get-tuple-element.84), channel_id=1, source_target_pairs={{0,4},{1,5},{2,6},{3,7},{4,8},{5,9},{6,10},{7,11},{8,12},{9,13},{1... | collective-permute-start | bytes 393224 | tf_op jit(solution)/shard_map/ppermute | solution.py:547
  57.9 5.3 %collective-permute-start.14 = (f32[8,32,128]{2,1,0:T(8,128)S(1)}, f32[8,32,128]{2,1,0:T(8,128)S(1)}, u32[]{:S(2)}, u32[]{:S(2)}) collective-permute-start(f32[8,32,128]{2,1,0:T(8,128)S(1)} %get-tuple-element.85), channel_id=1, source_target_pairs={{0,28},{1,29},{2,30},{3,31},{4,0},{5,1},{6,2},{7,3},{8,4},{9,5},{1... | collective-permute-start | bytes 393224 | tf_op jit(solution)/shard_map/ppermute | solution.py:547
  63.2 8.5 %collective-permute-start.15 = (f32[544,128]{1,0:T(8,128)S(1)}, f32[544,128]{1,0:T(8,128)S(1)}, u32[]{:S(2)}, u32[]{:S(2)}) collective-permute-start(f32[544,128]{1,0:T(8,128)S(1)} %shard_map.61.refs_1_), channel_id=1, source_target_pairs={{0,32},{32,0},{64,96},{96,64},{128,160},{160,128},{192,224},{224,1... | collective-permute-start | bytes 835592 | tf_op jit(solution)/shard_map/ppermute | solution.py:555
  72.2 5.0 %collective-permute-start.16 = (f32[8,32,128]{2,1,0:T(8,128)S(1)}, f32[8,32,128]{2,1,0:T(8,128)S(1)}, u32[]{:S(2)}, u32[]{:S(2)}) collective-permute-start(f32[8,32,128]{2,1,0:T(8,128)S(1)} %get-tuple-element.87), channel_id=1, source_target_pairs={{0,4},{1,5},{2,6},{3,7},{4,8},{5,9},{6,10},{7,11},{8,12},{9,13},{1... | collective-permute-start | bytes 393224 | tf_op jit(solution)/shard_map/ppermute | solution.py:547
  74.0 5.0 %collective-permute-start.17 = (f32[8,32,128]{2,1,0:T(8,128)S(1)}, f32[8,32,128]{2,1,0:T(8,128)S(1)}, u32[]{:S(2)}, u32[]{:S(2)}) collective-permute-start(f32[8,32,128]{2,1,0:T(8,128)S(1)} %get-tuple-element.88), channel_id=1, source_target_pairs={{0,28},{1,29},{2,30},{3,31},{4,0},{5,1},{6,2},{7,3},{8,4},{9,5},{1... | collective-permute-start | bytes 393224 | tf_op jit(solution)/shard_map/ppermute | solution.py:547
  79.1 4.0 %collective-permute-start.18 = (f32[4,128,128]{2,1,0:T(8,128)S(1)}, f32[4,128,128]{2,1,0:T(8,128)S(1)}, u32[]{:S(2)}, u32[]{:S(2)}) collective-permute-start(f32[4,128,128]{2,1,0:T(8,128)S(1)} %shard_map.63), channel_id=1, source_target_pairs={{0,3},{1,0},{2,1},{3,2},{4,7},{5,4},{6,5},{7,6},{8,11},{9,8},{10,9... | collective-permute-start | bytes 786440 | tf_op jit(solution)/shard_map/ppermute | solution.py:551
  84.0 10.8 %collective-permute-start.20 = (f32[512,128]{1,0:T(8,128)S(1)}, f32[512,128]{1,0:T(8,128)S(1)}, u32[]{:S(2)}, u32[]{:S(2)}) collective-permute-start(f32[512,128]{1,0:T(8,128)S(1)} %get-tuple-element.91), channel_id=1, source_target_pairs={{0,192},{1,65},{2,194},{3,67},{4,196},{5,69},{6,198},{7,71},{8,200... | collective-permute-start | bytes 786440 | tf_op jit(solution)/shard_map/ppermute | solution.py:566
  85.3 9.5 %collective-permute-start.19 = (f32[512,128]{1,0:T(8,128)S(1)}, f32[512,128]{1,0:T(8,128)S(1)}, u32[]{:S(2)}, u32[]{:S(2)}) collective-permute-start(f32[512,128]{1,0:T(8,128)S(1)} %get-tuple-element.90.refs_10_), channel_id=1, source_target_pairs={{0,64},{1,193},{2,66},{3,195},{4,68},{5,197},{6,70},{7,199},{8,72}... | collective-permute-start | bytes 786440 | tf_op jit(solution)/shard_map/ppermute | solution.py:566
  86.7 13.4 %collective-permute-start.21 = (f32[512,128]{1,0:T(8,128)S(1)}, f32[512,128]{1,0:T(8,128)S(1)}, u32[]{:S(2)}, u32[]{:S(2)}) collective-permute-start(f32[512,128]{1,0:T(8,128)S(1)} %get-tuple-element.93), channel_id=1, source_target_pairs={{0,128},{1,129},{2,130},{3,131},{4,132},{5,133},{6,134},{7,135},{8... | collective-permute-start | bytes 786440 | tf_op jit(solution)/shard_map/ppermute | solution.py:566
  101.5 9.4 %collective-permute-start.22 = (f32[512,128]{1,0:T(8,128)S(1)}, f32[512,128]{1,0:T(8,128)S(1)}, u32[]{:S(2)}, u32[]{:S(2)}) collective-permute-start(f32[512,128]{1,0:T(8,128)S(1)} %get-tuple-element.96), channel_id=1, source_target_pairs={{0,64},{1,193},{2,66},{3,195},{4,68},{5,197},{6,70},{7,199},{8,72}... | collective-permute-start | bytes 786440 | tf_op jit(solution)/shard_map/ppermute | solution.py:566
  102.4 8.6 %collective-permute-start.23 = (f32[512,128]{1,0:T(8,128)S(1)}, f32[512,128]{1,0:T(8,128)S(1)}, u32[]{:S(2)}, u32[]{:S(2)}) collective-permute-start(f32[512,128]{1,0:T(8,128)S(1)} %get-tuple-element.97), channel_id=1, source_target_pairs={{0,192},{1,65},{2,194},{3,67},{4,196},{5,69},{6,198},{7,71},{8,200... | collective-permute-start | bytes 786440 | tf_op jit(solution)/shard_map/ppermute | solution.py:566
  103.9 12.8 %collective-permute-start.24 = (f32[512,128]{1,0:T(8,128)S(1)}, f32[512,128]{1,0:T(8,128)S(1)}, u32[]{:S(2)}, u32[]{:S(2)}) collective-permute-start(f32[512,128]{1,0:T(8,128)S(1)} %get-tuple-element.98), channel_id=1, source_target_pairs={{0,128},{1,129},{2,130},{3,131},{4,132},{5,133},{6,134},{7,135},{8... | collective-permute-start | bytes 786440 | tf_op jit(solution)/shard_map/ppermute | solution.py:566
  117.4 5.9 %collective-permute-start.25 = (f32[4,128,128]{2,1,0:T(8,128)S(1)}, f32[4,128,128]{2,1,0:T(8,128)S(1)}, u32[]{:S(2)}, u32[]{:S(2)}) collective-permute-start(f32[4,128,128]{2,1,0:T(8,128)S(1)} %get-tuple-element.100), channel_id=1, source_target_pairs={{0,1},{1,2},{2,3},{3,0},{4,5},{5,6},{6,7},{7,4},{8,9},{9,10},{10,1... | collective-permute-start | bytes 786440 | tf_op jit(solution)/shard_map/ppermute | solution.py:551
  123.4 5.1 %collective-permute-start.26 = (f32[8,32,128]{2,1,0:T(8,128)S(1)}, f32[8,32,128]{2,1,0:T(8,128)S(1)}, u32[]{:S(2)}, u32[]{:S(2)}) collective-permute-start(f32[8,32,128]{2,1,0:T(8,128)S(1)} %get-tuple-element.102), channel_id=1, source_target_pairs={{0,4},{1,5},{2,6},{3,7},{4,8},{5,9},{6,10},{7,11},{8,12},{9,13},{1... | collective-permute-start | bytes 393224 | tf_op jit(solution)/shard_map/ppermute | solution.py:547
  125.2 5.4 %collective-permute-start.27 = (f32[8,32,128]{2,1,0:T(8,128)S(1)}, f32[8,32,128]{2,1,0:T(8,128)S(1)}, u32[]{:S(2)}, u32[]{:S(2)}) collective-permute-start(f32[8,32,128]{2,1,0:T(8,128)S(1)} %get-tuple-element.103), channel_id=1, source_target_pairs={{0,28},{1,29},{2,30},{3,31},{4,0},{5,1},{6,2},{7,3},{8,4},{9,5},{1... | collective-permute-start | bytes 393224 | tf_op jit(solution)/shard_map/ppermute | solution.py:547
  130.6 8.0 %collective-permute-start.28 = (f32[512,128]{1,0:T(8,128)S(1)}, f32[512,128]{1,0:T(8,128)S(1)}, u32[]{:S(2)}, u32[]{:S(2)}) collective-permute-start(f32[512,128]{1,0:T(8,128)S(1)} %shard_map.71.refs_1_), channel_id=1, source_target_pairs={{0,32},{32,0},{64,96},{96,64},{128,160},{160,128},{192,224},{224,1... | collective-permute-start | bytes 786440 | tf_op jit(solution)/shard_map/ppermute | solution.py:555
  138.6 8.7 %collective-permute-start.31 = (f32[512,128]{1,0:T(8,128)S(1)}, f32[512,128]{1,0:T(8,128)S(1)}, u32[]{:S(2)}, u32[]{:S(2)}) collective-permute-start(f32[512,128]{1,0:T(8,128)S(1)} %shard_map.72.refs_0_), channel_id=1, source_target_pairs={{0,128},{1,129},{2,130},{3,131},{4,132},{5,133},{6,134},{7,135},{8... | collective-permute-start | bytes 786440 | tf_op jit(solution)/shard_map/ppermute | solution.py:566
  140.3 9.7 %collective-permute-start.30 = (f32[512,128]{1,0:T(8,128)S(1)}, f32[512,128]{1,0:T(8,128)S(1)}, u32[]{:S(2)}, u32[]{:S(2)}) collective-permute-start(f32[512,128]{1,0:T(8,128)S(1)} %shard_map.72.refs_0_), channel_id=1, source_target_pairs={{0,192},{1,65},{2,194},{3,67},{4,196},{5,69},{6,198},{7,71},{8,200... | collective-permute-start | bytes 786440 | tf_op jit(solution)/shard_map/ppermute | solution.py:566
  141.7 8.3 %collective-permute-start.29 = (f32[512,128]{1,0:T(8,128)S(1)}, f32[512,128]{1,0:T(8,128)S(1)}, u32[]{:S(2)}, u32[]{:S(2)}) collective-permute-start(f32[512,128]{1,0:T(8,128)S(1)} %shard_map.72.refs_0_), channel_id=1, source_target_pairs={{0,64},{1,193},{2,66},{3,195},{4,68},{5,197},{6,70},{7,199},{8,72}... | collective-permute-start | bytes 786440 | tf_op jit(solution)/shard_map/ppermute | solution.py:566
  (5 other events, 22.4 us)

commit v5 on v4

--- a/solution.py
+++ b/solution.py
@@ -597,7 +597,8 @@
             got = send_rows(top, bottom)
             packs = along_cols(call(shard_cols_kernel, [PACK], new, *got), -1)
             one, three = spread((1, 2), new, got, packs, [*near[:3], *near[:3]])
-            two, own = spread((0, 0), new, got, packs, [*far[:3], *near[:3]], after=(one,))
+            two = spread((0,), new, got, packs, far[:3], after=(one,))
+            own = spread((0,), new, got, packs, near[:3], after=(two,))
             own, one, three, two = trade(own, one, three, two)
             mark = call(touch_kernel, [sds(8, BY)], before=(one, three))
             parts = call(ratio_kernel, [SHARD] * 4, one, three, two, own, kzf, kzb, obs,

time: 152 us -> 152 us (level)
    pallas_call x28 -> x29, Pallas kernels: 15.6 us -> 16 us  [call(): pl.pallas_call(inner, out_shape=out_shape, in_specs=specs, out_specs=[pl....]
where the time goes in v5:
time: 152 us; the launch traced here: 151 us
  waiting for transfers between devices  92 us (61%)
  starting transfers between devices  40.4 us (27%)
  Pallas kernels  16 us (11%)
  local copies, waits for them, and re-layouts  2.27 us (1%)
    ppermute x12, waiting for transfers between devices, swap(): return lax.ppermute(x, ('view', 'blk'), pairs)  37.6 us
    ppermute x12, waiting for transfers between devices, along_rows(): return lax.ppermute(x, 'blk', [(i, (i + 4 * by) % 32) for i in range(32)])  25.5 us
    ppermute x6, waiting for transfers between devices, along_cols(): lax.ppermute(x, 'blk', [(i, i // 4 * 4 + (i + by) % 4) for i in range(32)])  18.8 us
    ppermute x12, starting transfers between devices, swap(): return lax.ppermute(x, ('view', 'blk'), pairs)  17.2 us
    pallas_call x29, Pallas kernels, call(): pl.pallas_call(inner, out_shape=out_shape, in_specs=specs, out_specs=[pl....  16 us
    ppermute x12, starting transfers between devices, along_rows(): return lax.ppermute(x, 'blk', [(i, (i + 4 * by) % 32) for i in range(32)])  14.5 us
    ppermute x2, waiting for transfers between devices, view_swap(): return lax.ppermute(x, 'view', [(i, i ^ mask) for i in range(8)])  10.1 us
    ppermute x2, starting transfers between devices, view_swap(): return lax.ppermute(x, 'view', [(i, i ^ mask) for i in range(8)])  6.37 us
  transfers between devices with their start and end apart: 32, of which 25 were waited for; matrix products, arithmetic and copies ran while one was open for 0% of the time, Pallas kernels for 5%

profile of v5, /device:TPU:32, one launch (start us, length us, event | category | flops | bytes accessed | tf_op | source)
XLA Modules:
  0.0 150.9 jit_solution(5738688405472414055)
XLA Ops:
  3.8 1.9 %collective-permute-start.1 = (f32[16,32,128]{2,1,0:T(8,128)S(1)}, f32[16,32,128]{2,1,0:T(8,128)S(1)}, u32[]{:S(2)}, u32[]{:S(2)}) collective-permute-start(f32[16,32,128]{2,1,0:T(8,128)S(1)} %get-tuple-element.55), channel_id=1, source_target_pairs={{0,4},{1,5},{2,6},{3,7},{4,8},{5,9},{6,10},{7,11},{8,12},{9,13},{1... | collective-permute-start | bytes 786440 | tf_op jit(solution)/shard_map/ppermute | solution.py:547
  7.2 3.3 %collective-permute-done.refs_2_ = f32[16,64,128]{2,1,0:T(8,128)S(1)} collective-permute-done((f32[16,64,128]{2,1,0:T(8,128)S(1)}, f32[16,64,128]{2,1,0:T(8,128)S(1)}, u32[]{:S(2)}, u32[]{:S(2)}) %collective-permute-start) | collective-permute-done | bytes 524320 | tf_op jit(solution)/shard_map/ppermute | solution.py:551
  14.5 3.3 %collective-permute-start.4 = (f32[32,16,128]{2,1,0:T(8,128)S(1)}, f32[32,16,128]{2,1,0:T(8,128)S(1)}, u32[]{:S(2)}, u32[]{:S(2)}) collective-permute-start(f32[32,16,128]{2,1,0:T(8,128)S(1)} %get-tuple-element.61), channel_id=1, source_target_pairs={{0,4},{1,5},{2,6},{3,7},{4,8},{5,9},{6,10},{7,11},{8,12},{9,13},{1... | collective-permute-start | bytes 786440 | tf_op jit(solution)/shard_map/ppermute | solution.py:547
  18.3 2.7 %collective-permute-start.7 = (f32[16,32,128]{2,1,0:T(8,128)S(1)}, f32[16,32,128]{2,1,0:T(8,128)S(1)}, u32[]{:S(2)}, u32[]{:S(2)}) collective-permute-start(f32[16,32,128]{2,1,0:T(8,128)S(1)} %get-tuple-element.64), channel_id=1, source_target_pairs={{0,4},{1,5},{2,6},{3,7},{4,8},{5,9},{6,10},{7,11},{8,12},{9,13},{1... | collective-permute-start | bytes 786440 | tf_op jit(solution)/shard_map/ppermute | solution.py:547
  21.2 3.3 %collective-permute-done.4.refs_3_ = f32[32,16,128]{2,1,0:T(8,128)S(1)} collective-permute-done((f32[32,16,128]{2,1,0:T(8,128)S(1)}, f32[32,16,128]{2,1,0:T(8,128)S(1)}, u32[]{:S(2)}, u32[]{:S(2)}) %collective-permute-start.4) | collective-permute-done | bytes 262176 | tf_op jit(solution)/shard_map/ppermute | solution.py:547
  24.5 3.0 %collective-permute-done.5.refs_4_ = f32[32,16,128]{2,1,0:T(8,128)S(1)} collective-permute-done((f32[32,16,128]{2,1,0:T(8,128)S(1)}, f32[32,16,128]{2,1,0:T(8,128)S(1)}, u32[]{:S(2)}, u32[]{:S(2)}) %collective-permute-start.5) | collective-permute-done | bytes 262176 | tf_op jit(solution)/shard_map/ppermute | solution.py:547
  29.0 3.2 %collective-permute-done.8.refs_3_ = f32[16,32,128]{2,1,0:T(8,128)S(1)} collective-permute-done((f32[16,32,128]{2,1,0:T(8,128)S(1)}, f32[16,32,128]{2,1,0:T(8,128)S(1)}, u32[]{:S(2)}, u32[]{:S(2)}) %collective-permute-start.8) | collective-permute-done | bytes 262176 | tf_op jit(solution)/shard_map/ppermute | solution.py:547
  35.4 2.1 %collective-permute-start.10 = (f32[520,128]{1,0:T(8,128)S(1)}, f32[520,128]{1,0:T(8,128)S(1)}, u32[]{:S(2)}, u32[]{:S(2)}) collective-permute-start(f32[520,128]{1,0:T(8,128)S(1)} %get-tuple-element.71), channel_id=1, source_target_pairs={{0,192},{1,65},{2,194},{3,67},{4,196},{5,69},{6,198},{7,71},{8,200... | collective-permute-start | bytes 798728 | tf_op jit(solution)/shard_map/ppermute | solution.py:566
  38.1 4.4 %collective-permute-done.9.refs_1_.refs_4_ = f32[520,128]{1,0:T(8,128)S(1)} collective-permute-done((f32[520,128]{1,0:T(8,128)S(1)}, f32[520,128]{1,0:T(8,128)S(1)}, u32[]{:S(2)}, u32[]{:S(2)}) %collective-permute-start.9) | collective-permute-done | bytes 266272 | tf_op jit(solution)/shard_map/ppermute | solution.py:566
  45.3 4.1 %collective-permute-done.11.refs_1_.refs_6_ = f32[520,128]{1,0:T(8,128)S(1)} collective-permute-done((f32[520,128]{1,0:T(8,128)S(1)}, f32[520,128]{1,0:T(8,128)S(1)}, u32[]{:S(2)}, u32[]{:S(2)}) %collective-permute-start.11) | collective-permute-done | bytes 266272 | tf_op jit(solution)/shard_map/ppermute | solution.py:566
  50.5 5.8 %collective-permute-done.12.refs_1_ = f32[4,128,128]{2,1,0:T(8,128)S(1)} collective-permute-done((f32[4,128,128]{2,1,0:T(8,128)S(1)}, f32[4,128,128]{2,1,0:T(8,128)S(1)}, u32[]{:S(2)}, u32[]{:S(2)}) %collective-permute-start.12) | collective-permute-done | bytes 262176 | tf_op jit(solution)/shard_map/ppermute | solution.py:551
  58.5 3.1 %collective-permute-done.13.refs_1_ = f32[8,32,128]{2,1,0:T(8,128)S(1)} collective-permute-done((f32[8,32,128]{2,1,0:T(8,128)S(1)}, f32[8,32,128]{2,1,0:T(8,128)S(1)}, u32[]{:S(2)}, u32[]{:S(2)}) %collective-permute-start.13) | collective-permute-done | bytes 131104 | tf_op jit(solution)/shard_map/ppermute | solution.py:547
  63.2 3.5 %collective-permute-start.15 = (f32[544,128]{1,0:T(8,128)S(1)}, f32[544,128]{1,0:T(8,128)S(1)}, u32[]{:S(2)}, u32[]{:S(2)}) collective-permute-start(f32[544,128]{1,0:T(8,128)S(1)} %shard_map.61.refs_1_), channel_id=1, source_target_pairs={{0,32},{32,0},{64,96},{96,64},{128,160},{160,128},{192,224},{224,1... | collective-permute-start | bytes 835592 | tf_op jit(solution)/shard_map/ppermute | solution.py:555
  66.7 5.0 %collective-permute-done.15.refs_2_ = f32[544,128]{1,0:T(8,128)S(1)} collective-permute-done((f32[544,128]{1,0:T(8,128)S(1)}, f32[544,128]{1,0:T(8,128)S(1)}, u32[]{:S(2)}, u32[]{:S(2)}) %collective-permute-start.15) | collective-permute-done | bytes 278560 | tf_op jit(solution)/shard_map/ppermute | solution.py:555
  72.2 1.8 %collective-permute-start.16 = (f32[8,32,128]{2,1,0:T(8,128)S(1)}, f32[8,32,128]{2,1,0:T(8,128)S(1)}, u32[]{:S(2)}, u32[]{:S(2)}) collective-permute-start(f32[8,32,128]{2,1,0:T(8,128)S(1)} %get-tuple-element.85), channel_id=1, source_target_pairs={{0,4},{1,5},{2,6},{3,7},{4,8},{5,9},{6,10},{7,11},{8,12},{9,13},{1... | collective-permute-start | bytes 393224 | tf_op jit(solution)/shard_map/ppermute | solution.py:547
  74.3 2.9 %collective-permute-done.16.refs_1_ = f32[8,32,128]{2,1,0:T(8,128)S(1)} collective-permute-done((f32[8,32,128]{2,1,0:T(8,128)S(1)}, f32[8,32,128]{2,1,0:T(8,128)S(1)}, u32[]{:S(2)}, u32[]{:S(2)}) %collective-permute-start.16) | collective-permute-done | bytes 131104 | tf_op jit(solution)/shard_map/ppermute | solution.py:547
  77.3 1.7 %collective-permute-done.17.refs_2_ = f32[8,32,128]{2,1,0:T(8,128)S(1)} collective-permute-done((f32[8,32,128]{2,1,0:T(8,128)S(1)}, f32[8,32,128]{2,1,0:T(8,128)S(1)}, u32[]{:S(2)}, u32[]{:S(2)}) %collective-permute-start.17) | collective-permute-done | bytes 131104 | tf_op jit(solution)/shard_map/ppermute | solution.py:547
  79.2 3.9 %collective-permute-done.18.refs_3_ = f32[4,128,128]{2,1,0:T(8,128)S(1)} collective-permute-done((f32[4,128,128]{2,1,0:T(8,128)S(1)}, f32[4,128,128]{2,1,0:T(8,128)S(1)}, u32[]{:S(2)}, u32[]{:S(2)}) %collective-permute-start.18) | collective-permute-done | bytes 262176 | tf_op jit(solution)/shard_map/ppermute | solution.py:551
  86.4 3.3 %collective-permute-start.21 = (f32[512,128]{1,0:T(8,128)S(1)}, f32[512,128]{1,0:T(8,128)S(1)}, u32[]{:S(2)}, u32[]{:S(2)}) collective-permute-start(f32[512,128]{1,0:T(8,128)S(1)} %shard_map.66.refs_7_), channel_id=1, source_target_pairs={{0,128},{1,129},{2,130},{3,131},{4,132},{5,133},{6,134},{7,135},{8... | collective-permute-start | bytes 786440 | tf_op jit(solution)/shard_map/ppermute | solution.py:566
  90.3 4.5 %collective-permute-done.20.refs_1_.refs_2_ = f32[512,128]{1,0:T(8,128)S(1)} collective-permute-done((f32[512,128]{1,0:T(8,128)S(1)}, f32[512,128]{1,0:T(8,128)S(1)}, u32[]{:S(2)}, u32[]{:S(2)}) %collective-permute-start.20) | collective-permute-done | bytes 262176 | tf_op jit(solution)/shard_map/ppermute | solution.py:566
  94.8 5.3 %collective-permute-done.21.refs_3_ = f32[512,128]{1,0:T(8,128)S(1)} collective-permute-done((f32[512,128]{1,0:T(8,128)S(1)}, f32[512,128]{1,0:T(8,128)S(1)}, u32[]{:S(2)}, u32[]{:S(2)}) %collective-permute-start.21) | collective-permute-done | bytes 262176 | tf_op jit(solution)/shard_map/ppermute | solution.py:566
  103.7 2.0 %collective-permute-start.24 = (f32[512,128]{1,0:T(8,128)S(1)}, f32[512,128]{1,0:T(8,128)S(1)}, u32[]{:S(2)}, u32[]{:S(2)}) collective-permute-start(f32[512,128]{1,0:T(8,128)S(1)} %get-tuple-element.94), channel_id=1, source_target_pairs={{0,128},{1,129},{2,130},{3,131},{4,132},{5,133},{6,134},{7,135},{8... | collective-permute-start | bytes 786440 | tf_op jit(solution)/shard_map/ppermute | solution.py:566
  105.7 5.0 %collective-permute-done.22.refs_1_ = f32[512,128]{1,0:T(8,128)S(1)} collective-permute-done((f32[512,128]{1,0:T(8,128)S(1)}, f32[512,128]{1,0:T(8,128)S(1)}, u32[]{:S(2)}, u32[]{:S(2)}) %collective-permute-start.22) | collective-permute-done | bytes 262176 | tf_op jit(solution)/shard_map/ppermute | solution.py:566
  111.5 5.0 %collective-permute-done.24.refs_1_ = f32[512,128]{1,0:T(8,128)S(1)} collective-permute-done((f32[512,128]{1,0:T(8,128)S(1)}, f32[512,128]{1,0:T(8,128)S(1)}, u32[]{:S(2)}, u32[]{:S(2)}) %collective-permute-start.24) | collective-permute-done | bytes 262176 | tf_op jit(solution)/shard_map/ppermute | solution.py:566
  117.3 5.8 %collective-permute-done.25.refs_1_ = f32[4,128,128]{2,1,0:T(8,128)S(1)} collective-permute-done((f32[4,128,128]{2,1,0:T(8,128)S(1)}, f32[4,128,128]{2,1,0:T(8,128)S(1)}, u32[]{:S(2)}, u32[]{:S(2)}) %collective-permute-start.25) | collective-permute-done | bytes 262176 | tf_op jit(solution)/shard_map/ppermute | solution.py:551
  123.2 1.8 %collective-permute-start.26 = (f32[8,32,128]{2,1,0:T(8,128)S(1)}, f32[8,32,128]{2,1,0:T(8,128)S(1)}, u32[]{:S(2)}, u32[]{:S(2)}) collective-permute-start(f32[8,32,128]{2,1,0:T(8,128)S(1)} %get-tuple-element.98), channel_id=1, source_target_pairs={{0,4},{1,5},{2,6},{3,7},{4,8},{5,9},{6,10},{7,11},{8,12},{9,13},{1... | collective-permute-start | bytes 393224 | tf_op jit(solution)/shard_map/ppermute | solution.py:547
  125.3 3.0 %collective-permute-done.26.refs_1_ = f32[8,32,128]{2,1,0:T(8,128)S(1)} collective-permute-done((f32[8,32,128]{2,1,0:T(8,128)S(1)}, f32[8,32,128]{2,1,0:T(8,128)S(1)}, u32[]{:S(2)}, u32[]{:S(2)}) %collective-permute-start.26) | collective-permute-done | bytes 131104 | tf_op jit(solution)/shard_map/ppermute | solution.py:547
  128.2 2.1 %collective-permute-done.27.refs_2_ = f32[8,32,128]{2,1,0:T(8,128)S(1)} collective-permute-done((f32[8,32,128]{2,1,0:T(8,128)S(1)}, f32[8,32,128]{2,1,0:T(8,128)S(1)}, u32[]{:S(2)}, u32[]{:S(2)}) %collective-permute-start.27) | collective-permute-done | bytes 131104 | tf_op jit(solution)/shard_map/ppermute | solution.py:547
  130.4 2.9 %collective-permute-start.28 = (f32[512,128]{1,0:T(8,128)S(1)}, f32[512,128]{1,0:T(8,128)S(1)}, u32[]{:S(2)}, u32[]{:S(2)}) collective-permute-start(f32[512,128]{1,0:T(8,128)S(1)} %shard_map.72.refs_1_), channel_id=1, source_target_pairs={{0,32},{32,0},{64,96},{96,64},{128,160},{160,128},{192,224},{224,1... | collective-permute-start | bytes 786440 | tf_op jit(solution)/shard_map/ppermute | solution.py:555
  133.3 5.1 %collective-permute-done.28.refs_2_ = f32[512,128]{1,0:T(8,128)S(1)} collective-permute-done((f32[512,128]{1,0:T(8,128)S(1)}, f32[512,128]{1,0:T(8,128)S(1)}, u32[]{:S(2)}, u32[]{:S(2)}) %collective-permute-start.28) | collective-permute-done | bytes 262176 | tf_op jit(solution)/shard_map/ppermute | solution.py:555
  142.0 5.1 %collective-permute-done.31.refs_3_ = f32[512,128]{1,0:T(8,128)S(1)} collective-permute-done((f32[512,128]{1,0:T(8,128)S(1)}, f32[512,128]{1,0:T(8,128)S(1)}, u32[]{:S(2)}, u32[]{:S(2)}) %collective-permute-start.31) | collective-permute-done | bytes 262176 | tf_op jit(solution)/shard_map/ppermute | solution.py:566
  147.1 2.7 %collective-permute-done.30.refs_2_ = f32[512,128]{1,0:T(8,128)S(1)} collective-permute-done((f32[512,128]{1,0:T(8,128)S(1)}, f32[512,128]{1,0:T(8,128)S(1)}, u32[]{:S(2)}, u32[]{:S(2)}) %collective-permute-start.30) | collective-permute-done | bytes 262176 | tf_op jit(solution)/shard_map/ppermute | solution.py:566
  (72 shorter events, 38.1 us)
Async XLA Ops:
  2.7 7.8 %collective-permute-start = (f32[16,64,128]{2,1,0:T(8,128)S(1)}, f32[16,64,128]{2,1,0:T(8,128)S(1)}, u32[]{:S(2)}, u32[]{:S(2)}) collective-permute-start(f32[16,64,128]{2,1,0:T(8,128)S(1)} %shard_map.48), channel_id=1, source_target_pairs={{0,3},{1,0},{2,1},{3,2},{4,7},{5,4},{6,5},{7,6},{8,11},{9,8},{10,9... | collective-permute-start | bytes 1572872 | tf_op jit(solution)/shard_map/ppermute | solution.py:551
  3.8 7.8 %collective-permute-start.1 = (f32[16,32,128]{2,1,0:T(8,128)S(1)}, f32[16,32,128]{2,1,0:T(8,128)S(1)}, u32[]{:S(2)}, u32[]{:S(2)}) collective-permute-start(f32[16,32,128]{2,1,0:T(8,128)S(1)} %get-tuple-element.55), channel_id=1, source_target_pairs={{0,4},{1,5},{2,6},{3,7},{4,8},{5,9},{6,10},{7,11},{8,12},{9,13},{1... | collective-permute-start | bytes 786440 | tf_op jit(solution)/shard_map/ppermute | solution.py:547
  5.7 7.6 %collective-permute-start.2 = (f32[16,32,128]{2,1,0:T(8,128)S(1)}, f32[16,32,128]{2,1,0:T(8,128)S(1)}, u32[]{:S(2)}, u32[]{:S(2)}) collective-permute-start(f32[16,32,128]{2,1,0:T(8,128)S(1)} %get-tuple-element.53.refs_0_), channel_id=1, source_target_pairs={{0,28},{1,29},{2,30},{3,31},{4,0},{5,1},{6,2},{7,3},{8,4},{9,5},{1... | collective-permute-start | bytes 786440 | tf_op jit(solution)/shard_map/ppermute | solution.py:547
  5.8 11.9 %collective-permute-start.3 = (f32[8,64,128]{2,1,0:T(8,128)S(1)}, f32[8,64,128]{2,1,0:T(8,128)S(1)}, u32[]{:S(2)}, u32[]{:S(2)}) collective-permute-start(f32[8,64,128]{2,1,0:T(8,128)S(1)} %shard_map.46.refs_0_), channel_id=1, source_target_pairs={{0,3},{1,0},{2,1},{3,2},{4,7},{5,4},{6,5},{7,6},{8,11},{9,8},{10,9... | collective-permute-start | bytes 786440 | tf_op jit(solution)/shard_map/ppermute | solution.py:551
  13.7 14.7 %collective-permute-start.6 = (f32[8,64,128]{2,1,0:T(8,128)S(1)}, f32[8,64,128]{2,1,0:T(8,128)S(1)}, u32[]{:S(2)}, u32[]{:S(2)}) collective-permute-start(f32[8,64,128]{2,1,0:T(8,128)S(1)} %get-tuple-element.63), channel_id=1, source_target_pairs={{0,3},{1,0},{2,1},{3,2},{4,7},{5,4},{6,5},{7,6},{8,11},{9,8},{10,9... | collective-permute-start | bytes 786440 | tf_op jit(solution)/shard_map/ppermute | solution.py:551
  14.5 10.0 %collective-permute-start.4 = (f32[32,16,128]{2,1,0:T(8,128)S(1)}, f32[32,16,128]{2,1,0:T(8,128)S(1)}, u32[]{:S(2)}, u32[]{:S(2)}) collective-permute-start(f32[32,16,128]{2,1,0:T(8,128)S(1)} %get-tuple-element.61), channel_id=1, source_target_pairs={{0,4},{1,5},{2,6},{3,7},{4,8},{5,9},{6,10},{7,11},{8,12},{9,13},{1... | collective-permute-start | bytes 786440 | tf_op jit(solution)/shard_map/ppermute | solution.py:547
  17.7 9.8 %collective-permute-start.5 = (f32[32,16,128]{2,1,0:T(8,128)S(1)}, f32[32,16,128]{2,1,0:T(8,128)S(1)}, u32[]{:S(2)}, u32[]{:S(2)}) collective-permute-start(f32[32,16,128]{2,1,0:T(8,128)S(1)} %get-tuple-element.62), channel_id=1, source_target_pairs={{0,28},{1,29},{2,30},{3,31},{4,0},{5,1},{6,2},{7,3},{8,4},{9,5},{1... | collective-permute-start | bytes 786440 | tf_op jit(solution)/shard_map/ppermute | solution.py:547
  18.3 10.7 %collective-permute-start.7 = (f32[16,32,128]{2,1,0:T(8,128)S(1)}, f32[16,32,128]{2,1,0:T(8,128)S(1)}, u32[]{:S(2)}, u32[]{:S(2)}) collective-permute-start(f32[16,32,128]{2,1,0:T(8,128)S(1)} %get-tuple-element.64), channel_id=1, source_target_pairs={{0,4},{1,5},{2,6},{3,7},{4,8},{5,9},{6,10},{7,11},{8,12},{9,13},{1... | collective-permute-start | bytes 786440 | tf_op jit(solution)/shard_map/ppermute | solution.py:547
  21.0 11.1 %collective-permute-start.8 = (f32[16,32,128]{2,1,0:T(8,128)S(1)}, f32[16,32,128]{2,1,0:T(8,128)S(1)}, u32[]{:S(2)}, u32[]{:S(2)}) collective-permute-start(f32[16,32,128]{2,1,0:T(8,128)S(1)} %get-tuple-element.65), channel_id=1, source_target_pairs={{0,28},{1,29},{2,30},{3,31},{4,0},{5,1},{6,2},{7,3},{8,4},{9,5},{1... | collective-permute-start | bytes 786440 | tf_op jit(solution)/shard_map/ppermute | solution.py:547
  33.8 8.8 %collective-permute-start.9 = (f32[520,128]{1,0:T(8,128)S(1)}, f32[520,128]{1,0:T(8,128)S(1)}, u32[]{:S(2)}, u32[]{:S(2)}) collective-permute-start(f32[520,128]{1,0:T(8,128)S(1)} %get-tuple-element.70), channel_id=1, source_target_pairs={{0,64},{1,193},{2,66},{3,195},{4,68},{5,197},{6,70},{7,199},{8,72}... | collective-permute-start | bytes 798728 | tf_op jit(solution)/shard_map/ppermute | solution.py:566
  35.4 8.6 %collective-permute-start.10 = (f32[520,128]{1,0:T(8,128)S(1)}, f32[520,128]{1,0:T(8,128)S(1)}, u32[]{:S(2)}, u32[]{:S(2)}) collective-permute-start(f32[520,128]{1,0:T(8,128)S(1)} %get-tuple-element.71), channel_id=1, source_target_pairs={{0,192},{1,65},{2,194},{3,67},{4,196},{5,69},{6,198},{7,71},{8,200... | collective-permute-start | bytes 798728 | tf_op jit(solution)/shard_map/ppermute | solution.py:566
  37.5 12.0 %collective-permute-start.11 = (f32[520,128]{1,0:T(8,128)S(1)}, f32[520,128]{1,0:T(8,128)S(1)}, u32[]{:S(2)}, u32[]{:S(2)}) collective-permute-start(f32[520,128]{1,0:T(8,128)S(1)} %get-tuple-element.74), channel_id=1, source_target_pairs={{0,128},{1,129},{2,130},{3,131},{4,132},{5,133},{6,134},{7,135},{8... | collective-permute-start | bytes 798728 | tf_op jit(solution)/shard_map/ppermute | solution.py:566
  50.4 5.9 %collective-permute-start.12 = (f32[4,128,128]{2,1,0:T(8,128)S(1)}, f32[4,128,128]{2,1,0:T(8,128)S(1)}, u32[]{:S(2)}, u32[]{:S(2)}) collective-permute-start(f32[4,128,128]{2,1,0:T(8,128)S(1)} %get-tuple-element.80), channel_id=1, source_target_pairs={{0,1},{1,2},{2,3},{3,0},{4,5},{5,6},{6,7},{7,4},{8,9},{9,10},{10,1... | collective-permute-start | bytes 786440 | tf_op jit(solution)/shard_map/ppermute | solution.py:551
  56.4 5.2 %collective-permute-start.13 = (f32[8,32,128]{2,1,0:T(8,128)S(1)}, f32[8,32,128]{2,1,0:T(8,128)S(1)}, u32[]{:S(2)}, u32[]{:S(2)}) collective-permute-start(f32[8,32,128]{2,1,0:T(8,128)S(1)} %get-tuple-element.82), channel_id=1, source_target_pairs={{0,4},{1,5},{2,6},{3,7},{4,8},{5,9},{6,10},{7,11},{8,12},{9,13},{1... | collective-permute-start | bytes 393224 | tf_op jit(solution)/shard_map/ppermute | solution.py:547
  57.9 5.3 %collective-permute-start.14 = (f32[8,32,128]{2,1,0:T(8,128)S(1)}, f32[8,32,128]{2,1,0:T(8,128)S(1)}, u32[]{:S(2)}, u32[]{:S(2)}) collective-permute-start(f32[8,32,128]{2,1,0:T(8,128)S(1)} %get-tuple-element.83), channel_id=1, source_target_pairs={{0,28},{1,29},{2,30},{3,31},{4,0},{5,1},{6,2},{7,3},{8,4},{9,5},{1... | collective-permute-start | bytes 393224 | tf_op jit(solution)/shard_map/ppermute | solution.py:547
  63.2 8.5 %collective-permute-start.15 = (f32[544,128]{1,0:T(8,128)S(1)}, f32[544,128]{1,0:T(8,128)S(1)}, u32[]{:S(2)}, u32[]{:S(2)}) collective-permute-start(f32[544,128]{1,0:T(8,128)S(1)} %shard_map.61.refs_1_), channel_id=1, source_target_pairs={{0,32},{32,0},{64,96},{96,64},{128,160},{160,128},{192,224},{224,1... | collective-permute-start | bytes 835592 | tf_op jit(solution)/shard_map/ppermute | solution.py:555
  72.2 5.0 %collective-permute-start.16 = (f32[8,32,128]{2,1,0:T(8,128)S(1)}, f32[8,32,128]{2,1,0:T(8,128)S(1)}, u32[]{:S(2)}, u32[]{:S(2)}) collective-permute-start(f32[8,32,128]{2,1,0:T(8,128)S(1)} %get-tuple-element.85), channel_id=1, source_target_pairs={{0,4},{1,5},{2,6},{3,7},{4,8},{5,9},{6,10},{7,11},{8,12},{9,13},{1... | collective-permute-start | bytes 393224 | tf_op jit(solution)/shard_map/ppermute | solution.py:547
  74.0 5.0 %collective-permute-start.17 = (f32[8,32,128]{2,1,0:T(8,128)S(1)}, f32[8,32,128]{2,1,0:T(8,128)S(1)}, u32[]{:S(2)}, u32[]{:S(2)}) collective-permute-start(f32[8,32,128]{2,1,0:T(8,128)S(1)} %get-tuple-element.86), channel_id=1, source_target_pairs={{0,28},{1,29},{2,30},{3,31},{4,0},{5,1},{6,2},{7,3},{8,4},{9,5},{1... | collective-permute-start | bytes 393224 | tf_op jit(solution)/shard_map/ppermute | solution.py:547
  79.1 4.0 %collective-permute-start.18 = (f32[4,128,128]{2,1,0:T(8,128)S(1)}, f32[4,128,128]{2,1,0:T(8,128)S(1)}, u32[]{:S(2)}, u32[]{:S(2)}) collective-permute-start(f32[4,128,128]{2,1,0:T(8,128)S(1)} %shard_map.63), channel_id=1, source_target_pairs={{0,3},{1,0},{2,1},{3,2},{4,7},{5,4},{6,5},{7,6},{8,11},{9,8},{10,9... | collective-permute-start | bytes 786440 | tf_op jit(solution)/shard_map/ppermute | solution.py:551
  84.0 10.8 %collective-permute-start.20 = (f32[512,128]{1,0:T(8,128)S(1)}, f32[512,128]{1,0:T(8,128)S(1)}, u32[]{:S(2)}, u32[]{:S(2)}) collective-permute-start(f32[512,128]{1,0:T(8,128)S(1)} %get-tuple-element.89), channel_id=1, source_target_pairs={{0,192},{1,65},{2,194},{3,67},{4,196},{5,69},{6,198},{7,71},{8,200... | collective-permute-start | bytes 786440 | tf_op jit(solution)/shard_map/ppermute | solution.py:566
  85.3 9.5 %collective-permute-start.19 = (f32[512,128]{1,0:T(8,128)S(1)}, f32[512,128]{1,0:T(8,128)S(1)}, u32[]{:S(2)}, u32[]{:S(2)}) collective-permute-start(f32[512,128]{1,0:T(8,128)S(1)} %get-tuple-element.88.refs_7_), channel_id=1, source_target_pairs={{0,64},{1,193},{2,66},{3,195},{4,68},{5,197},{6,70},{7,199},{8,72}... | collective-permute-start | bytes 786440 | tf_op jit(solution)/shard_map/ppermute | solution.py:566
  86.4 13.7 %collective-permute-start.21 = (f32[512,128]{1,0:T(8,128)S(1)}, f32[512,128]{1,0:T(8,128)S(1)}, u32[]{:S(2)}, u32[]{:S(2)}) collective-permute-start(f32[512,128]{1,0:T(8,128)S(1)} %shard_map.66.refs_7_), channel_id=1, source_target_pairs={{0,128},{1,129},{2,130},{3,131},{4,132},{5,133},{6,134},{7,135},{8... | collective-permute-start | bytes 786440 | tf_op jit(solution)/shard_map/ppermute | solution.py:566
  101.5 9.2 %collective-permute-start.22 = (f32[512,128]{1,0:T(8,128)S(1)}, f32[512,128]{1,0:T(8,128)S(1)}, u32[]{:S(2)}, u32[]{:S(2)}) collective-permute-start(f32[512,128]{1,0:T(8,128)S(1)} %get-tuple-element.92), channel_id=1, source_target_pairs={{0,64},{1,193},{2,66},{3,195},{4,68},{5,197},{6,70},{7,199},{8,72}... | collective-permute-start | bytes 786440 | tf_op jit(solution)/shard_map/ppermute | solution.py:566
  102.2 8.5 %collective-permute-start.23 = (f32[512,128]{1,0:T(8,128)S(1)}, f32[512,128]{1,0:T(8,128)S(1)}, u32[]{:S(2)}, u32[]{:S(2)}) collective-permute-start(f32[512,128]{1,0:T(8,128)S(1)} %get-tuple-element.93), channel_id=1, source_target_pairs={{0,192},{1,65},{2,194},{3,67},{4,196},{5,69},{6,198},{7,71},{8,200... | collective-permute-start | bytes 786440 | tf_op jit(solution)/shard_map/ppermute | solution.py:566
  103.7 12.8 %collective-permute-start.24 = (f32[512,128]{1,0:T(8,128)S(1)}, f32[512,128]{1,0:T(8,128)S(1)}, u32[]{:S(2)}, u32[]{:S(2)}) collective-permute-start(f32[512,128]{1,0:T(8,128)S(1)} %get-tuple-element.94), channel_id=1, source_target_pairs={{0,128},{1,129},{2,130},{3,131},{4,132},{5,133},{6,134},{7,135},{8... | collective-permute-start | bytes 786440 | tf_op jit(solution)/shard_map/ppermute | solution.py:566
  117.2 5.9 %collective-permute-start.25 = (f32[4,128,128]{2,1,0:T(8,128)S(1)}, f32[4,128,128]{2,1,0:T(8,128)S(1)}, u32[]{:S(2)}, u32[]{:S(2)}) collective-permute-start(f32[4,128,128]{2,1,0:T(8,128)S(1)} %get-tuple-element.96), channel_id=1, source_target_pairs={{0,1},{1,2},{2,3},{3,0},{4,5},{5,6},{6,7},{7,4},{8,9},{9,10},{10,1... | collective-permute-start | bytes 786440 | tf_op jit(solution)/shard_map/ppermute | solution.py:551
  123.2 5.1 %collective-permute-start.26 = (f32[8,32,128]{2,1,0:T(8,128)S(1)}, f32[8,32,128]{2,1,0:T(8,128)S(1)}, u32[]{:S(2)}, u32[]{:S(2)}) collective-permute-start(f32[8,32,128]{2,1,0:T(8,128)S(1)} %get-tuple-element.98), channel_id=1, source_target_pairs={{0,4},{1,5},{2,6},{3,7},{4,8},{5,9},{6,10},{7,11},{8,12},{9,13},{1... | collective-permute-start | bytes 393224 | tf_op jit(solution)/shard_map/ppermute | solution.py:547
  125.0 5.4 %collective-permute-start.27 = (f32[8,32,128]{2,1,0:T(8,128)S(1)}, f32[8,32,128]{2,1,0:T(8,128)S(1)}, u32[]{:S(2)}, u32[]{:S(2)}) collective-permute-start(f32[8,32,128]{2,1,0:T(8,128)S(1)} %get-tuple-element.99), channel_id=1, source_target_pairs={{0,28},{1,29},{2,30},{3,31},{4,0},{5,1},{6,2},{7,3},{8,4},{9,5},{1... | collective-permute-start | bytes 393224 | tf_op jit(solution)/shard_map/ppermute | solution.py:547
  130.4 8.0 %collective-permute-start.28 = (f32[512,128]{1,0:T(8,128)S(1)}, f32[512,128]{1,0:T(8,128)S(1)}, u32[]{:S(2)}, u32[]{:S(2)}) collective-permute-start(f32[512,128]{1,0:T(8,128)S(1)} %shard_map.72.refs_1_), channel_id=1, source_target_pairs={{0,32},{32,0},{64,96},{96,64},{128,160},{160,128},{192,224},{224,1... | collective-permute-start | bytes 786440 | tf_op jit(solution)/shard_map/ppermute | solution.py:555
  138.4 8.7 %collective-permute-start.31 = (f32[512,128]{1,0:T(8,128)S(1)}, f32[512,128]{1,0:T(8,128)S(1)}, u32[]{:S(2)}, u32[]{:S(2)}) collective-permute-start(f32[512,128]{1,0:T(8,128)S(1)} %shard_map.73.refs_0_), channel_id=1, source_target_pairs={{0,128},{1,129},{2,130},{3,131},{4,132},{5,133},{6,134},{7,135},{8... | collective-permute-start | bytes 786440 | tf_op jit(solution)/shard_map/ppermute | solution.py:566
  140.0 9.8 %collective-permute-start.30 = (f32[512,128]{1,0:T(8,128)S(1)}, f32[512,128]{1,0:T(8,128)S(1)}, u32[]{:S(2)}, u32[]{:S(2)}) collective-permute-start(f32[512,128]{1,0:T(8,128)S(1)} %shard_map.73.refs_0_), channel_id=1, source_target_pairs={{0,192},{1,65},{2,194},{3,67},{4,196},{5,69},{6,198},{7,71},{8,200... | collective-permute-start | bytes 786440 | tf_op jit(solution)/shard_map/ppermute | solution.py:566
  141.5 8.3 %collective-permute-start.29 = (f32[512,128]{1,0:T(8,128)S(1)}, f32[512,128]{1,0:T(8,128)S(1)}, u32[]{:S(2)}, u32[]{:S(2)}) collective-permute-start(f32[512,128]{1,0:T(8,128)S(1)} %shard_map.73.refs_0_), channel_id=1, source_target_pairs={{0,64},{1,193},{2,66},{3,195},{4,68},{5,197},{6,70},{7,199},{8,72}... | collective-permute-start | bytes 786440 | tf_op jit(solution)/shard_map/ppermute | solution.py:566
  (5 other events, 22.4 us)
